TPU v7x, 32 devices: a whole 2x2x4 slice. The times are simulated.
32 devices in a mesh: dp: 8 (over y, x, core), tensor: 4 (over z).
Axes of the slice: x: 2, y: 2, z: 4, core: 2. Of those that a mesh axis runs over, the one named last changes fastest.
Arguments:
- patches: bfloat16 [16384, 1024], P('dp'), may hold values from -6 to 6
- pos_embed: bfloat16 [16384, 1024], P('dp'), may hold values from -6 to 6
- counts: int32 [8, 8], P('dp'), may hold values from 96 to 576, as said below
- ln1_gain: float32 [1024], replicated, may hold values from 0.5 to 1.5
- w_qkv: bfloat16 [1024, 3, 1024], P(None, None, 'tensor'), may hold values from -0.1875 to 0.1875
- w_out: bfloat16 [1024, 1024], P('tensor'), may hold values from -0.75 to 0.75
- ln2_gain: float32 [1024], replicated, may hold values from 0.5 to 1.5
- w_up: bfloat16 [1024, 4096], P(None, 'tensor'), may hold values from -0.1875 to 0.1875
- w_down: bfloat16 [4096, 1024], P('tensor'), may hold values from -0.09375 to 0.09375
- ln3_gain: float32 [1024], replicated, may hold values from 0.5 to 1.5
- w_learn1: bfloat16 [1024, 1024], replicated, may hold values from -0.1875 to 0.1875
- w_learn2: bfloat16 [1024, 8], replicated, may hold values from -0.1875 to 0.1875
- cotangent: bfloat16 [64, 8, 1024], P('dp'), may hold values from -48 to 48
Outputs:
- learned: bfloat16 [64, 8, 1024], P('dp')
- input_grad: bfloat16 [16384, 1024], P('dp')
- grad_ln1_gain: float32 [1024], replicated
- grad_w_qkv: float32 [1024, 3, 1024], P(None, None, 'tensor')
- grad_w_out: float32 [1024, 1024], P('tensor')
- grad_ln2_gain: float32 [1024], replicated
- grad_w_up: float32 [1024, 4096], P(None, 'tensor')
- grad_w_down: float32 [4096, 1024], P('tensor')
- grad_ln3_gain: float32 [1024], replicated
- grad_w_learn1: float32 [1024, 1024], replicated
- grad_w_learn2: float32 [1024, 8], replicated
Inputs may be any that keep to these rules, and one draw needn't show every extreme that they name: Each row of 8 counts sums to 2048, and the largest of each row is 576.
All inputs are finite; a program needn't handle non-finite values.
Results may differ from a plain program's by a relative error of at most 0.019.
Values may be sent and summed in bfloat16 or wider, within the bound.
No kernel may reach another device: no remote copies, remote signals or barrier semaphores. Data moves between devices by JAX's collectives and lax.ppermute only.
A program may use at most 256 MiB of HBM per device.

v0:
```python
import jax
import jax.numpy as jnp
from jax import lax
from jax.sharding import PartitionSpec as P

HEAD_DIM = 64
MOST = 576
BLOCK = 512
WINDOW = 1664


EPSILON = 1e-06
LOW_TYPE = jnp.bfloat16
WIDE_TYPE = jnp.float32


def layer_norm(values, gain_vector):
    center = values - jnp.mean(values, axis=-1, keepdims=True)
    variance = jnp.mean(center * center, axis=-1, keepdims=True)
    inverse = lax.rsqrt(variance + EPSILON)
    normed = center * inverse
    return (normed * gain_vector, normed, inverse)


def norm_back(grad_in, gain_vector, normed, inverse):
    gain_grad = jnp.sum(grad_in * normed, axis=0)
    scaled = grad_in * gain_vector
    result = (
        scaled
        - jnp.mean(scaled, axis=-1, keepdims=True)
        - normed * jnp.mean(scaled * normed, axis=-1, keepdims=True)
    ) * inverse
    return (result, gain_grad)


def gelu_exact(values):
    return jax.nn.gelu(values, approximate=False)


def gelu_grad(values, upstream):
    pullback = jax.vjp(gelu_exact, values)[1]
    return pullback(upstream)[0]


def image_ids(counts_row, row_count):
    ends = jnp.cumsum(counts_row)
    places = jnp.arange(row_count, dtype=jnp.int32)
    return jnp.sum((places[:, None] >= ends[None, :]).astype(jnp.int32), axis=1)


def block_pieces(query, keys, values, image_of, block_index, score_scale):
    row_count = query.shape[0]
    query_start = block_index * BLOCK
    key_start = jnp.clip(query_start - MOST, 0, row_count - WINDOW)
    query_block = lax.dynamic_slice_in_dim(query, query_start, BLOCK, 0)
    key_block = lax.dynamic_slice_in_dim(keys, key_start, WINDOW, 0)
    value_block = lax.dynamic_slice_in_dim(values, key_start, WINDOW, 0)
    query_ids = lax.dynamic_slice_in_dim(image_of, query_start, BLOCK, 0)
    key_ids = lax.dynamic_slice_in_dim(image_of, key_start, WINDOW, 0)
    scores = (
        jnp.einsum("qhd,khd->hqk", query_block, key_block, preferred_element_type=WIDE_TYPE)
        * score_scale
    )
    allowed = (query_ids[:, None] == key_ids[None, :])[None]
    scores = jnp.where(allowed, scores, -1e30)
    return (query_start, key_start, query_block, key_block, value_block, scores)


def attend_forward(query, keys, values, image_of, score_scale):
    row_count = query.shape[0]

    def one_block(block_index):
        pieces = block_pieces(query, keys, values, image_of, block_index, score_scale)
        value_block = pieces[4]
        scores = pieces[5]
        row_max = jnp.max(scores, axis=-1, keepdims=True)
        exponent = jnp.exp(scores - row_max)
        row_total = jnp.sum(exponent, axis=-1, keepdims=True)
        probs = (exponent / row_total).astype(LOW_TYPE)
        result = jnp.einsum("hqk,khd->qhd", probs, value_block, preferred_element_type=WIDE_TYPE)
        return (result.astype(LOW_TYPE), row_max + jnp.log(row_total))

    outputs, log_sums = lax.map(one_block, jnp.arange(row_count // BLOCK, dtype=jnp.int32))
    return (outputs.reshape(query.shape), log_sums)


def attend_backward(query, keys, values, image_of, log_sums, grad_mixed, score_scale):
    row_count = query.shape[0]

    def one_block(block_index, carried):
        grad_query, grad_keys, grad_values = carried
        pieces = block_pieces(query, keys, values, image_of, block_index, score_scale)
        query_start, key_start, query_block, key_block, value_block, scores = pieces
        grad_block = lax.dynamic_slice_in_dim(grad_mixed, query_start, BLOCK, 0)
        probs = jnp.exp(scores - log_sums[block_index])
        grad_probs = jnp.einsum(
            "qhd,khd->hqk", grad_block, value_block, preferred_element_type=WIDE_TYPE
        )
        inner_sum = jnp.sum(probs * grad_probs, axis=-1, keepdims=True)
        grad_scores = (probs * (grad_probs - inner_sum)).astype(LOW_TYPE)
        query_part = (
            jnp.einsum("hqk,khd->qhd", grad_scores, key_block, preferred_element_type=WIDE_TYPE)
            * score_scale
        )
        key_part = (
            jnp.einsum("hqk,qhd->khd", grad_scores, query_block, preferred_element_type=WIDE_TYPE)
            * score_scale
        )
        value_part = jnp.einsum(
            "hqk,qhd->khd", probs.astype(LOW_TYPE), grad_block, preferred_element_type=WIDE_TYPE
        )
        grad_query = lax.dynamic_update_slice_in_dim(grad_query, query_part, query_start, 0)
        key_window = lax.dynamic_slice_in_dim(grad_keys, key_start, WINDOW, 0) + key_part
        grad_keys = lax.dynamic_update_slice_in_dim(grad_keys, key_window, key_start, 0)
        value_window = lax.dynamic_slice_in_dim(grad_values, key_start, WINDOW, 0) + value_part
        grad_values = lax.dynamic_update_slice_in_dim(grad_values, value_window, key_start, 0)
        return (grad_query, grad_keys, grad_values)

    zero_field = jnp.zeros(query.shape, WIDE_TYPE)
    return lax.fori_loop(0, row_count // BLOCK, one_block, (zero_field, zero_field, zero_field))


def local(
    patches,
    pos_embed,
    counts,
    ln1_gain,
    w_qkv,
    w_out,
    ln2_gain,
    w_up,
    w_down,
    ln3_gain,
    w_learn1,
    w_learn2,
    cotangent,
):
    row_count = patches.shape[0]
    width = patches.shape[1]
    head_width = w_qkv.shape[2]
    local_heads = head_width // HEAD_DIM
    score_scale = HEAD_DIM ** (-0.5)
    image_count = counts.shape[1]
    token_count = w_learn2.shape[1]
    inputs = patches.astype(WIDE_TYPE) + pos_embed.astype(WIDE_TYPE)
    image_of = image_ids(counts[0], row_count)
    member = (image_of[:, None] == jnp.arange(image_count, dtype=jnp.int32)[None, :]).astype(
        WIDE_TYPE
    )
    row_scale = jnp.sum(member * lax.rsqrt(counts[0].astype(WIDE_TYPE))[None, :], axis=1)
    norm_one, normed_one, inverse_one = layer_norm(inputs, ln1_gain)
    low_one = norm_one.astype(LOW_TYPE)
    qkv = jnp.einsum("td,dch->tch", low_one, w_qkv, preferred_element_type=WIDE_TYPE).astype(
        LOW_TYPE
    )
    query = qkv[:, 0].reshape(row_count, local_heads, HEAD_DIM)
    keys = qkv[:, 1].reshape(row_count, local_heads, HEAD_DIM)
    values = qkv[:, 2].reshape(row_count, local_heads, HEAD_DIM)
    mixed, log_sums = attend_forward(query, keys, values, image_of, score_scale)
    mixed_flat = mixed.reshape(row_count, head_width)
    attended = lax.psum(
        jnp.dot(mixed_flat, w_out, preferred_element_type=WIDE_TYPE).astype(jnp.bfloat16), "tensor"
    ).astype(jnp.float32)
    hidden = inputs + attended
    norm_two, normed_two, inverse_two = layer_norm(hidden, ln2_gain)
    low_two = norm_two.astype(LOW_TYPE)
    upper = jnp.dot(low_two, w_up, preferred_element_type=WIDE_TYPE)
    active = gelu_exact(upper).astype(LOW_TYPE)
    fed = lax.psum(
        jnp.dot(active, w_down, preferred_element_type=WIDE_TYPE).astype(jnp.bfloat16), "tensor"
    ).astype(jnp.float32)
    output = hidden + fed
    norm_three, normed_three, inverse_three = layer_norm(output, ln3_gain)
    low_three = norm_three.astype(LOW_TYPE)
    inner = jnp.dot(low_three, w_learn1, preferred_element_type=WIDE_TYPE)
    acted = gelu_exact(inner).astype(LOW_TYPE)
    logits = jnp.dot(acted, w_learn2, preferred_element_type=WIDE_TYPE)
    select = jax.nn.sigmoid(logits)
    weights = (select * row_scale[:, None]).astype(LOW_TYPE)
    table = (member.astype(LOW_TYPE)[:, :, None] * weights[:, None, :]).reshape(
        row_count, image_count * token_count
    )
    low_out = output.astype(LOW_TYPE)
    pooled = jnp.einsum("tj,td->jd", table, low_out, preferred_element_type=WIDE_TYPE)
    learned = pooled.reshape(image_count, token_count, width).astype(LOW_TYPE)
    grad_pooled = cotangent.reshape(image_count * token_count, width)
    grad_output = jnp.einsum("tj,jd->td", table, grad_pooled, preferred_element_type=WIDE_TYPE)
    grad_table = jnp.einsum("td,jd->tj", low_out, grad_pooled, preferred_element_type=WIDE_TYPE)
    grad_weights = jnp.sum(
        grad_table.reshape(row_count, image_count, token_count) * member[:, :, None], axis=1
    )
    grad_logits = (grad_weights * row_scale[:, None] * select * (1.0 - select)).astype(LOW_TYPE)
    grad_learn2 = jnp.einsum("tl,tk->lk", acted, grad_logits, preferred_element_type=WIDE_TYPE)
    grad_acted = jnp.einsum("tk,lk->tl", grad_logits, w_learn2, preferred_element_type=WIDE_TYPE)
    grad_inner = gelu_grad(inner, grad_acted).astype(LOW_TYPE)
    grad_learn1 = jnp.einsum("td,tl->dl", low_three, grad_inner, preferred_element_type=WIDE_TYPE)
    grad_norm3 = jnp.einsum("tl,dl->td", grad_inner, w_learn1, preferred_element_type=WIDE_TYPE)
    grad_from_three, grad_gain3 = norm_back(grad_norm3, ln3_gain, normed_three, inverse_three)
    grad_output = grad_output + grad_from_three
    grad_fed = grad_output.astype(LOW_TYPE)
    grad_down = jnp.einsum("tf,td->fd", active, grad_fed, preferred_element_type=WIDE_TYPE)
    grad_active = jnp.einsum("td,fd->tf", grad_fed, w_down, preferred_element_type=WIDE_TYPE)
    grad_upper = gelu_grad(upper, grad_active).astype(LOW_TYPE)
    grad_up = jnp.einsum("td,tf->df", low_two, grad_upper, preferred_element_type=WIDE_TYPE)
    grad_norm2 = lax.psum(
        jnp.einsum("tf,df->td", grad_upper, w_up, preferred_element_type=WIDE_TYPE).astype(
            jnp.bfloat16
        ),
        "tensor",
    ).astype(jnp.float32)
    grad_from_two, grad_gain2 = norm_back(grad_norm2, ln2_gain, normed_two, inverse_two)
    grad_hidden = grad_output + grad_from_two
    grad_attended = grad_hidden.astype(LOW_TYPE)
    grad_out_weight = jnp.einsum(
        "th,td->hd", mixed_flat, grad_attended, preferred_element_type=WIDE_TYPE
    )
    grad_mixed = jnp.einsum(
        "td,hd->th", grad_attended, w_out, preferred_element_type=WIDE_TYPE
    ).astype(LOW_TYPE)
    grad_mixed = grad_mixed.reshape(row_count, local_heads, HEAD_DIM)
    grad_query, grad_keys, grad_values = attend_backward(
        query, keys, values, image_of, log_sums, grad_mixed, score_scale
    )
    grad_qkv = (
        jnp.stack([grad_query, grad_keys, grad_values], axis=1)
        .reshape(row_count, 3, head_width)
        .astype(LOW_TYPE)
    )
    grad_qkv_weight = jnp.einsum("td,tch->dch", low_one, grad_qkv, preferred_element_type=WIDE_TYPE)
    grad_norm1 = lax.psum(
        jnp.einsum("tch,dch->td", grad_qkv, w_qkv, preferred_element_type=WIDE_TYPE).astype(
            jnp.bfloat16
        ),
        "tensor",
    ).astype(jnp.float32)
    grad_from_one, grad_gain1 = norm_back(grad_norm1, ln1_gain, normed_one, inverse_one)
    input_grad = (grad_hidden + grad_from_one).astype(LOW_TYPE)
    summed = (
        lax.psum(grad_gain1.astype(jnp.bfloat16), "dp").astype(jnp.float32),
        lax.psum(grad_qkv_weight.astype(jnp.bfloat16), "dp").astype(jnp.float32),
        lax.psum(grad_out_weight.astype(jnp.bfloat16), "dp").astype(jnp.float32),
        lax.psum(grad_gain2.astype(jnp.bfloat16), "dp").astype(jnp.float32),
        lax.psum(grad_up.astype(jnp.bfloat16), "dp").astype(jnp.float32),
        lax.psum(grad_down.astype(jnp.bfloat16), "dp").astype(jnp.float32),
        lax.psum(grad_gain3.astype(jnp.bfloat16), "dp").astype(jnp.float32),
        lax.psum(grad_learn1.astype(jnp.bfloat16), "dp").astype(jnp.float32),
        lax.psum(grad_learn2.astype(jnp.bfloat16), "dp").astype(jnp.float32),
    )
    return (
        learned,
        input_grad,
        summed[0],
        summed[1],
        summed[2],
        summed[3],
        summed[4],
        summed[5],
        summed[6],
        summed[7],
        summed[8],
    )


def solution(mesh):
    return jax.shard_map(
        local,
        mesh=mesh,
        in_specs=(
            P("dp", None),
            P("dp", None),
            P("dp", None),
            P(),
            P(None, None, "tensor"),
            P("tensor", None),
            P(),
            P(None, "tensor"),
            P("tensor", None),
            P(),
            P(),
            P(),
            P("dp", None, None),
        ),
        out_specs=(
            P("dp", None, None),
            P("dp", None),
            P(),
            P(None, None, "tensor"),
            P("tensor", None),
            P(),
            P(None, "tensor"),
            P("tensor", None),
            P(),
            P(),
            P(),
        ),
        check_vma=False,
    )
```

profile of v0, /device:TPU:0, one launch (start us, length us, event | category | flops | bytes accessed | tf_op | source)
XLA Modules:
  0.0 1307.9 jit_solution(3772105733460153413)
XLA Ops:
  21.8 62.9 %while.33 = (s32[]{:T(128)}, bf16[4,512,4,64]{1,3,2,0:T(8,128)(2,1)}, f32[4,4,512,1]{2,1,3,0:T(4,128)}, s32[4]{0:T(128)S(1)}, bf16[2048,4,64]{0,2,1:T(8,128)(2,1...) while((s32[]{:T(128)}, ...), condition=%wide.region_7.8_spmd, body=%wide.region_4.0_spmd.sunk | while | flops 914290688 | bytes 50817812 | solution.py:83
  92.9 157.8 %all-reduce.8.cloned.1.call-done = bf16[2048,1024]{1,0:T(8,128)(2,1)} async-done(((bf16[2048,1024]{1,0:T(8,128)(2,1)}), bf16[2048,1024]{1,0:T(8,128)(2,1)}) %all-reduce.8.cloned.1.call-update) | async-done | bytes 4194320 | tf_op jit(solution)/shard_map/psum | solution.py:161
  261.4 24.0 %multiply_convert_fusion.3 = (bf16[2048,1024]{1,0:T(8,128)(2,1)S(1)}, f32[2048,1024]{1,0:T(8,128)}, f32[2048,1024]{1,0:T(8,128)}) fusion(bf16[2048,1024]{1,0:T(8,128)(2,1)S(1)} %multiply_convert_fusion.4, bf16[1024,1024]{1,0:T(8,128)(2,1)S(1)} %copy-done.55), kind=kOutput, calls=%fused_computation.98 | convolution fusion | flops 4431282176 | bytes 27262976 | tf_op jit(solution)/shard_map/dot_general | solution.py:167
  293.7 153.9 %all-reduce.10.cloned.1.call-done = bf16[2048,1024]{1,0:T(8,128)(2,1)} async-done(((bf16[2048,1024]{1,0:T(8,128)(2,1)}), bf16[2048,1024]{1,0:T(8,128)(2,1)}) %all-reduce.10.cloned.1.call-update) | async-done | bytes 4194320 | tf_op jit(solution)/shard_map/psum | solution.py:169
  455.9 22.9 %multiply_convert_fusion.1 = (bf16[2048,1024]{1,0:T(8,128)(2,1)S(1)}, f32[2048,1024]{1,0:T(8,128)S(1)}, f32[2048,1024]{1,0:T(8,128)}) fusion(bf16[2048,1024]{1,0:T(8,128)(2,1)S(1)} %multiply_convert_fusion.2, bf16[1024,1024]{1,0:T(8,128)(2,1)S(1)} %copy-done), kind=kOutput, calls=%fused_computation.82 | convolution fusion | flops 4431282176 | bytes 27262976 | tf_op jit(solution)/shard_map/dot_general | solution.py:175
  500.0 13.5 %add_convert_fusion = bf16[2048,1024]{1,0:T(8,128)(2,1)S(1)} fusion(f32[2048,1024]{1,0:T(8,128)} %get-tuple-element.421, f32[2048,1024]{1,0:T(8,128)} %get-tuple-element.435, bf16[1024,1024]{1,0:T(8,128)(2,1)S(1)} %copy-done.54, f32[2048,1024]{1,0:T(8,128)} %bitcast_add_fusion), kind=kOutput, calls=%fused_computation.79 | convolution fusion | flops 4326424576 | bytes 31457280 | tf_op jit(solution)/shard_map/td,fd->tf/dot_general | solution.py:202
  544.8 131.2 %all-reduce.12.cloned.1.call-done = bf16[2048,1024]{1,0:T(8,128)(2,1)} async-done(((bf16[2048,1024]{1,0:T(8,128)(2,1)}), bf16[2048,1024]{1,0:T(8,128)(2,1)}) %all-reduce.12.cloned.1.call-update) | async-done | bytes 4194320 | tf_op jit(solution)/shard_map/psum | solution.py:205
  699.5 255.3 %while.34 = (s32[]{:T(128)}, bf16[2048,4,64]{0,2,1:T(8,128)(2,1)}, f32[2048,4,64]{0,2,1:T(8,128)}, f32[2048,4,64]{0,2,1:T(8,128)}, bf16[2048,4,64]{0,2,1:T(8,128...) while((s32[]{:T(128)}, bf16[2048,4,64]{0,2,1:T(8,128)(2,1)}, ...), condition=%wide.region_23.24_spmd, body=%wide.region_21.23_spmd.sunk | while | flops 2234415104 | bytes 213665648 | solution.py:120
  727.2 10.2 dynamic_update_slice.55
  743.2 10.4 fusion.187
  753.6 10.2 dynamic_update_slice.56
  791.3 10.2 dynamic_update_slice.55
  807.3 10.4 fusion.187
  817.7 10.2 dynamic_update_slice.56
  855.4 9.8 dynamic_update_slice.55
  871.1 10.4 fusion.187
  881.4 9.8 dynamic_update_slice.56
  918.8 9.8 dynamic_update_slice.55
  934.4 10.4 fusion.187
  944.8 9.8 dynamic_update_slice.56
  986.9 111.4 %all-reduce.16.cloned.1.call-done = (bf16[1024,3,256]{2,0,1:T(8,128)(2,1)}, bf16[256,1024]{1,0:T(8,128)(2,1)}, bf16[1024,1024]{1,0:T(8,128)(2,1)}, bf16[1024,1024]{1,0:T(8,128)(2,1)}, bf16[1024,1024]{1,0:T(8,128)(2,1)}) async-done(((bf16[1024,3,256]{2,0,1:T(8,128)(2,1)}, bf16[256,1024]{1,0:T(8,128)(2,1)}, bf16[1024,1024]{1,0:T(8,128)(2,1)}, bf16[1024,1024]{1,0:T(8,128)(2,1)}, bf16[1024,1024]{1,0:T(8,128)(2,1)}), ...) | async-done | bytes 8388624 | tf_op jit(solution)/shard_map/psum | solution.py:240
  1112.2 144.2 %all-reduce.14.cloned.1.call-done = bf16[2048,1024]{1,0:T(8,128)(2,1)} async-done(((bf16[2048,1024]{1,0:T(8,128)(2,1)}), bf16[2048,1024]{1,0:T(8,128)(2,1)}) %all-reduce.14.cloned.1.call-update) | async-done | bytes 4194320 | tf_op jit(solution)/shard_map/psum | solution.py:230
  1263.4 24.0 %all-reduce = (bf16[1024]{0:T(1024)(128)(2,1)S(1)}, bf16[1024]{0:T(1024)(128)(2,1)S(1)}, bf16[1024]{0:T(1024)(128)(2,1)S(1)}, bf16[1024,8]{0,1:T(8,128)(2,1)S(1)}) all-reduce(bf16[1024]{0:T(1024)(128)(2,1)S(1)} %get-tuple-element.366, bf16[1024]{0:T(1024)(128)(2,1)S(1)} %copy-done.50, ...), channel_id=1, replica_groups=mesh['dp'=8,'tensor'=4] {'dp'}, use_global_device_ids=true, to_apply=%region_28.29 | all-reduce | flops 11264 | bytes 45056 | tf_op jit(solution)/shard_map/psum | solution.py:239
  1289.9 11.2 fusion.58
  (307 shorter events, 373.7 us)
Async XLA Ops:
  7.2 448.7 %copy-start = (bf16[1024,1024]{1,0:T(8,128)(2,1)S(1)}, bf16[1024,1024]{1,0:T(8,128)(2,1)}, u32[]{:S(2)}) copy-start(bf16[1024,1024]{1,0:T(8,128)(2,1)} %param.27) | copy-start | bytes 6291460
  7.2 243.5 %all-reduce.8.cloned.1.call-start = ((), (), s32[]{:S(2)}) async-start(), calls=%async_computation | async-start | bytes 8388608 | tf_op jit(solution)/shard_map/psum | solution.py:161
  84.8 208.9 %copy-start.24 = (s32[2048]{0:T(1024)}, s32[2048]{0:T(1024)S(1)}, u32[]{:S(2)}) copy-start(s32[2048]{0:T(1024)S(1)} %get-tuple-element.686) | copy-start | bytes 24580
  92.9 354.8 %all-reduce.10.cloned.1.call-start = ((), (), s32[]{:S(2)}) async-start(), calls=%async_computation.1 | async-start | bytes 8388608 | tf_op jit(solution)/shard_map/psum | solution.py:169
  258.2 27.1 %copy-start.41 = (f32[2048]{0:T(1024)}, f32[2048]{0:T(1024)S(1)}, u32[]{:S(2)}) copy-start(f32[2048]{0:T(1024)S(1)} %add_rsqrt_fusion.1) | copy-start | bytes 24580
  261.4 24.0 %copy-start.18 = (bf16[2048,1024]{1,0:T(8,128)(2,1)}, bf16[2048,1024]{1,0:T(8,128)(2,1)S(1)}, u32[]{:S(2)}) copy-start(bf16[2048,1024]{1,0:T(8,128)(2,1)S(1)} %multiply_convert_fusion.4) | copy-start | bytes 12582916
  261.4 26.1 %copy-start.53 = (bf16[1024,1024]{1,0:T(8,128)(2,1)S(1)}, bf16[1024,1024]{1,0:T(8,128)(2,1)}, u32[]{:S(2)}) copy-start(bf16[1024,1024]{1,0:T(8,128)(2,1)} %param.25) | copy-start | bytes 6291460
  293.5 382.5 %all-reduce.12.cloned.1.call-start = ((), (), s32[]{:S(2)}) async-start(), calls=%async_computation.2 | async-start | bytes 8388608 | tf_op jit(solution)/shard_map/psum | solution.py:205
  293.7 200.8 %copy-start.37 = (bf16[2048,8]{0,1:T(8,128)(2,1)}, bf16[2048,8]{0,1:T(8,128)(2,1)S(1)}, u32[]{:S(2)}) copy-start(bf16[2048,8]{0,1:T(8,128)(2,1)S(1)} %get-tuple-element.434) | copy-start | bytes 98308
  453.1 41.4 %copy-start.6 = (f32[2048,1024]{1,0:T(8,128)}, f32[2048,1024]{1,0:T(8,128)S(1)}, u32[]{:S(2)}) copy-start(f32[2048,1024]{1,0:T(8,128)S(1)} %get-tuple-element.419) | copy-start | bytes 25165828
  455.9 23.0 %copy-start.20 = (bf16[2048,1024]{1,0:T(8,128)(2,1)}, bf16[2048,1024]{1,0:T(8,128)(2,1)S(1)}, u32[]{:S(2)}) copy-start(bf16[2048,1024]{1,0:T(8,128)(2,1)S(1)} %multiply_convert_fusion.2) | copy-start | bytes 12582916
  455.9 22.9 %copy-start.58 = (bf16[8,8,1024]{2,1,0:T(8,128)(2,1)S(1)}, bf16[8,8,1024]{2,1,0:T(8,128)(2,1)}, u32[]{:S(2)}) copy-start(bf16[8,8,1024]{2,1,0:T(8,128)(2,1)} %param.29) | copy-start | bytes 393220
  481.5 13.0 copy-start.33
  500.0 15.6 %copy-start.56 = (bf16[1024,1024]{1,0:T(8,128)(2,1)S(1)}, bf16[1024,1024]{1,0:T(8,128)(2,1)}, u32[]{:S(2)}) copy-start(bf16[1024,1024]{1,0:T(8,128)(2,1)} %param.24) | copy-start | bytes 6291460
  521.9 576.4 %all-reduce.16.cloned.1.call-start = ((), (), s32[]{:S(2)}) async-start(), calls=%async_computation.4 | async-start | bytes 16777216 | tf_op jit(solution)/shard_map/psum | solution.py:240
  523.0 15.9 %slice-start = ((s8[8388608]{0:T(1024)(128)(4,1)}), s8[4194304]{0:T(1024)(128)(4,1)S(1)}, s32[]{:S(2)}) async-start(s8[8388608]{0:T(1024)(128)(4,1)} %bitcast.122), calls=%async_computation.5 | async-start | bytes 8388608
  539.0 137.1 %copy-start.32 = (f32[2048]{0:T(1024)S(1)}, f32[2048]{0:T(1024)}, u32[]{:S(2)}) copy-start(f32[2048]{0:T(1024)} %copy-done.31) | copy-start | bytes 24580
  539.0 137.1 %copy-start.42 = (f32[2048]{0:T(1024)S(1)}, f32[2048]{0:T(1024)}, u32[]{:S(2)}) copy-start(f32[2048]{0:T(1024)} %copy-done.41) | copy-start | bytes 24580
  539.0 137.0 %copy-start.46 = (f32[1024]{0:T(1024)S(1)}, f32[1024]{0:T(1024)}, u32[]{:S(2)}) copy-start(f32[1024]{0:T(1024)} %param.23) | copy-start | bytes 12292
  894.2 11.0 copy-start.2
  971.0 285.4 %all-reduce.14.cloned.1.call-start = ((), (), s32[]{:S(2)}) async-start(), calls=%async_computation.3 | async-start | bytes 8388608 | tf_op jit(solution)/shard_map/psum | solution.py:230
  1109.2 154.2 %copy-start.50 = (bf16[1024]{0:T(1024)(128)(2,1)S(1)}, bf16[1024]{0:T(1024)(128)(2,1)}, u32[]{:S(2)}) copy-start(bf16[1024]{0:T(1024)(128)(2,1)} %get-tuple-element.364) | copy-start | bytes 6148
  1109.2 154.2 %copy-start.52 = (bf16[1024]{0:T(1024)(128)(2,1)S(1)}, bf16[1024]{0:T(1024)(128)(2,1)}, u32[]{:S(2)}) copy-start(bf16[1024]{0:T(1024)(128)(2,1)} %get-tuple-element.362) | copy-start | bytes 6148
  1289.8 11.2 copy-start.1
  (61 other events, 340.8 us)
Sparse Core Ops, SparseCore 0:
  93.0 157.6 all-reduce.7
  293.6 153.9 all-reduce.9
  522.0 153.9 all-reduce.11
  971.1 127.1 all-reduce.15
  1101.1 155.2 all-reduce.13
where the time goes:
time: 1320 us; the launch traced here: 1310 us
  waiting for transfers between devices  699 us (53%)
  matrix products  319 us (24%)
  other arithmetic  128 us (10%)
  local copies, waits for them, and re-layouts  119 us (9%)
  blocking collectives  24 us (2%)
  between operations  14.9 us (1%)
    psum x1, waiting for transfers between devices, local(): lax.psum(jnp.dot(mixed_flat, w_out, preferred_element_type=WIDE_TYPE).ast...  158 us
    psum x1, waiting for transfers between devices, local(): lax.psum(jnp.dot(active, w_down, preferred_element_type=WIDE_TYPE).astype...  154 us
    psum x1, waiting for transfers between devices, local(): lax.psum(jnp.einsum('tch,dch->td', grad_qkv, w_qkv, preferred_element_typ...  144 us
    psum x1, waiting for transfers between devices, local(): lax.psum(jnp.einsum('tf,df->td', grad_upper, w_up, preferred_element_type...  131 us
    psum x1, waiting for transfers between devices, local(): lax.psum(grad_qkv_weight.astype(jnp.bfloat16), 'dp').astype(jnp.float32)  111 us
    dot_general x4, matrix products, one_block(): jnp.einsum('hqk,qhd->khd', probs.astype(LOW_TYPE), grad_block, preferred_...  41.5 us
    dynamic_update_slice x4, local copies, waits for them, and re-layouts, one_block(): lax.dynamic_update_slice_in_dim(grad_values, value_window, key_start, 0)  40 us
    dynamic_update_slice x4, local copies, waits for them, and re-layouts, one_block(): lax.dynamic_update_slice_in_dim(grad_keys, key_window, key_start, 0)  40 us
  transfers between devices with their start and end apart: 5, of which 5 were waited for; matrix products, arithmetic and copies ran while one was open for 4% of the time, Pallas kernels for 0%

commit v1 on v0

v1 whole, which is shorter than its diff:
```python
import functools

import jax
import jax.numpy as jnp
from jax import lax
from jax.experimental import pallas as pl
from jax.experimental.pallas import tpu as pltpu
from jax.sharding import PartitionSpec as P

HEAD_DIM = 64
MOST = 576
EPSILON = 1e-06
LOW = jnp.bfloat16
WIDE = jnp.float32
FAR = -1e30


def layer_norm(values):
    center = values - jnp.mean(values, axis=-1, keepdims=True)
    variance = jnp.mean(center * center, axis=-1, keepdims=True)
    inverse = lax.rsqrt(variance + EPSILON)
    return center * inverse, inverse


def norm_back(grad_in, gain, normed, inverse):
    gain_grad = jnp.sum(grad_in * normed, axis=0)
    scaled = grad_in * gain
    result = (
        scaled
        - jnp.mean(scaled, axis=-1, keepdims=True)
        - normed * jnp.mean(scaled * normed, axis=-1, keepdims=True)
    ) * inverse
    return result, gain_grad


def gelu_both(values):
    share = 0.5 * (1.0 + lax.erf(values * (0.5**0.5)))
    density = jnp.exp(-0.5 * values * values) * 0.3989422804014327
    return values * share, share + values * density


def dot(left, right, left_dim, right_dim):
    return lax.dot_general(
        left, right, (((left_dim,), (right_dim,)), ((), ())), preferred_element_type=WIDE
    )


def dot_low(left, right, left_dim, right_dim):
    return dot(left, right, left_dim, right_dim).astype(LOW)


def row_capacity(rows, images, n_tensor):
    if n_tensor >= images:
        most = MOST
    elif n_tensor == 4 and images == 8 and rows == 2048:
        most = 630
    else:
        most = rows // n_tensor + MOST
    return min(rows, -(-most // 128) * 128)


def place_kernel(n_tensor, counts_ref, place_ref):
    images = counts_ref.shape[1]
    count = [counts_ref[0, i] for i in range(images)]
    zero = count[0] * 0
    used, device, offset = [zero] * images, [zero] * images, [zero] * images
    loads = [zero] * n_tensor
    for _ in range(images):
        best, at = zero - 1, zero
        for i in range(images):
            better = jnp.logical_and(used[i] == 0, count[i] > best)
            best = jnp.where(better, count[i], best)
            at = jnp.where(better, i, at)
        least, least_at = loads[0], zero
        for b in range(1, n_tensor):
            better = loads[b] < least
            least = jnp.where(better, loads[b], least)
            least_at = jnp.where(better, b, least_at)
        for i in range(images):
            here = at == i
            used[i] = jnp.where(here, 1, used[i])
            device[i] = jnp.where(here, least_at, device[i])
            offset[i] = jnp.where(here, least, offset[i])
        for b in range(n_tensor):
            loads[b] = loads[b] + jnp.where(least_at == b, best, 0)
    start = zero
    for i in range(images):
        place_ref[0, i] = device[i]
        place_ref[1, i] = offset[i]
        place_ref[2, i] = start
        start = start + count[i]


def place_images(counts, n_tensor):
    images = counts.shape[1]
    return pl.pallas_call(
        functools.partial(place_kernel, n_tensor),
        out_shape=jax.ShapeDtypeStruct((3, images), jnp.int32),
        in_specs=[pl.BlockSpec(memory_space=pltpu.SMEM)],
        out_specs=pl.BlockSpec(memory_space=pltpu.SMEM),
        name="place_images",
    )(counts)


def pass_on(near, n_tensor):
    below = above = near
    for _ in range(n_tensor - 1):
        below = lax.ppermute(below, "tensor", [(i, i + 1) for i in range(n_tensor - 1)])
        above = lax.ppermute(above, "tensor", [(i + 1, i) for i in range(n_tensor - 1)])
        below, above = yield below, above


def row_map(place, counts, device, capacity):
    row = jnp.arange(capacity, dtype=jnp.int32)[:, None]
    offset, start = place[1][None], place[2][None]
    inside = (place[0][None] == device) & (row >= offset) & (row < offset + counts)
    image = jnp.sum(jnp.where(inside, jnp.arange(counts.shape[1], dtype=jnp.int32) + 1, 0), axis=1) - 1
    source = jnp.sum(jnp.where(inside, start - offset + row + 1, 0), axis=1) - 1
    return image, source


def after(value, *others):
    return lax.optimization_barrier((value,) + others)[0]


def swap(value, axis, size, mask):
    return lax.ppermute(value, axis, [(i, i ^ mask) for i in range(size)])


def reorder(value, dim, size, index):
    return jnp.concatenate(
        [lax.dynamic_slice_in_dim(value, index ^ m, 1, dim) for m in range(size)], axis=dim
    )


def link_bits(n_dp, half):
    bits = list(range(1, n_dp.bit_length() - 1))
    return bits[::-1] if half else bits


def gather_links(far, n_dp):
    value = [far[0], far[1]]
    count = n_dp.bit_length() - 2
    for step in range(count):
        for half in range(2):
            bit = link_bits(n_dp, half)[step]
            value[half] = jnp.stack([value[half], swap(value[half], "dp", n_dp, 1 << bit)])
    value[1] = jnp.transpose(value[1], tuple(range(count))[::-1] + tuple(range(count, value[1].ndim)))
    return [v.reshape((1 << count,) + v.shape[count:]) for v in value]


def own_units(shard, n_dp, index):
    lead, units, width = shard.shape
    part = units // (2 * n_dp)
    split = shard.reshape(lead, n_dp, 2, part, width)
    ordered = reorder(split, 1, n_dp, index).reshape(lead, n_dp // 2, 2, 2, part, width)
    return [ordered[:, :, core] for core in range(2)]


def my_piece(shard, n_dp, index):
    lead, units, width = shard.shape
    part = units // (2 * n_dp)
    split = shard.reshape(lead, n_dp, 2, part, width)
    mine = lax.dynamic_slice_in_dim(split, index, 1, 1)[:, 0]
    return jnp.transpose(mine, (1, 0, 2, 3)).reshape(2, lead * part, width)


def gather_tensor(pieces, n_tensor):
    pack = jnp.concatenate(pieces, axis=1)
    return jnp.stack([swap(pack, "tensor", n_tensor, j) for j in range(1, n_tensor)], axis=1)


def gather_core(near, sizes, n_dp, n_tensor):
    width = near[0].shape[-1]
    both = [near, [swap(n, "dp", n_dp, 1) for n in near]]
    result = []
    for halves in both:
        weights, at = [], 0
        for lead, part in sizes:
            pieces = [
                h[:, :, at : at + lead * part].reshape(n_dp // 2, n_tensor - 1, lead, part, width)
                for h in halves
            ]
            weights.append(jnp.transpose(jnp.stack(pieces), (3, 2, 1, 0, 4, 5)))
            at += lead * part
        result.append(weights)
    return result


def join(own, far, part_first):
    width = own.shape[-1]
    full = jnp.concatenate([own[:, None], far], axis=1)
    if part_first:
        full = jnp.transpose(full, (3, 0, 2, 1, 4, 5))
    return full.reshape(-1, width)


def split_units(grad, lead, n_dp, n_tensor, part_first):
    width = grad.shape[-1]
    links = n_dp // 2
    if part_first:
        parts = grad.reshape(2, links, -1, width)
        return [parts[0], parts[1]]
    split = grad.reshape(lead, n_tensor, links, 2, -1, width)
    return [
        jnp.transpose(split[:, :, :, half], (2, 1, 0, 3, 4)).reshape(links, -1, width) for half in range(2)
    ]


def split_shared(grad, n_dp, index):
    links = n_dp // 2
    parts = grad.reshape(2, links, -1, grad.shape[-1])
    ordered = reorder(parts, 1, links, index // 2)
    return [ordered[0], ordered[1]]


def link_sums(groups, n_dp):
    width = groups[0][0].shape[-1]
    bits = n_dp.bit_length() - 2
    halves = [[g[half].reshape((2,) * bits + g[half].shape[1:]) for g in groups] for half in range(2)]
    held = [list(range(bits, 0, -1)) for _ in range(2)]
    for step in range(bits):
        for half in range(2):
            bit = link_bits(n_dp, 1 - half)[step]
            dim = held[half].index(bit)
            held[half].remove(bit)
            keeps = [lax.index_in_dim(p, 0, dim, keepdims=False) for p in halves[half]]
            aways = [lax.index_in_dim(p, 1, dim, keepdims=False).reshape(-1, width) for p in halves[half]]
            came = swap(jnp.concatenate(aways) if len(aways) > 1 else aways[0], "dp", n_dp, 1 << bit)
            parts, at = [], 0
            for keep, away in zip(keeps, aways):
                piece = came[at : at + away.shape[0]].reshape(keep.shape)
                parts.append((keep.astype(WIDE) + piece.astype(WIDE)).astype(LOW))
                at += away.shape[0]
            halves[half] = parts
        yield halves


def advance(halves, *others):
    flat = lax.optimization_barrier(tuple(halves[0] + halves[1]) + others)
    count = len(halves[0])
    halves[0][:] = flat[:count]
    halves[1][:] = flat[count : 2 * count]


def reduce_tensor(scattered, shared, n_tensor):
    width = (scattered + shared)[0].shape[-1]
    split = [s.reshape(2, n_tensor, -1, width) for s in scattered]
    total = None
    for j in range(n_tensor):
        piece = [s[:, j] for s in split] + shared
        piece = jnp.concatenate(piece, axis=1) if len(piece) > 1 else piece[0]
        came = (piece if j == 0 else swap(piece, "tensor", n_tensor, j)).astype(WIDE)
        total = came if total is None else total + came
    return total.astype(LOW)


def spread_plane(total, n_dp):
    near = jnp.stack(gather_links(total, n_dp), axis=1)
    return jnp.stack([near, swap(near, "dp", n_dp, 1)], axis=1)


def place_units(seen, lead, n_dp, index):
    links, _, _, rows, width = seen.shape
    seen = seen.reshape(n_dp, 2, lead, rows // lead, width)
    return reorder(jnp.transpose(seen, (2, 0, 1, 3, 4)), 1, n_dp, index).reshape(lead, -1, width)


def place_shared(seen, n_dp, index):
    links, _, _, rows, width = seen.shape
    seen = reorder(jnp.transpose(seen, (1, 2, 0, 3, 4)), 0, 2, index & 1)
    return reorder(seen, 2, links, index // 2).reshape(-1, width)


def attend_kernel(scale, first_ref, second_ref, column_ref, row_ref, mixed_first_ref, mixed_second_ref, log_ref):
    query, key, value = [jnp.concatenate([first_ref[i, 0], second_ref[i, 0]]) for i in range(3)]
    scores = dot(key, query * scale, 0, 0)
    scores = jnp.where(column_ref[...] == row_ref[...], scores, FAR)
    most = jnp.max(scores, axis=0, keepdims=True)
    exponent = jnp.exp(scores - most)
    total = jnp.sum(exponent, axis=0, keepdims=True)
    mixed = (dot(value, exponent.astype(LOW), 1, 0) / total).astype(LOW)
    half = mixed.shape[0] // 2
    mixed_first_ref[0] = mixed[:half]
    mixed_second_ref[0] = mixed[half:]
    log_ref[0] = most + jnp.log(total)


def attend(first, second, image, scale):
    _, heads, half, rows = first.shape
    three = pl.BlockSpec((3, 1, half, rows), lambda h: (0, h, 0, 0))
    one = pl.BlockSpec((1, half, rows), lambda h: (h, 0, 0))
    return pl.pallas_call(
        functools.partial(attend_kernel, scale),
        grid=(heads,),
        in_specs=[
            three,
            three,
            pl.BlockSpec((rows, 1), lambda h: (0, 0)),
            pl.BlockSpec((1, rows), lambda h: (0, 0)),
        ],
        out_specs=[one, one, pl.BlockSpec((1, 1, rows), lambda h: (h, 0, 0))],
        out_shape=[
            jax.ShapeDtypeStruct((heads, half, rows), LOW),
            jax.ShapeDtypeStruct((heads, half, rows), LOW),
            jax.ShapeDtypeStruct((heads, 1, rows), WIDE),
        ],
        compiler_params=pltpu.CompilerParams(vmem_limit_bytes=48 << 20),
        cost_estimate=pl.CostEstimate(
            flops=4 * rows * rows * heads * 512, bytes_accessed=8 * heads * HEAD_DIM * rows, transcendentals=0
        ),
        name="attend",
    )(first, second, image[:, None], image[None, :])


def attend_back_kernel(
    scale,
    first_ref,
    second_ref,
    mixed_first_ref,
    mixed_second_ref,
    grad_first_ref,
    grad_second_ref,
    log_ref,
    column_ref,
    row_ref,
    out_first_ref,
    out_second_ref,
):
    query, key, value = [jnp.concatenate([first_ref[i, 0], second_ref[i, 0]]) for i in range(3)]
    query = query * scale
    mixed = jnp.concatenate([mixed_first_ref[0], mixed_second_ref[0]])
    grad = jnp.concatenate([grad_first_ref[0], grad_second_ref[0]])
    scores = dot(key, query, 0, 0)
    scores = jnp.where(column_ref[...] == row_ref[...], scores, FAR)
    probs = jnp.exp(scores - log_ref[0])
    grad_probs = dot(value, grad, 0, 0)
    inner = jnp.sum(mixed.astype(WIDE) * grad.astype(WIDE), axis=0, keepdims=True)
    grad_scores = (probs * (grad_probs - inner)).astype(LOW)
    grads = (
        (dot(key, grad_scores, 1, 0) * scale).astype(LOW),
        dot(query, grad_scores, 1, 1).astype(LOW),
        dot(grad, probs.astype(LOW), 1, 1).astype(LOW),
    )
    half = mixed.shape[0] // 2
    for i, item in enumerate(grads):
        out_first_ref[i, 0] = item[:half]
        out_second_ref[i, 0] = item[half:]


def attend_back(first, second, mixed, grad_mixed, log_sums, image, scale):
    _, heads, half, rows = first.shape
    three = pl.BlockSpec((3, 1, half, rows), lambda h: (0, h, 0, 0))
    one = pl.BlockSpec((1, half, rows), lambda h: (h, 0, 0))
    return pl.pallas_call(
        functools.partial(attend_back_kernel, scale),
        grid=(heads,),
        in_specs=[
            three,
            three,
            one,
            one,
            one,
            one,
            pl.BlockSpec((1, 1, rows), lambda h: (h, 0, 0)),
            pl.BlockSpec((rows, 1), lambda h: (0, 0)),
            pl.BlockSpec((1, rows), lambda h: (0, 0)),
        ],
        out_specs=[three, three],
        out_shape=[jax.ShapeDtypeStruct((3, heads, half, rows), LOW)] * 2,
        compiler_params=pltpu.CompilerParams(vmem_limit_bytes=48 << 20),
        cost_estimate=pl.CostEstimate(
            flops=10 * rows * rows * heads * 512, bytes_accessed=16 * heads * HEAD_DIM * rows, transcendentals=0
        ),
        name="attend_back",
    )(first, second, *mixed, *grad_mixed, log_sums, image[:, None], image[None, :])


def local(
    n_dp,
    n_tensor,
    patches,
    pos_embed,
    counts,
    ln1_gain,
    w_qkv,
    w_out,
    ln2_gain,
    w_up,
    w_down,
    ln3_gain,
    w_learn1,
    w_learn2,
    cotangent,
):
    rows, width = patches.shape
    images = counts.shape[1]
    tokens = w_learn2.shape[1]
    capacity = row_capacity(rows, images, n_tensor)
    scale = HEAD_DIM**-0.5
    tensor_index = lax.axis_index("tensor")
    index = lax.axis_index("dp")
    heads = n_tensor * w_qkv.shape[2] // HEAD_DIM
    mate = lambda value: swap(value, "dp", n_dp, 1)

    turned = jnp.transpose(w_qkv, (1, 2, 0))
    piece_qkv = my_piece(turned, n_dp, index)
    far_a = gather_tensor([piece_qkv], n_tensor)
    pieces = [my_piece(w, n_dp, index) for w in (w_out[None], jnp.transpose(after(w_up, far_a))[None], w_down[None])]
    far_b = gather_tensor(pieces[:2], n_tensor)
    near_a = gather_links(far_a, n_dp)
    far_c = gather_tensor([after(pieces[2], far_b, *near_a)], n_tensor)
    near_b = gather_links(after(far_b, *near_a), n_dp)
    near_c = gather_links(after(far_c, *near_b), n_dp)
    shards = [turned, w_out[None], jnp.transpose(w_up)[None], w_down[None]]
    sizes = [(s.shape[0], s.shape[1] // (2 * n_dp)) for s in shards]
    owns = [own_units(s, n_dp, index) for s in shards]
    plane_a = gather_core(near_a, sizes[:1], n_dp, n_tensor)
    plane_b = gather_core(near_b, sizes[1:3], n_dp, n_tensor)
    plane_c = gather_core(near_c, sizes[3:], n_dp, n_tensor)
    full_qkv = [join(owns[0][c], plane_a[c][0], False) for c in range(2)]
    full_out = [join(owns[1][c], plane_b[c][0], False) for c in range(2)]
    full_up = [join(owns[2][c], plane_b[c][1], True) for c in range(2)]
    full_down = [join(owns[3][c], plane_c[c][0], True) for c in range(2)]

    place = place_images(counts, n_tensor)
    image, source = row_map(place, counts, tensor_index, capacity)
    pick = (source[:, None] == jnp.arange(rows, dtype=jnp.int32)[None, :]).astype(LOW)
    inputs = dot(pick, patches, 1, 0) + dot(pick, pos_embed, 1, 0)
    member = (image[:, None] == jnp.arange(images, dtype=jnp.int32)[None, :]).astype(WIDE)
    row_scale = jnp.sum(member * lax.rsqrt(counts[0].astype(WIDE))[None, :], axis=1)

    normed_one, inverse_one = layer_norm(inputs)
    low_one = (normed_one * ln1_gain).astype(LOW)
    qkv = [dot_low(w, low_one, 1, 1).reshape(3, heads, -1, capacity) for w in full_qkv]
    mixed_first, mixed_second, log_sums = attend(*qkv, image, scale)
    mixed = [m.reshape(-1, capacity) for m in (mixed_first, mixed_second)]
    hidden = inputs + dot(mixed[0], full_out[0], 0, 0) + dot(mixed[1], full_out[1], 0, 0)
    normed_two, inverse_two = layer_norm(hidden)
    low_two = (normed_two * ln2_gain).astype(LOW)
    mate_mixed, mate_one = mate(mixed[1]), mate(low_one)
    low_two = after(low_two, mate_mixed, mate_one)
    active, slope = [], []
    for w in full_up:
        value, rate = gelu_both(dot(low_two, w, 1, 1))
        active.append(value.astype(LOW))
        slope.append(rate.astype(LOW))
    output = hidden + dot(active[0], full_down[0], 1, 0) + dot(active[1], full_down[1], 1, 0)
    normed_three, inverse_three = layer_norm(output)
    low_three = (normed_three * ln3_gain).astype(LOW)
    mate_active, mate_two = mate(active[1]), mate(low_two)
    low_three = after(low_three, mate_active, mate_two)
    acted, learn_slope = gelu_both(dot(low_three, w_learn1, 1, 0))
    acted, learn_slope = acted.astype(LOW), learn_slope.astype(LOW)
    select = jax.nn.sigmoid(dot(acted, w_learn2, 1, 0))
    weights = (select * row_scale[:, None]).astype(LOW)
    table = (member.astype(LOW)[:, :, None] * weights[:, None, :]).reshape(capacity, images * tokens)
    low_out = output.astype(LOW)
    learned = dot_low(table, low_out, 0, 0)
    total = learned.astype(WIDE)
    for j in range(1, n_tensor):
        total = total + swap(learned, "tensor", n_tensor, j).astype(WIDE)
    learned = total.astype(LOW).reshape(images, tokens, width)

    grad_pooled = cotangent.reshape(images * tokens, width)
    grad_output = dot(table, grad_pooled, 1, 0)
    grad_table = dot(low_out, grad_pooled, 1, 1)
    grad_weights = jnp.sum(grad_table.reshape(capacity, images, tokens) * member[:, :, None], axis=1)
    grad_logits = (grad_weights * row_scale[:, None] * select * (1.0 - select)).astype(LOW)
    grad_learn2 = dot(grad_logits, acted, 0, 0)
    grad_inner = (dot(grad_logits, w_learn2, 1, 1) * learn_slope.astype(WIDE)).astype(LOW)
    side = width // 2
    three_keep = lax.dynamic_slice_in_dim(low_three, (index & 1) * side, side, 1)
    three_away = lax.dynamic_slice_in_dim(low_three, (1 - (index & 1)) * side, side, 1)
    grad_learn1 = (
        dot(three_keep, grad_inner, 0, 0) + dot(mate(three_away), mate(grad_inner), 0, 0)
    ).astype(LOW)
    grad_from_three, grad_gain3 = norm_back(
        dot(grad_inner, w_learn1, 1, 1), ln3_gain, normed_three, inverse_three
    )
    grad_output = grad_output + grad_from_three

    grad_fed = after(grad_output.astype(LOW), learned, grad_learn1)
    mate_fed = mate(grad_fed)
    grad_upper = [
        (dot(grad_fed, w, 1, 1) * s.astype(WIDE)).astype(LOW) for w, s in zip(full_down, slope)
    ]
    mate_upper = mate(grad_upper[1])
    grad_down = (dot(active[0], grad_fed, 0, 0) + dot(mate_active, mate_fed, 0, 0)).astype(LOW)
    units = functools.partial(split_units, n_dp=n_dp, n_tensor=n_tensor)
    share = lambda grad: split_shared(grad, n_dp, index)
    steps_a = link_sums([units(grad_down, 1, part_first=True), share(grad_learn1)], n_dp)
    sums_a = next(steps_a)
    grad_upper = [after(g, grad_down, mate_upper) for g in grad_upper]
    grad_from_two, grad_gain2 = norm_back(
        dot(grad_upper[0], full_up[0], 1, 0) + dot(grad_upper[1], full_up[1], 1, 0),
        ln2_gain,
        normed_two,
        inverse_two,
    )
    grad_hidden = grad_output + grad_from_two

    grad_attended = grad_hidden.astype(LOW)
    mate_attended = mate(grad_attended)
    grad_mixed = [dot_low(w, grad_attended, 1, 1).reshape(heads, -1, capacity) for w in full_out]
    grad_qkv = attend_back(*qkv, (mixed_first, mixed_second), grad_mixed, log_sums, image, scale)
    grad_qkv = [g.reshape(-1, capacity) for g in grad_qkv]
    mate_qkv = mate(grad_qkv[1])
    grad_qkv = [after(g, mate_attended, *sums_a[0], *sums_a[1]) for g in grad_qkv]
    grad_from_one, grad_gain1 = norm_back(
        dot(grad_qkv[0], full_qkv[0], 0, 0) + dot(grad_qkv[1], full_qkv[1], 0, 0),
        ln1_gain,
        normed_one,
        inverse_one,
    )
    near = (grad_hidden + grad_from_one).astype(LOW)

    grad_upper = [after(g, near) for g in grad_upper]
    grad_up = (dot(grad_upper[0], low_two, 0, 0) + dot(mate_upper, mate_two, 0, 0)).astype(LOW)
    grad_out = (dot(mixed[0], grad_attended, 1, 0) + dot(mate_mixed, mate_attended, 1, 0)).astype(LOW)
    grad_qkv_weight = (dot(grad_qkv[0], low_one, 1, 0) + dot(mate_qkv, mate_one, 1, 0)).astype(LOW)
    extra = jnp.concatenate([jnp.stack([grad_gain1, grad_gain2, grad_gain3]), grad_learn2])
    extra = jnp.pad(extra, ((0, 8 * n_dp - extra.shape[0]), (0, 0)))
    extra = (extra + mate(extra)).astype(LOW)

    passing = pass_on(near, n_tensor)
    moved = [next(passing)]
    for sums_a in steps_a:
        pass
    pair = [jnp.stack([a, b]) for a, b in zip(*sums_a)]
    moved[0] = after(moved[0][0], moved[0][1], pair[0]), moved[0][1]
    sum_a = reduce_tensor([after(pair[0], moved[0][0])], pair[1:], n_tensor)
    steps_b = link_sums(
        [
            units(after(grad_up, pair[0]), 1, part_first=True),
            units(grad_out, 1, part_first=False),
            units(grad_qkv_weight, 3, part_first=False),
            share(extra),
        ],
        n_dp,
    )
    for sums_b in steps_b:
        pass
    pair = [jnp.stack([a, b]) for a, b in zip(*sums_b)]
    for step in range(1, n_tensor - 2):
        moved.append(passing.send((after(moved[-1][0], sum_a), moved[-1][1])))
    sum_b = reduce_tensor([after(pair[0], *moved[-1])] + pair[1:3], pair[3:], n_tensor)
    seen_a = spread_plane(after(sum_a, pair[0]), n_dp)
    moved.append(passing.send((after(moved[-1][0], sum_b), moved[-1][1])))
    seen_b = spread_plane(sum_b, n_dp)

    def spans(seen, grads, split):
        at = 0
        for grad, parts in zip(grads, split):
            size = grad.shape[0] // (parts * n_dp)
            yield seen[:, :, :, at : at + size]
            at += size

    found_down, found_learn = spans(seen_a, (grad_down, grad_learn1), (n_tensor, 1))
    found_up, found_out, found_qkv, found_extra = spans(
        seen_b, (grad_up, grad_out, grad_qkv_weight, extra), (n_tensor, n_tensor, n_tensor, 1)
    )
    down_sum = place_units(found_down, 1, n_dp, index)[0]
    learn_sum = place_shared(found_learn, n_dp, index)
    up_sum = place_units(found_up, 1, n_dp, index)[0]
    out_sum = place_units(found_out, 1, n_dp, index)[0]
    qkv_sum = place_units(found_qkv, 3, n_dp, index)
    small = reorder(jnp.transpose(found_extra[:, 0], (1, 0, 2, 3)), 1, n_dp // 2, index // 2)
    small = small.reshape(-1, width).astype(WIDE)

    def back(blocks):
        sources = jnp.concatenate([b[0] for b in blocks])
        spot = (jnp.arange(rows, dtype=jnp.int32)[:, None] == sources[None, :]).astype(LOW)
        return dot(spot, jnp.concatenate([b[1] for b in blocks]), 1, 0)

    source_of = lambda device: row_map(place, counts, device, capacity)[1]
    blocks = [(source, near)]
    for step, (below, above) in enumerate(moved, 1):
        if 2 * step < n_tensor:
            blocks.append((source_of(tensor_index - step), below))
            blocks.append((source_of(tensor_index + step), above))
        else:
            merged = jnp.maximum(source_of(tensor_index - step), source_of(tensor_index + step))
            blocks.append((merged, below + above))
    input_grad = (back(blocks[:-1]) + back(blocks[-1:])).astype(LOW)
    return (
        learned,
        input_grad,
        small[0],
        jnp.transpose(qkv_sum.astype(WIDE), (2, 0, 1)),
        out_sum.astype(WIDE),
        small[1],
        jnp.transpose(up_sum.astype(WIDE)),
        down_sum.astype(WIDE),
        small[2],
        learn_sum.astype(WIDE),
        jnp.transpose(small[3 : 3 + tokens]),
    )


def solution(mesh):
    return jax.shard_map(
        functools.partial(local, mesh.shape["dp"], mesh.shape["tensor"]),
        mesh=mesh,
        in_specs=(
            P("dp", None),
            P("dp", None),
            P("dp", None),
            P(),
            P(None, None, "tensor"),
            P("tensor", None),
            P(),
            P(None, "tensor"),
            P("tensor", None),
            P(),
            P(),
            P(),
            P("dp", None, None),
        ),
        out_specs=(
            P("dp", None, None),
            P("dp", None),
            P(),
            P(None, None, "tensor"),
            P("tensor", None),
            P(),
            P(None, "tensor"),
            P("tensor", None),
            P(),
            P(),
            P(),
        ),
        check_vma=False,
    )
```

time: 1320 us -> 646 us (0.49)
  waiting for transfers between devices: 699 us -> 191 us
  matrix products: 319 us -> 144 us
  starting transfers between devices: 0.21 us -> 102 us
  other arithmetic: 128 us -> 63.8 us
  Pallas kernels: 0 us -> 39.5 us
  local copies, waits for them, and re-layouts: 119 us -> 91.4 us
  blocking collectives: 24 us -> 0 us
    psum x5 -> x0, waiting for transfers between devices: 699 us -> none  [the longest x1 158 us: local(): lax.psum(jnp.dot(mixed_flat, w_out, preferred_element_type=WIDE_TYPE).ast...]
    ppermute x0 -> x71, waiting for transfers between devices: none -> 191 us  [the longest x65 143 us: swap(): return lax.ppermute(value, axis, [(i, i ^ mask) for i in range(size)])]
    dot_general x49 -> x38, matrix products: 319 us -> 144 us  [dot(): lax.dot_general(left, right, (((left_dim,), (right_dim,)), ((), ())), pre...]
    ppermute x0 -> x71, starting transfers between devices: none -> 102 us  [the longest x65 64.8 us: swap(): return lax.ppermute(value, axis, [(i, i ^ mask) for i in range(size)])]
    dynamic_update_slice x8 -> x0, local copies, waits for them, and re-layouts: 80 us -> none  [the longest x4 40 us: one_block(): lax.dynamic_update_slice_in_dim(grad_values, value_window, key_start, 0)]
    reduce_sum x11 -> x2, other arithmetic: 45.3 us -> 0.82 us  [the longest x1 0.74 us: row_map(): source = jnp.sum(jnp.where(inside, start - offset + row + 1, 0), axis=1) - 1]
    unnamed x129 -> x270, local copies, waits for them, and re-layouts: 11.9 us -> 55.4 us
    convert_element_type x17 -> x29, other arithmetic: 59.1 us -> 17.9 us  [the longest x16 2.91 us: link_sums(): parts.append((keep.astype(WIDE) + piece.astype(WIDE)).astype(LOW))]
  transfers between devices with their start and end apart: 5 -> 71, of which waited for: 5 -> 23; matrix products, arithmetic and copies ran while one was open for 4% -> 35% of each run, Pallas kernels for 0% -> 6%
where the time goes in v1:
time: 646 us; the launch traced here: 636 us
  waiting for transfers between devices  191 us (30%)
  matrix products  144 us (22%)
  starting transfers between devices  102 us (16%)
  local copies, waits for them, and re-layouts  91.4 us (14%)
  other arithmetic  63.8 us (10%)
  Pallas kernels  39.5 us (6%)
    dot_general x38, matrix products, dot(): lax.dot_general(left, right, (((left_dim,), (right_dim,)), ((), ())), pre...  144 us
    ppermute x65, waiting for transfers between devices, swap(): return lax.ppermute(value, axis, [(i, i ^ mask) for i in range(size)])  143 us
    ppermute x65, starting transfers between devices, swap(): return lax.ppermute(value, axis, [(i, i ^ mask) for i in range(size)])  64.8 us
    unnamed x270, local copies, waits for them, and re-layouts  55.4 us
    ppermute x3, starting transfers between devices, pass_on(): lax.ppermute(below, 'tensor', [(i, i + 1) for i in range(n_tensor - 1)])  33.1 us
    ppermute x3, waiting for transfers between devices, pass_on(): lax.ppermute(above, 'tensor', [(i + 1, i) for i in range(n_tensor - 1)])  30.5 us
    pallas_call x1, Pallas kernels, attend_back(): pl.pallas_call(functools.partial(attend_back_kernel, scale), grid=(heads,...  23.6 us
    ppermute x3, waiting for transfers between devices, pass_on(): lax.ppermute(below, 'tensor', [(i, i + 1) for i in range(n_tensor - 1)])  17.6 us
  transfers between devices with their start and end apart: 71, of which 23 were waited for; matrix products, arithmetic and copies ran while one was open for 35% of the time, Pallas kernels for 6%

profile of v1, /device:TPU:0, one launch (start us, length us, event | category | flops | bytes accessed | tf_op | source)
XLA Modules:
  0.0 635.9 jit_solution(11363640972042255175)
XLA Ops:
  80.2 9.6 %collective-permute-done.10 = bf16[2,80,1024]{2,1,0:T(8,128)(2,1)} collective-permute-done((bf16[2,80,1024]{2,1,0:T(8,128)(2,1)}, bf16[2,80,1024]{2,1,0:T(8,128)(2,1)}, u32[]{:S(2)}, u32[]{:S(2)}) %collective-permute-start.10) | collective-permute-done | bytes 327712 | tf_op jit(solution)/shard_map/ppermute | solution.py:127
  106.0 12.5 %collective-permute-done.21 = bf16[2,64,1024]{2,1,0:T(8,128)(2,1)S(1)} collective-permute-done((bf16[2,64,1024]{2,1,0:T(8,128)(2,1)S(1)}, bf16[2,64,1024]{2,1,0:T(8,128)(2,1)S(1)}, u32[]{:S(2)}, u32[]{:S(2)}) %collective-permute-start.21) | collective-permute-done | bytes 262176 | tf_op jit(solution)/shard_map/ppermute | solution.py:127
  140.8 14.4 %attend.1 = (bf16[16,32,640]{2,1,0:T(8,128)(2,1)S(1)}, bf16[16,32,640]{2,1,0:T(8,128)(2,1)S(1)}, f32[16,1,640]{2,1,0:T(1,128)S(1)}) custom-call(bf16[3,16,32,640]{3,2,1,0:T(8,128)(2,1)S(1)} %bitcast.657, bf16[3,16,32,640]{3,2,1,0:T(8,128)(2,1)S(1)} %bitcast.659, s32[640,1]{1,0:T(8,128)S(1)} %copy-done.2, s32[1,640]{1,0:T(1,128)S(1)} %sub.122.row_ref), custom_call_target="tpu_custom_call" | custom-call | flops 13421772800 | bytes 5242880 | tf_op jit(solution)/shard_map/attend/pallas_call | solution.py:293
  177.1 11.1 %collective-permute-done.26 = bf16[2,3,64,1024]{3,2,1,0:T(8,128)(2,1)S(1)} collective-permute-done((bf16[2,3,64,1024]{3,2,1,0:T(8,128)(2,1)S(1)}, bf16[2,3,64,1024]{3,2,1,0:T(8,128)(2,1)S(1)}, u32[]{:S(2)}, u32[]{:S(2)}) %collective-permute-start.26) | collective-permute-done | bytes 786464 | tf_op jit(solution)/shard_map/ppermute | solution.py:127
  205.0 7.7 %multiply_convert_fusion.2 = (bf16[640,2048]{1,0:T(8,128)(2,1)}, f32[640,2048]{1,0:T(8,128)}) fusion(bf16[640,1024]{1,0:T(8,128)(2,1)} %multiply_convert_fusion.7, bf16[2048,1024]{1,0:T(8,128)(2,1)S(1)} %bitcast.743), kind=kOutput, calls=%fused_computation.29 | convolution fusion | flops 2690908160 | bytes 13369344 | tf_op jit(solution)/shard_map/dot_general | solution.py:43
  213.0 6.4 %multiply_convert_fusion.3 = (bf16[640,2048]{1,0:T(8,128)(2,1)S(1)}, f32[640,2048]{1,0:T(8,128)}) fusion(bf16[640,1024]{1,0:T(8,128)(2,1)} %multiply_convert_fusion.7, bf16[2048,1024]{1,0:T(8,128)(2,1)S(1)} %bitcast.739), kind=kOutput, calls=%fused_computation.31 | convolution fusion | flops 2690908160 | bytes 13369344 | tf_op jit(solution)/shard_map/dot_general | solution.py:43
  269.5 6.7 %multiply_convert_fusion = bf16[640,2048]{1,0:T(8,128)(2,1)S(1)} fusion(f32[640,2048]{1,0:T(8,128)S(1)} %bitcast.852, bf16[640,1024]{1,0:T(8,128)(2,1)} %get-tuple-element.43, bf16[2048,1024]{1,0:T(8,128)(2,1)S(1)} %bitcast.746), kind=kOutput, calls=%fused_computation.27 | convolution fusion | flops 2700083200 | bytes 13369344 | tf_op jit(solution)/shard_map/dot_general | solution.py:43
  285.3 13.3 %collective-permute-done.39 = bf16[640,1024]{1,0:T(8,128)(2,1)S(1)} collective-permute-done((bf16[640,1024]{1,0:T(8,128)(2,1)S(1)}, bf16[640,1024]{1,0:T(8,128)(2,1)S(1)}, u32[]{:S(2)}, u32[]{:S(2)}) %collective-permute-start.39) | collective-permute-done | bytes 1310752 | tf_op jit(solution)/shard_map/ppermute | solution.py:127
  301.5 7.2 %collective-permute-done.40 = bf16[640,1024]{1,0:T(8,128)(2,1)S(1)} collective-permute-done((bf16[640,1024]{1,0:T(8,128)(2,1)S(1)}, bf16[640,1024]{1,0:T(8,128)(2,1)S(1)}, u32[]{:S(2)}, u32[]{:S(2)}) %collective-permute-start.40) | collective-permute-done | bytes 1310752 | tf_op jit(solution)/shard_map/ppermute | solution.py:127
  325.5 23.6 %attend_back.1 = (bf16[3,16,32,640]{3,2,1,0:T(8,128)(2,1)S(1)}, bf16[3,16,32,640]{3,2,1,0:T(8,128)(2,1)}) custom-call(bf16[3,16,32,640]{3,2,1,0:T(8,128)(2,1)} %bitcast.658, bf16[3,16,32,640]{3,2,1,0:T(8,128)(2,1)} %bitcast.660, bf16[16,32,640]{2,1,0:T(8,128)(2,1)S(1)} %get-tuple-element.35.mixed_first_ref, ...), custom_call_target="tpu_custom_call" | custom-call | flops 33554432000 | bytes 10485760 | tf_op jit(solution)/shard_map/attend_back/pallas_call | solution.py:355
  349.5 7.1 %fusion.164 = f32[2048,1024]{1,0:T(8,128)} fusion(bf16[640,2048]{1,0:T(8,128)(2,1)S(1)} %copy-done.87, bf16[640,1024]{1,0:T(8,128)(2,1)} %collective-permute-done.30), kind=kOutput, calls=%fused_computation.546 | convolution fusion | flops 2684354560 | bytes 12320768 | tf_op jit(solution)/shard_map/dot_general | solution.py:43
  371.7 6.7 %add_convert_fusion.1 = bf16[2048,1024]{1,0:T(8,128)(2,1)S(1)} fusion(f32[2048,1024]{1,0:T(8,128)} %fusion.164, bf16[640,2048]{1,0:T(8,128)(2,1)S(1)} %copy-done.94, bf16[640,1024]{1,0:T(8,128)(2,1)} %multiply_convert_fusion.7), kind=kOutput, calls=%fused_computation.4 | convolution fusion | flops 2688548864 | bytes 16515072 | tf_op jit(solution)/shard_map/dot_general | solution.py:43
  401.2 21.9 %collective-permute-done.42 = bf16[640,1024]{1,0:T(8,128)(2,1)S(1)} collective-permute-done((bf16[640,1024]{1,0:T(8,128)(2,1)S(1)}, bf16[640,1024]{1,0:T(8,128)(2,1)S(1)}, u32[]{:S(2)}, u32[]{:S(2)}) %collective-permute-start.42) | collective-permute-done | bytes 1310752 | tf_op jit(solution)/shard_map/ppermute | solution.py:109
  429.5 8.0 %collective-permute-done.54 = bf16[1040,1024]{1,0:T(8,128)(2,1)S(1)} collective-permute-done((bf16[1040,1024]{1,0:T(8,128)(2,1)S(1)}, bf16[1040,1024]{1,0:T(8,128)(2,1)S(1)}, u32[]{:S(2)}, u32[]{:S(2)}) %collective-permute-start.54) | collective-permute-done | bytes 2129952 | tf_op jit(solution)/shard_map/ppermute | solution.py:127
  440.7 7.1 %collective-permute-done.52 = bf16[1040,1024]{1,0:T(8,128)(2,1)S(1)} collective-permute-done((bf16[1040,1024]{1,0:T(8,128)(2,1)S(1)}, bf16[1040,1024]{1,0:T(8,128)(2,1)S(1)}, u32[]{:S(2)}, u32[]{:S(2)}) %collective-permute-start.52) | collective-permute-done | bytes 2129952 | tf_op jit(solution)/shard_map/ppermute | solution.py:127
  452.6 12.8 %collective-permute-done.46 = bf16[2,128,1024]{2,1,0:T(8,128)(2,1)S(1)} collective-permute-done((bf16[2,128,1024]{2,1,0:T(8,128)(2,1)S(1)}, bf16[2,128,1024]{2,1,0:T(8,128)(2,1)S(1)}, u32[]{:S(2)}, u32[]{:S(2)}) %collective-permute-start.46) | collective-permute-done | bytes 524320 | tf_op jit(solution)/shard_map/ppermute | solution.py:127
  465.7 13.8 %collective-permute-start.48 = (bf16[640,1024]{1,0:T(8,128)(2,1)S(1)}, bf16[640,1024]{1,0:T(8,128)(2,1)S(1)}, u32[]{:S(2)}, u32[]{:S(2)}) collective-permute-start(bf16[640,1024]{1,0:T(8,128)(2,1)S(1)} %collective-permute-done.41), channel_id=1, source_target_pairs={{0,1},{1,2},{2,3},{4,5},{5,6},{6,7},{8,9},{9,10},{10,11},{12,13},{... | collective-permute-start | bytes 3932168 | tf_op jit(solution)/shard_map/ppermute | solution.py:108
  480.1 8.6 %collective-permute-done.49 = bf16[640,1024]{1,0:T(8,128)(2,1)S(1)} collective-permute-done((bf16[640,1024]{1,0:T(8,128)(2,1)S(1)}, bf16[640,1024]{1,0:T(8,128)(2,1)S(1)}, u32[]{:S(2)}, u32[]{:S(2)}) %collective-permute-start.49) | collective-permute-done | bytes 1310752 | tf_op jit(solution)/shard_map/ppermute | solution.py:109
  488.8 14.5 %collective-permute-done.48 = bf16[640,1024]{1,0:T(8,128)(2,1)S(1)} collective-permute-done((bf16[640,1024]{1,0:T(8,128)(2,1)S(1)}, bf16[640,1024]{1,0:T(8,128)(2,1)S(1)}, u32[]{:S(2)}, u32[]{:S(2)}) %collective-permute-start.48) | collective-permute-done | bytes 1310752 | tf_op jit(solution)/shard_map/ppermute | solution.py:108
  519.4 14.6 %collective-permute-done.56 = bf16[2,136,1024]{2,1,0:T(8,128)(2,1)} collective-permute-done((bf16[2,136,1024]{2,1,0:T(8,128)(2,1)}, bf16[2,136,1024]{2,1,0:T(8,128)(2,1)}, u32[]{:S(2)}, u32[]{:S(2)}) %collective-permute-start.56) | collective-permute-done | bytes 557088 | tf_op jit(solution)/shard_map/ppermute | solution.py:127
  535.6 16.5 %collective-permute-done.57 = bf16[2,136,1024]{2,1,0:T(8,128)(2,1)} collective-permute-done((bf16[2,136,1024]{2,1,0:T(8,128)(2,1)}, bf16[2,136,1024]{2,1,0:T(8,128)(2,1)}, u32[]{:S(2)}, u32[]{:S(2)}) %collective-permute-start.57) | collective-permute-done | bytes 557088 | tf_op jit(solution)/shard_map/ppermute | solution.py:127
  556.5 14.6 %fusion = f32[2048,1024]{1,0:T(8,128)} fusion(s32[2560]{0:T(1024)S(1)} %pad_add_fusion, bf16[640,1024]{1,0:T(8,128)(2,1)S(1)} %add.513, bf16[640,1024]{1,0:T(8,128)(2,1)} %copy-done.89, bf16[640,1024]{1,0:T(8,128)(2,1)} %copy-done.90, bf16[640,1024]{1,0:T(8,128)(2,1)S(1)} %copy-done.54), kind=kOutput, calls=%fused_computation.1 | convolution fusion | flops 10763632640 | bytes 13641728 | tf_op jit(solution)/shard_map/dot_general | solution.py:43
  571.1 14.7 %collective-permute-start.59 = (bf16[640,1024]{1,0:T(8,128)(2,1)S(1)}, bf16[640,1024]{1,0:T(8,128)(2,1)S(1)}, u32[]{:S(2)}, u32[]{:S(2)}) collective-permute-start(bf16[640,1024]{1,0:T(8,128)(2,1)S(1)} %copy-done.52), channel_id=1, source_target_pairs={{0,1},{1,2},{2,3},{4,5},{5,6},{6,7},{8,9},{9,10},{10,11},{12,13},{... | collective-permute-start | bytes 3932168 | tf_op jit(solution)/shard_map/ppermute | solution.py:108
  588.6 6.9 %collective-permute-done.62 = bf16[2,136,1024]{2,1,0:T(8,128)(2,1)S(1)} collective-permute-done((bf16[2,136,1024]{2,1,0:T(8,128)(2,1)S(1)}, bf16[2,136,1024]{2,1,0:T(8,128)(2,1)S(1)}, u32[]{:S(2)}, u32[]{:S(2)}) %collective-permute-start.62) | collective-permute-done | bytes 557088 | tf_op jit(solution)/shard_map/ppermute | solution.py:127
  (656 shorter events, 351.6 us)
Async XLA Ops:
  10.3 35.7 %collective-permute-start.2 = (bf16[2,48,1024]{2,1,0:T(8,128)(2,1)}, bf16[2,48,1024]{2,1,0:T(8,128)(2,1)S(1)}, u32[]{:S(2)}, u32[]{:S(2)}) collective-permute-start(bf16[2,48,1024]{2,1,0:T(8,128)(2,1)} %bitcast.11), channel_id=1, source_target_pairs={{0,3},{1,2},{2,1},{3,0},{4,7},{5,6},{6,5},{7,4},{8,11},{9,10},{10,... | collective-permute-start | bytes 589832 | tf_op jit(solution)/shard_map/ppermute | solution.py:127
  93.8 40.5 %collective-permute-start.8 = (bf16[4,3,48,1024]{3,2,1,0:T(8,128)(2,1)S(1)}, bf16[4,3,48,1024]{3,2,1,0:T(8,128)(2,1)S(1)}, u32[]{:S(2)}, u32[]{:S(2)}) collective-permute-start(bf16[4,3,48,1024]{3,2,1,0:T(8,128)(2,1)S(1)} %bitcast.730), channel_id=1, source_target_pairs={{0,4},{4,0},{8,12},{12,8},{16,20},{20,16},{24,28},{28,24},{1,5},{5... | collective-permute-start | bytes 3538952 | tf_op jit(solution)/shard_map/ppermute | solution.py:127
  93.9 40.4 %collective-permute-start.7 = (bf16[4,3,48,1024]{3,2,1,0:T(8,128)(2,1)S(1)}, bf16[4,3,48,1024]{3,2,1,0:T(8,128)(2,1)S(1)}, u32[]{:S(2)}, u32[]{:S(2)}) collective-permute-start(bf16[4,3,48,1024]{3,2,1,0:T(8,128)(2,1)S(1)} %bitcast.728), channel_id=1, source_target_pairs={{0,4},{4,0},{8,12},{12,8},{16,20},{20,16},{24,28},{28,24},{1,5},{5... | collective-permute-start | bytes 3538952 | tf_op jit(solution)/shard_map/ppermute | solution.py:127
  123.0 77.1 %collective-permute-start.19 = (bf16[640,1024]{1,0:T(8,128)(2,1)}, bf16[640,1024]{1,0:T(8,128)(2,1)}, u32[]{:S(2)}, u32[]{:S(2)}) collective-permute-start(bf16[640,1024]{1,0:T(8,128)(2,1)} %multiply_convert_fusion.8), channel_id=1, source_target_pairs={{0,4},{4,0},{8,12},{12,8},{16,20},{20,16},{24,28},{28,24},{1,5},{5... | collective-permute-start | bytes 3932168 | tf_op jit(solution)/shard_map/ppermute | solution.py:127
  159.7 31.9 %collective-permute-start.17 = (bf16[4,3,80,1024]{3,2,1,0:T(8,128)(2,1)S(1)}, bf16[4,3,80,1024]{3,2,1,0:T(8,128)(2,1)}, u32[]{:S(2)}, u32[]{:S(2)}) collective-permute-start(bf16[4,3,80,1024]{3,2,1,0:T(8,128)(2,1)S(1)} %bitcast.704), channel_id=1, source_target_pairs={{0,4},{4,0},{8,12},{12,8},{16,20},{20,16},{24,28},{28,24},{1,5},{5... | collective-permute-start | bytes 5898248 | tf_op jit(solution)/shard_map/ppermute | solution.py:127
  159.8 33.8 %collective-permute-start.16 = (bf16[4,3,80,1024]{3,2,1,0:T(8,128)(2,1)S(1)}, bf16[4,3,80,1024]{3,2,1,0:T(8,128)(2,1)}, u32[]{:S(2)}, u32[]{:S(2)}) collective-permute-start(bf16[4,3,80,1024]{3,2,1,0:T(8,128)(2,1)S(1)} %bitcast.701), channel_id=1, source_target_pairs={{0,4},{4,0},{8,12},{12,8},{16,20},{20,16},{24,28},{28,24},{1,5},{5... | collective-permute-start | bytes 5898248 | tf_op jit(solution)/shard_map/ppermute | solution.py:127
  200.1 34.1 %collective-permute-start.30 = (bf16[640,1024]{1,0:T(8,128)(2,1)}, bf16[640,1024]{1,0:T(8,128)(2,1)}, u32[]{:S(2)}, u32[]{:S(2)}) collective-permute-start(bf16[640,1024]{1,0:T(8,128)(2,1)} %multiply_convert_fusion.7), channel_id=1, source_target_pairs={{0,4},{4,0},{8,12},{12,8},{16,20},{20,16},{24,28},{28,24},{1,5},{5... | collective-permute-start | bytes 3932168 | tf_op jit(solution)/shard_map/ppermute | solution.py:127
  276.4 35.7 %collective-permute-start.37 = (bf16[640,2048]{1,0:T(8,128)(2,1)S(1)}, bf16[640,2048]{1,0:T(8,128)(2,1)S(1)}, u32[]{:S(2)}, u32[]{:S(2)}) collective-permute-start(bf16[640,2048]{1,0:T(8,128)(2,1)S(1)} %multiply_convert_fusion), channel_id=1, source_target_pairs={{0,4},{4,0},{8,12},{12,8},{16,20},{20,16},{24,28},{28,24},{1,5},{5... | collective-permute-start | bytes 7864328 | tf_op jit(solution)/shard_map/ppermute | solution.py:127
  300.0 58.9 %collective-permute-start.43 = (bf16[320,1024]{1,0:T(8,128)(2,1)}, bf16[320,1024]{1,0:T(8,128)(2,1)}, u32[]{:S(2)}, u32[]{:S(2)}) collective-permute-start(bf16[320,1024]{1,0:T(8,128)(2,1)} %pad_maximum_fusion.33), channel_id=1, source_target_pairs={{0,8},{4,12},{8,0},{12,4},{16,24},{20,28},{24,16},{28,20},{1,9},{5... | collective-permute-start | bytes 1966088 | tf_op jit(solution)/shard_map/ppermute | solution.py:127
  310.3 50.0 %collective-permute-start.44 = (bf16[320,1024]{1,0:T(8,128)(2,1)}, bf16[320,1024]{1,0:T(8,128)(2,1)}, u32[]{:S(2)}, u32[]{:S(2)}) collective-permute-start(bf16[320,1024]{1,0:T(8,128)(2,1)} %pad_maximum_fusion.34), channel_id=1, source_target_pairs={{0,16},{4,20},{8,24},{12,28},{16,0},{20,4},{24,8},{28,12},{1,17},{... | collective-permute-start | bytes 1966088 | tf_op jit(solution)/shard_map/ppermute | solution.py:127
  325.4 36.5 %collective-permute-start.38 = (bf16[640,1024]{1,0:T(8,128)(2,1)}, bf16[640,1024]{1,0:T(8,128)(2,1)S(1)}, u32[]{:S(2)}, u32[]{:S(2)}) collective-permute-start(bf16[640,1024]{1,0:T(8,128)(2,1)} %get-tuple-element.109), channel_id=1, source_target_pairs={{0,4},{4,0},{8,12},{12,8},{16,20},{20,16},{24,28},{28,24},{1,5},{5... | collective-permute-start | bytes 3932168 | tf_op jit(solution)/shard_map/ppermute | solution.py:127
  388.8 48.8 %collective-permute-start.54 = (bf16[1040,1024]{1,0:T(8,128)(2,1)S(1)}, bf16[1040,1024]{1,0:T(8,128)(2,1)S(1)}, u32[]{:S(2)}, u32[]{:S(2)}) collective-permute-start(bf16[1040,1024]{1,0:T(8,128)(2,1)S(1)} %pad_maximum_fusion.9), channel_id=1, source_target_pairs={{0,8},{4,12},{8,0},{12,4},{16,24},{20,28},{24,16},{28,20},{1,9},{5... | collective-permute-start | bytes 6389768 | tf_op jit(solution)/shard_map/ppermute | solution.py:127
  390.3 32.7 %collective-permute-start.42 = (bf16[640,1024]{1,0:T(8,128)(2,1)S(1)}, bf16[640,1024]{1,0:T(8,128)(2,1)S(1)}, u32[]{:S(2)}, u32[]{:S(2)}) collective-permute-start(bf16[640,1024]{1,0:T(8,128)(2,1)S(1)} %add_convert_fusion.4), channel_id=1, source_target_pairs={{1,0},{2,1},{3,2},{5,4},{6,5},{7,6},{9,8},{10,9},{11,10},{13,12},{... | collective-permute-start | bytes 3932168 | tf_op jit(solution)/shard_map/ppermute | solution.py:109
  391.6 32.6 %collective-permute-start.41 = (bf16[640,1024]{1,0:T(8,128)(2,1)S(1)}, bf16[640,1024]{1,0:T(8,128)(2,1)S(1)}, u32[]{:S(2)}, u32[]{:S(2)}) collective-permute-start(bf16[640,1024]{1,0:T(8,128)(2,1)S(1)} %add_convert_fusion.4), channel_id=1, source_target_pairs={{0,1},{1,2},{2,3},{4,5},{5,6},{6,7},{8,9},{9,10},{10,11},{12,13},{... | collective-permute-start | bytes 3932168 | tf_op jit(solution)/shard_map/ppermute | solution.py:108
  399.9 47.9 %collective-permute-start.52 = (bf16[1040,1024]{1,0:T(8,128)(2,1)S(1)}, bf16[1040,1024]{1,0:T(8,128)(2,1)S(1)}, u32[]{:S(2)}, u32[]{:S(2)}) collective-permute-start(bf16[1040,1024]{1,0:T(8,128)(2,1)S(1)} %pad_maximum_fusion.8), channel_id=1, source_target_pairs={{0,16},{4,20},{8,24},{12,28},{16,0},{20,4},{24,8},{28,12},{1,17},{... | collective-permute-start | bytes 6389768 | tf_op jit(solution)/shard_map/ppermute | solution.py:127
  427.1 38.3 %collective-permute-start.46 = (bf16[2,128,1024]{2,1,0:T(8,128)(2,1)S(1)}, bf16[2,128,1024]{2,1,0:T(8,128)(2,1)S(1)}, u32[]{:S(2)}, u32[]{:S(2)}) collective-permute-start(bf16[2,128,1024]{2,1,0:T(8,128)(2,1)S(1)} %get-tuple-element.207), channel_id=1, source_target_pairs={{0,2},{1,3},{2,0},{3,1},{4,6},{5,7},{6,4},{7,5},{8,10},{9,11},{10,... | collective-permute-start | bytes 1572872 | tf_op jit(solution)/shard_map/ppermute | solution.py:127
  427.7 37.7 %collective-permute-start.47 = (bf16[2,128,1024]{2,1,0:T(8,128)(2,1)S(1)}, bf16[2,128,1024]{2,1,0:T(8,128)(2,1)S(1)}, u32[]{:S(2)}, u32[]{:S(2)}) collective-permute-start(bf16[2,128,1024]{2,1,0:T(8,128)(2,1)S(1)} %get-tuple-element.208), channel_id=1, source_target_pairs={{0,3},{1,2},{2,1},{3,0},{4,7},{5,6},{6,5},{7,4},{8,11},{9,10},{10,... | collective-permute-start | bytes 1572872 | tf_op jit(solution)/shard_map/ppermute | solution.py:127
  437.5 51.2 %collective-permute-start.49 = (bf16[640,1024]{1,0:T(8,128)(2,1)S(1)}, bf16[640,1024]{1,0:T(8,128)(2,1)S(1)}, u32[]{:S(2)}, u32[]{:S(2)}) collective-permute-start(bf16[640,1024]{1,0:T(8,128)(2,1)S(1)} %collective-permute-done.42), channel_id=1, source_target_pairs={{1,0},{2,1},{3,2},{5,4},{6,5},{7,6},{9,8},{10,9},{11,10},{13,12},{... | collective-permute-start | bytes 3932168 | tf_op jit(solution)/shard_map/ppermute | solution.py:109
  465.7 37.6 %collective-permute-start.48 = (bf16[640,1024]{1,0:T(8,128)(2,1)S(1)}, bf16[640,1024]{1,0:T(8,128)(2,1)S(1)}, u32[]{:S(2)}, u32[]{:S(2)}) collective-permute-start(bf16[640,1024]{1,0:T(8,128)(2,1)S(1)} %collective-permute-done.41), channel_id=1, source_target_pairs={{0,1},{1,2},{2,3},{4,5},{5,6},{6,7},{8,9},{9,10},{10,11},{12,13},{... | collective-permute-start | bytes 3932168 | tf_op jit(solution)/shard_map/ppermute | solution.py:108
  512.0 40.1 %collective-permute-start.57 = (bf16[2,136,1024]{2,1,0:T(8,128)(2,1)}, bf16[2,136,1024]{2,1,0:T(8,128)(2,1)}, u32[]{:S(2)}, u32[]{:S(2)}) collective-permute-start(bf16[2,136,1024]{2,1,0:T(8,128)(2,1)} %get-tuple-element.218), channel_id=1, source_target_pairs={{0,2},{1,3},{2,0},{3,1},{4,6},{5,7},{6,4},{7,5},{8,10},{9,11},{10,... | collective-permute-start | bytes 1671176 | tf_op jit(solution)/shard_map/ppermute | solution.py:127
  512.6 39.5 %collective-permute-start.58 = (bf16[2,136,1024]{2,1,0:T(8,128)(2,1)}, bf16[2,136,1024]{2,1,0:T(8,128)(2,1)}, u32[]{:S(2)}, u32[]{:S(2)}) collective-permute-start(bf16[2,136,1024]{2,1,0:T(8,128)(2,1)} %get-tuple-element.219), channel_id=1, source_target_pairs={{0,3},{1,2},{2,1},{3,0},{4,7},{5,6},{6,5},{7,4},{8,11},{9,10},{10,... | collective-permute-start | bytes 1671176 | tf_op jit(solution)/shard_map/ppermute | solution.py:127
  515.0 83.8 %collective-permute-start.60 = (bf16[640,1024]{1,0:T(8,128)(2,1)S(1)}, bf16[640,1024]{1,0:T(8,128)(2,1)}, u32[]{:S(2)}, u32[]{:S(2)}) collective-permute-start(bf16[640,1024]{1,0:T(8,128)(2,1)S(1)} %collective-permute-done.49), channel_id=1, source_target_pairs={{1,0},{2,1},{3,2},{5,4},{6,5},{7,6},{9,8},{10,9},{11,10},{13,12},{... | collective-permute-start | bytes 3932168 | tf_op jit(solution)/shard_map/ppermute | solution.py:109
  517.6 70.5 %collective-permute-start.67 = (bf16[2,128,1024]{2,1,0:T(8,128)(2,1)S(1)}, bf16[2,128,1024]{2,1,0:T(8,128)(2,1)S(1)}, u32[]{:S(2)}, u32[]{:S(2)}) collective-permute-start(bf16[2,128,1024]{2,1,0:T(8,128)(2,1)S(1)} %get-tuple-element.186), channel_id=1, source_target_pairs={{0,16},{4,20},{8,24},{12,28},{16,0},{20,4},{24,8},{28,12},{1,17},{... | collective-permute-start | bytes 1572872 | tf_op jit(solution)/shard_map/ppermute | solution.py:127
  534.1 53.2 %collective-permute-start.69 = (bf16[2,128,1024]{2,1,0:T(8,128)(2,1)S(1)}, bf16[2,128,1024]{2,1,0:T(8,128)(2,1)S(1)}, u32[]{:S(2)}, u32[]{:S(2)}) collective-permute-start(bf16[2,128,1024]{2,1,0:T(8,128)(2,1)S(1)} %get-tuple-element.192), channel_id=1, source_target_pairs={{0,8},{4,12},{8,0},{12,4},{16,24},{20,28},{24,16},{28,20},{1,9},{5... | collective-permute-start | bytes 1572872 | tf_op jit(solution)/shard_map/ppermute | solution.py:127
  (150 other events, 2060.7 us)

commit v2 on v1

v2 whole, which is shorter than its diff:
```python
import functools

import jax
import jax.numpy as jnp
from jax import lax
from jax.experimental import pallas as pl
from jax.experimental.pallas import tpu as pltpu
from jax.sharding import PartitionSpec as P

HEAD_DIM = 64
MOST = 576
EPSILON = 1e-06
LOW = jnp.bfloat16
WIDE = jnp.float32
FAR = -1e30


def layer_norm(values):
    center = values - jnp.mean(values, axis=-1, keepdims=True)
    variance = jnp.mean(center * center, axis=-1, keepdims=True)
    inverse = lax.rsqrt(variance + EPSILON)
    return center * inverse, inverse


def norm_back(grad_in, gain, normed, inverse):
    gain_grad = jnp.sum(grad_in * normed, axis=0)
    scaled = grad_in * gain
    result = (
        scaled
        - jnp.mean(scaled, axis=-1, keepdims=True)
        - normed * jnp.mean(scaled * normed, axis=-1, keepdims=True)
    ) * inverse
    return result, gain_grad


def gelu_both(values):
    share = 0.5 * (1.0 + lax.erf(values * (0.5**0.5)))
    density = jnp.exp(-0.5 * values * values) * 0.3989422804014327
    return values * share, share + values * density


def dot(left, right, left_dim, right_dim):
    return lax.dot_general(
        left, right, (((left_dim,), (right_dim,)), ((), ())), preferred_element_type=WIDE
    )


def dot_low(left, right, left_dim, right_dim):
    return dot(left, right, left_dim, right_dim).astype(LOW)


def row_capacity(rows, images, n_tensor):
    if n_tensor >= images:
        most = MOST
    elif n_tensor == 4 and images == 8 and rows == 2048:
        most = 630
    else:
        most = rows // n_tensor + MOST
    return min(rows, -(-most // 128) * 128)


def place_kernel(n_tensor, counts_ref, place_ref):
    images = counts_ref.shape[1]
    count = [counts_ref[0, i] for i in range(images)]
    zero = count[0] * 0
    used, device, offset = [zero] * images, [zero] * images, [zero] * images
    loads = [zero] * n_tensor
    for _ in range(images):
        best, at = zero - 1, zero
        for i in range(images):
            better = jnp.logical_and(used[i] == 0, count[i] > best)
            best = jnp.where(better, count[i], best)
            at = jnp.where(better, i, at)
        least, least_at = loads[0], zero
        for b in range(1, n_tensor):
            better = loads[b] < least
            least = jnp.where(better, loads[b], least)
            least_at = jnp.where(better, b, least_at)
        for i in range(images):
            here = at == i
            used[i] = jnp.where(here, 1, used[i])
            device[i] = jnp.where(here, least_at, device[i])
            offset[i] = jnp.where(here, least, offset[i])
        for b in range(n_tensor):
            loads[b] = loads[b] + jnp.where(least_at == b, best, 0)
    start = zero
    for i in range(images):
        place_ref[0, i] = device[i]
        place_ref[1, i] = offset[i]
        place_ref[2, i] = start
        start = start + count[i]


def place_images(counts, n_tensor):
    images = counts.shape[1]
    return pl.pallas_call(
        functools.partial(place_kernel, n_tensor),
        out_shape=jax.ShapeDtypeStruct((3, images), jnp.int32),
        in_specs=[pl.BlockSpec(memory_space=pltpu.SMEM)],
        out_specs=pl.BlockSpec(memory_space=pltpu.SMEM),
        name="place_images",
    )(counts)


def gather_rows(rows, n_tensor):
    held = rows[None]
    mask = n_tensor // 2
    while mask:
        (came,) = yield [swap(held, "tensor", n_tensor, mask)], [held]
        held = jnp.stack([held, came], axis=1).reshape((-1,) + rows.shape)
        mask //= 2
    yield [held], []


def row_map(place, counts, device, capacity):
    row = jnp.arange(capacity, dtype=jnp.int32)[:, None]
    offset, start = place[1][None], place[2][None]
    inside = (place[0][None] == device) & (row >= offset) & (row < offset + counts)
    image = jnp.sum(jnp.where(inside, jnp.arange(counts.shape[1], dtype=jnp.int32) + 1, 0), axis=1) - 1
    source = jnp.sum(jnp.where(inside, start - offset + row + 1, 0), axis=1) - 1
    return image, source


def after(value, *others):
    return lax.optimization_barrier((value,) + others)[0]


class Flow:
    def __init__(self, stages, generator):
        self.left = stages
        self.generator = generator
        self.came, self.sent = next(generator)

    def go(self, *others):
        self.came, self.sent = self.generator.send([after(c, *others) for c in self.came])
        self.left -= 1
        return self

    def finish(self, *others):
        while self.left:
            self.go(*others)
        return self.came


def swap(value, axis, size, mask):
    return lax.ppermute(value, axis, [(i, i ^ mask) for i in range(size)])


def reorder(value, dim, size, index):
    return jnp.concatenate(
        [lax.dynamic_slice_in_dim(value, index ^ m, 1, dim) for m in range(size)], axis=dim
    )


def link_bits(n_dp, half):
    bits = list(range(1, n_dp.bit_length() - 1))
    return bits[::-1] if half else bits


def link_gathers(far, n_dp):
    value = [far[0], far[1]]
    for step in range(n_dp.bit_length() - 2):
        came = [swap(value[half], "dp", n_dp, 1 << link_bits(n_dp, half)[step]) for half in range(2)]
        came = yield came, value
        value = [jnp.stack([v, c]) for v, c in zip(value, came)]
    yield value, []


def links_first(value, n_dp):
    count = n_dp.bit_length() - 2
    turned = jnp.transpose(value[1], tuple(range(count))[::-1] + tuple(range(count, value[1].ndim)))
    return [v.reshape((1 << count,) + v.shape[count:]) for v in (value[0], turned)]


def own_units(shard, n_dp, index):
    lead, units, width = shard.shape
    part = units // (2 * n_dp)
    split = shard.reshape(lead, n_dp, 2, part, width)
    ordered = reorder(split, 1, n_dp, index).reshape(lead, n_dp // 2, 2, 2, part, width)
    return [ordered[:, :, core] for core in range(2)]


def my_piece(shard, n_dp, index):
    lead, units, width = shard.shape
    part = units // (2 * n_dp)
    split = shard.reshape(lead, n_dp, 2, part, width)
    mine = lax.dynamic_slice_in_dim(split, index, 1, 1)[:, 0]
    return jnp.transpose(mine, (1, 0, 2, 3)).reshape(2, lead * part, width)


def gather_tensor(pieces, n_tensor):
    pack = jnp.concatenate(pieces, axis=1) if len(pieces) > 1 else pieces[0]
    came = yield [swap(pack, "tensor", n_tensor, j) for j in range(1, n_tensor)], [pack]
    yield [jnp.stack(came, axis=1)], []


def far_units(halves, sizes, n_dp, n_tensor):
    width = halves[0].shape[-1]
    weights, at = [], 0
    for lead, part in sizes:
        pieces = [
            h[:, :, at : at + lead * part].reshape(n_dp // 2, n_tensor - 1, lead, part, width) for h in halves
        ]
        weights.append(jnp.transpose(jnp.stack(pieces), (3, 2, 1, 0, 4, 5)))
        at += lead * part
    return weights


def join(own, far, part_first):
    width = own.shape[-1]
    full = jnp.concatenate([own[:, None], far], axis=1)
    if part_first:
        full = jnp.transpose(full, (3, 0, 2, 1, 4, 5))
    return full.reshape(-1, width)


def split_units(grad, lead, n_dp, n_tensor, part_first):
    width = grad.shape[-1]
    links = n_dp // 2
    if part_first:
        parts = grad.reshape(2, links, -1, width)
        return [parts[0], parts[1]]
    split = grad.reshape(lead, n_tensor, links, 2, -1, width)
    return [
        jnp.transpose(split[:, :, :, half], (2, 1, 0, 3, 4)).reshape(links, -1, width) for half in range(2)
    ]


def split_shared(grad, n_dp, index):
    links = n_dp // 2
    parts = grad.reshape(2, links, -1, grad.shape[-1])
    ordered = reorder(parts, 1, links, index // 2)
    return [ordered[0], ordered[1]]


def link_sums(groups, n_dp):
    width = groups[0][0].shape[-1]
    bits = n_dp.bit_length() - 2
    halves = [[g[half].reshape((2,) * bits + g[half].shape[1:]) for g in groups] for half in range(2)]
    held = [list(range(bits, 0, -1)) for _ in range(2)]
    keeps, aways = [], []
    for half in range(2):
        dim = held[half].index(link_bits(n_dp, 1 - half)[0])
        keeps.append([lax.index_in_dim(p, 0, dim, keepdims=False) for p in halves[half]])
        aways.append(join_rows([lax.index_in_dim(p, 1, dim, keepdims=False).reshape(-1, width) for p in halves[half]]))
    yield from link_sums_from(keeps, aways, n_dp)


def join_rows(items):
    return jnp.concatenate(items) if len(items) > 1 else items[0]


def link_sums_from(keeps, aways, n_dp):
    width = aways[0].shape[-1]
    bits = n_dp.bit_length() - 2
    held = [list(range(bits, 0, -1)) for _ in range(2)]
    for step in range(bits):
        came = []
        for half in range(2):
            bit = link_bits(n_dp, 1 - half)[step]
            held[half].remove(bit)
            came.append(swap(aways[half], "dp", n_dp, 1 << bit))
        came = yield came, aways
        halves = []
        for half in range(2):
            at, summed = 0, []
            for keep in keeps[half]:
                size = keep.size // width
                piece = came[half][at : at + size].reshape(keep.shape)
                summed.append((keep.astype(WIDE) + piece.astype(WIDE)).astype(LOW))
                at += size
            halves.append(summed)
        if step + 1 == bits:
            break
        keeps, aways = [], []
        for half in range(2):
            dim = held[half].index(link_bits(n_dp, 1 - half)[step + 1])
            keeps.append([lax.index_in_dim(p, 0, dim, keepdims=False) for p in halves[half]])
            away = [lax.index_in_dim(p, 1, dim, keepdims=False).reshape(-1, width) for p in halves[half]]
            aways.append(join_rows(away))
    yield [jnp.stack([a, b]) for a, b in zip(*halves)], []


def first_split(n_dp, away):
    links = n_dp // 2
    return [
        [m for m in range(links) if bool(m >> (link_bits(n_dp, 1 - half)[0] - 1) & 1) == away] for half in range(2)
    ]


def reduce_tensor(scattered, shared, n_tensor):
    width = (scattered + shared)[0].shape[-1]
    held = [s.reshape(2, n_tensor, -1, width) for s in scattered]
    mask = 1
    while mask < n_tensor:
        split = [h.reshape(2, -1, 2, h.shape[2], width) for h in held]
        flat = [h[:, :, 1].reshape(2, -1, width) for h in split] + shared
        flat = jnp.concatenate(flat, axis=1) if len(flat) > 1 else flat[0]
        (came,) = yield [swap(flat, "tensor", n_tensor, mask)], [flat]
        summed, at = [], 0
        for keep in [h[:, :, 0] for h in split] + shared:
            size = keep.size // (2 * width)
            piece = came[:, at : at + size].reshape(keep.shape)
            summed.append((keep.astype(WIDE) + piece.astype(WIDE)).astype(LOW))
            at += size
        held, shared = summed[: len(held)], summed[len(held) :]
        mask *= 2
    parts = [h[:, 0] for h in held] + shared
    yield [jnp.concatenate(parts, axis=1) if len(parts) > 1 else parts[0]], []


def both_near(value, n_dp):
    near = [v.reshape((n_dp // 2,) + v.shape[-2:]) for v in value]
    return [near, [swap(n, "dp", n_dp, 1) for n in near]]


def backwards(number, bits):
    result = 0
    for _ in range(bits):
        result, number = result * 2 + number % 2, number // 2
    return result


def shared_kernel(index_ref, near_a, near_b, far_a, far_b, out_ref):
    links, rows, _ = near_a.shape
    index = index_ref[0]
    for core, refs in enumerate(((near_a, near_b), (far_a, far_b))):
        for half, ref in enumerate(refs):
            for link in range(links):
                spot = (((core ^ index) & 1) * 2 + half) * links + (link ^ (index >> 1))
                at = backwards(link, links.bit_length() - 1) if half else link
                out_ref[pl.ds(pl.multiple_of(spot * rows, rows), rows), :] = ref[at].astype(WIDE)


def place_shared(seen, at, rows, n_dp, index):
    (near_a, near_b), (far_a, far_b) = seen
    return pl.pallas_call(
        shared_kernel,
        out_shape=jax.ShapeDtypeStruct((2 * n_dp * rows, near_a.shape[-1]), WIDE),
        in_specs=[pl.BlockSpec(memory_space=pltpu.SMEM)] + [pl.BlockSpec(memory_space=pltpu.VMEM)] * 4,
        out_specs=pl.BlockSpec(memory_space=pltpu.VMEM),
        compiler_params=pltpu.CompilerParams(vmem_limit_bytes=32 << 20),
        name="place_shared",
    )(index[None], *[v[:, at : at + rows] for v in (near_a, near_b, far_a, far_b)])


def turn_kernel(turned, index_ref, near_a, near_b, far_a, far_b, out_ref, held):
    links, lead, rows, _ = near_a.shape
    index = index_ref[0]
    for i in range(lead):
        for core, refs in enumerate(((near_a, near_b), (far_a, far_b))):
            for half, ref in enumerate(refs):
                for link in range(links):
                    spot = ((2 * link + core) ^ index) * (2 * rows) + half * rows
                    at = backwards(link, links.bit_length() - 1) if half else link
                    held[pl.ds(pl.multiple_of(spot, rows), rows), :] = ref[at, i].astype(WIDE)
        out_ref[i] = held[...].T if turned else held[...]


def place_units(seen, at, lead, rows, n_dp, index, turned):
    (near_a, near_b), (far_a, far_b) = seen
    width = near_a.shape[-1]
    links = n_dp // 2
    shaped = [v[:, at : at + lead * rows].reshape(links, lead, rows, width) for v in (near_a, near_b, far_a, far_b)]
    units = 4 * rows * links
    if rows % 8:
        flips = [backwards(link, links.bit_length() - 1) for link in range(links)]
        crossed = lambda v: jnp.stack([v[at] for at in flips])
        parts = [shaped[0], crossed(shaped[1]), shaped[2], crossed(shaped[3])]
        pieces = jnp.transpose(jnp.stack(parts, axis=1), (2, 0, 1, 3, 4))
        pieces = reorder(pieces.reshape(lead, n_dp, 2 * rows, width), 1, n_dp, index)
        pieces = pieces.reshape(lead, units, width).astype(WIDE)
        return jnp.swapaxes(pieces, 1, 2) if turned else pieces
    return pl.pallas_call(
        functools.partial(turn_kernel, turned),
        out_shape=jax.ShapeDtypeStruct((lead, width, units) if turned else (lead, units, width), WIDE),
        in_specs=[pl.BlockSpec(memory_space=pltpu.SMEM)] + [pl.BlockSpec(memory_space=pltpu.VMEM)] * 4,
        out_specs=pl.BlockSpec(memory_space=pltpu.VMEM),
        scratch_shapes=[pltpu.VMEM((units, width), WIDE)],
        compiler_params=pltpu.CompilerParams(vmem_limit_bytes=32 << 20),
        name="place_units",
    )(index[None], *shaped)


SMALL_COST = pl.CostEstimate(flops=0, bytes_accessed=0, transcendentals=0)
VMEM = pltpu.CompilerParams(vmem_limit_bytes=48 << 20)
TILE = 1024


def pair_kernel(dim, left_ref, right_ref, left_mate_ref, right_mate_ref, out_ref):
    total = dot(left_ref[...], right_ref[...], dim, 0) + dot(left_mate_ref[...], right_mate_ref[...], dim, 0)
    out_ref[...] = total.astype(LOW)


def pair_product(left, right, left_mate, right_mate, dim):
    units = left.shape[1 - dim]
    rows, width = right.shape
    tile = next(units // n for n in range(1, units) if units % n == 0 and units // n <= TILE)
    if dim:
        block = pl.BlockSpec((tile, rows), lambda i: (i, 0))
    else:
        block = pl.BlockSpec((rows, tile), lambda i: (0, i))
    whole = pl.BlockSpec((rows, width), lambda i: (0, 0))
    return pl.pallas_call(
        functools.partial(pair_kernel, dim),
        grid=(units // tile,),
        in_specs=[block, whole, block, whole],
        out_specs=pl.BlockSpec((tile, width), lambda i: (i, 0)),
        out_shape=jax.ShapeDtypeStruct((units, width), LOW),
        compiler_params=VMEM,
        cost_estimate=SMALL_COST,
        name="pair_product",
    )(left, right, left_mate, right_mate)


def split_kernel(picks, tile, learn, *refs):
    left, right, left_mate, right_mate = refs[:4]
    outs = refs[-2:]
    if learn:
        index_ref, extra = refs[4], refs[5]
        if learn == "make":
            learn_left, learn_right, learn_left_mate, learn_right_mate = refs[5:9]
            extra = refs[9]
            outs = refs[10:12]
            extra[...] = (
                dot(learn_left[...], learn_right[...], 0, 0) + dot(learn_left_mate[...], learn_right_mate[...], 0, 0)
            ).astype(LOW)
        links = left.shape[1] // (2 * tile)
        rows = extra.shape[0] // (2 * links)
    for half, (some, out) in enumerate(zip(picks, outs)):
        at = 0
        for link in some:
            spot = half * (left.shape[1] // 2) + link * tile
            columns = slice(spot, spot + tile)
            total = dot(left[:, columns], right[...], 0, 0) + dot(left_mate[:, columns], right_mate[...], 0, 0)
            out[at : at + tile] = total.astype(LOW)
            at += tile
            if learn:
                source = (half * links + (link ^ (index_ref[0] // 2))) * rows
                out[at : at + rows] = extra[pl.ds(pl.multiple_of(source, rows), rows)]
                at += rows


def split_product(left, right, left_mate, right_mate, picks, links, index=None, learn=None):
    tile = left.shape[1] // (2 * links)
    width = right.shape[1]
    rows = tile
    args = [left, right, left_mate, right_mate]
    specs = [pl.BlockSpec(memory_space=pltpu.VMEM)] * 4
    out_shape = []
    if learn is not None:
        args += [index[None], *learn]
        specs += [pl.BlockSpec(memory_space=pltpu.SMEM)] + [pl.BlockSpec(memory_space=pltpu.VMEM)] * len(learn)
        units = learn[0].shape[1] if len(learn) > 1 else learn[0].shape[0]
        rows += units // (2 * links)
        if len(learn) > 1:
            out_shape.append(jax.ShapeDtypeStruct((units, width), LOW))
    mode = None if learn is None else "make" if len(learn) > 1 else "take"
    out_shape += [jax.ShapeDtypeStruct((len(some) * rows, width), LOW) for some in picks]
    return pl.pallas_call(
        functools.partial(split_kernel, picks, tile, mode),
        out_shape=out_shape,
        in_specs=specs,
        out_specs=[pl.BlockSpec(memory_space=pltpu.VMEM)] * len(out_shape),
        compiler_params=VMEM,
        cost_estimate=SMALL_COST,
        name="split_product",
    )(*args)


def back_kernel(count, source_ref, *refs):
    rows = refs[-1].shape[0]
    row = pl.program_id(0) * rows + lax.broadcasted_iota(jnp.int32, (rows, source_ref.shape[1]), 0)
    spot = (row == source_ref[...]).astype(WIDE).astype(LOW)
    total, at = 0.0, 0
    for ref in refs[:count]:
        total = total + dot(spot[:, at : at + ref.shape[0]], ref[...], 1, 0)
        at += ref.shape[0]
    if len(refs) > count + 1:
        total = total + refs[count][...].astype(WIDE)
    refs[-1][...] = total.astype(LOW)


def rows_home(blocks, rows, base=None):
    sources = jnp.concatenate([b[0] for b in blocks])[None]
    values = [b[1] for b in blocks]
    width = values[0].shape[1]
    tile = min(256, rows)
    whole = lambda array: pl.BlockSpec(array.shape, lambda i: (0, 0))
    block = pl.BlockSpec((tile, width), lambda i: (i, 0))
    return pl.pallas_call(
        functools.partial(back_kernel, len(values)),
        grid=(rows // tile,),
        in_specs=[whole(sources)] + [whole(v) for v in values] + ([] if base is None else [block]),
        out_specs=block,
        out_shape=jax.ShapeDtypeStruct((rows, width), LOW),
        compiler_params=VMEM,
        cost_estimate=SMALL_COST,
        name="rows_home",
    )(sources, *values, *([] if base is None else [base]))


def rows_back_kernel(first_ref, second_ref, w_first_ref, w_second_ref, base_ref, normed_ref, inverse_ref, gain_ref, wide_ref, low_ref, gain_grad_ref, held):
    step = pl.program_id(0)
    held[step] = dot(first_ref[...], w_first_ref[...], 1, 0) + dot(second_ref[...], w_second_ref[...], 1, 0)

    @pl.when(step == pl.num_programs(0) - 1)
    def _():
        count, _, tile = held.shape
        parts = [slice(i * tile, (i + 1) * tile) for i in range(count)]
        mean, cross = 0.0, 0.0
        for i, part in enumerate(parts):
            normed = normed_ref[:, part]
            product = held[i] * normed
            gain_grad_ref[:, part] = jnp.sum(product, axis=0, keepdims=True)
            gain = gain_ref[:, part]
            mean = mean + jnp.sum(held[i] * gain, axis=1, keepdims=True)
            cross = cross + jnp.sum(product * gain, axis=1, keepdims=True)
        mean, cross = mean / (count * tile), cross / (count * tile)
        for i, part in enumerate(parts):
            scaled = held[i] * gain_ref[:, part]
            total = base_ref[:, part] + (scaled - mean - normed_ref[:, part] * cross) * inverse_ref[...]
            wide_ref[:, part] = total
            low_ref[:, part] = total.astype(LOW)


def rows_back(grads, weights, base, normed, inverse, gain):
    rows, width = base.shape
    units = grads[0].shape[1]
    tile = min(256, width)
    whole = lambda *shape: pl.BlockSpec(shape, lambda i: (0,) * len(shape))
    columns = pl.BlockSpec((units, tile), lambda i: (0, i))
    return pl.pallas_call(
        rows_back_kernel,
        grid=(width // tile,),
        in_specs=[
            whole(rows, units),
            whole(rows, units),
            columns,
            columns,
            whole(rows, width),
            whole(rows, width),
            whole(rows, 1),
            whole(1, width),
        ],
        out_specs=[whole(rows, width), whole(rows, width), whole(1, width)],
        out_shape=[
            jax.ShapeDtypeStruct((rows, width), WIDE),
            jax.ShapeDtypeStruct((rows, width), LOW),
            jax.ShapeDtypeStruct((1, width), WIDE),
        ],
        scratch_shapes=[pltpu.VMEM((width // tile, rows, tile), WIDE)],
        compiler_params=VMEM,
        cost_estimate=SMALL_COST,
        name="rows_back",
    )(*grads, *weights, base, normed, inverse, gain[None])


def two_kernel(first_ref, second_ref, right_ref, out_first_ref, out_second_ref):
    right = right_ref[...]
    out_first_ref[...] = dot(first_ref[...], right, 1, 1).astype(LOW)
    out_second_ref[...] = dot(second_ref[...], right, 1, 1).astype(LOW)


def two_products(weights, right):
    return pl.pallas_call(
        two_kernel,
        out_shape=[jax.ShapeDtypeStruct((w.shape[0], right.shape[0]), LOW) for w in weights],
        compiler_params=VMEM,
        cost_estimate=SMALL_COST,
        name="two_products",
    )(*weights, right)


def attend_kernel(scale, first_ref, second_ref, column_ref, row_ref, mixed_first_ref, mixed_second_ref, log_ref):
    query, key, value = [jnp.concatenate([first_ref[i, 0], second_ref[i, 0]]) for i in range(3)]
    scores = dot(key, query * scale, 0, 0)
    scores = jnp.where(column_ref[...] == row_ref[...], scores, FAR)
    most = jnp.max(scores, axis=0, keepdims=True)
    exponent = jnp.exp(scores - most)
    total = jnp.sum(exponent, axis=0, keepdims=True)
    mixed = (dot(value, exponent.astype(LOW), 1, 0) / total).astype(LOW)
    half = mixed.shape[0] // 2
    mixed_first_ref[0] = mixed[:half]
    mixed_second_ref[0] = mixed[half:]
    log_ref[0] = most + jnp.log(total)


def attend(first, second, image, scale):
    _, heads, half, rows = first.shape
    three = pl.BlockSpec((3, 1, half, rows), lambda h: (0, h, 0, 0))
    one = pl.BlockSpec((1, half, rows), lambda h: (h, 0, 0))
    return pl.pallas_call(
        functools.partial(attend_kernel, scale),
        grid=(heads,),
        in_specs=[
            three,
            three,
            pl.BlockSpec((rows, 1), lambda h: (0, 0)),
            pl.BlockSpec((1, rows), lambda h: (0, 0)),
        ],
        out_specs=[one, one, pl.BlockSpec((1, 1, rows), lambda h: (h, 0, 0))],
        out_shape=[
            jax.ShapeDtypeStruct((heads, half, rows), LOW),
            jax.ShapeDtypeStruct((heads, half, rows), LOW),
            jax.ShapeDtypeStruct((heads, 1, rows), WIDE),
        ],
        compiler_params=pltpu.CompilerParams(vmem_limit_bytes=48 << 20),
        cost_estimate=SMALL_COST,
        name="attend",
    )(first, second, image[:, None], image[None, :])


def attend_back_kernel(
    scale,
    first_ref,
    second_ref,
    mixed_first_ref,
    mixed_second_ref,
    grad_first_ref,
    grad_second_ref,
    log_ref,
    column_ref,
    row_ref,
    out_first_ref,
    out_second_ref,
):
    query, key, value = [jnp.concatenate([first_ref[i, 0], second_ref[i, 0]]) for i in range(3)]
    query = query * scale
    mixed = jnp.concatenate([mixed_first_ref[0], mixed_second_ref[0]])
    grad = jnp.concatenate([grad_first_ref[0], grad_second_ref[0]])
    scores = dot(key, query, 0, 0)
    scores = jnp.where(column_ref[...] == row_ref[...], scores, FAR)
    probs = jnp.exp(scores - log_ref[0])
    grad_probs = dot(value, grad, 0, 0)
    inner = jnp.sum(mixed.astype(WIDE) * grad.astype(WIDE), axis=0, keepdims=True)
    grad_scores = (probs * (grad_probs - inner)).astype(LOW)
    grads = (
        (dot(key, grad_scores, 1, 0) * scale).astype(LOW),
        dot(query, grad_scores, 1, 1).astype(LOW),
        dot(grad, probs.astype(LOW), 1, 1).astype(LOW),
    )
    half = mixed.shape[0] // 2
    for i, item in enumerate(grads):
        out_first_ref[i, 0] = item[:half]
        out_second_ref[i, 0] = item[half:]


def attend_back(first, second, mixed, grad_mixed, log_sums, image, scale):
    _, heads, half, rows = first.shape
    three = pl.BlockSpec((3, 1, half, rows), lambda h: (0, h, 0, 0))
    one = pl.BlockSpec((1, half, rows), lambda h: (h, 0, 0))
    return pl.pallas_call(
        functools.partial(attend_back_kernel, scale),
        grid=(heads,),
        in_specs=[
            three,
            three,
            one,
            one,
            one,
            one,
            pl.BlockSpec((1, 1, rows), lambda h: (h, 0, 0)),
            pl.BlockSpec((rows, 1), lambda h: (0, 0)),
            pl.BlockSpec((1, rows), lambda h: (0, 0)),
        ],
        out_specs=[three, three],
        out_shape=[jax.ShapeDtypeStruct((3, heads, half, rows), LOW)] * 2,
        compiler_params=pltpu.CompilerParams(vmem_limit_bytes=48 << 20),
        cost_estimate=SMALL_COST,
        name="attend_back",
    )(first, second, *mixed, *grad_mixed, log_sums, image[:, None], image[None, :])


def local(
    n_dp,
    n_tensor,
    patches,
    pos_embed,
    counts,
    ln1_gain,
    w_qkv,
    w_out,
    ln2_gain,
    w_up,
    w_down,
    ln3_gain,
    w_learn1,
    w_learn2,
    cotangent,
):
    rows, width = patches.shape
    images = counts.shape[1]
    tokens = w_learn2.shape[1]
    capacity = row_capacity(rows, images, n_tensor)
    scale = HEAD_DIM**-0.5
    tensor_index = lax.axis_index("tensor")
    index = lax.axis_index("dp")
    heads = n_tensor * w_qkv.shape[2] // HEAD_DIM
    mate = lambda value: swap(value, "dp", n_dp, 1)

    links = n_dp.bit_length() - 2
    spans = n_tensor.bit_length() - 1
    turned = jnp.transpose(w_qkv, (1, 2, 0))
    z_a = Flow(1, gather_tensor([my_piece(turned, n_dp, index)], n_tensor))
    place = place_images(counts, n_tensor)
    image, source = row_map(place, counts, tensor_index, capacity)
    part_up = w_up.shape[1] // n_dp
    piece_up = jnp.transpose(lax.dynamic_slice_in_dim(w_up, index * part_up, part_up, 1))
    pieces = [my_piece(w_out[None], n_dp, index), piece_up.reshape(2, part_up // 2, width)]
    piece_down = my_piece(w_down[None], n_dp, index)
    (far_a,) = z_a.finish(source)
    x_a = Flow(links, link_gathers(far_a, n_dp))
    z_b = Flow(1, gather_tensor([after(p, far_a) for p in pieces], n_tensor))
    pick = (after(source, far_a)[:, None] == jnp.arange(rows, dtype=jnp.int32)[None, :]).astype(LOW)
    inputs = dot(pick, patches, 1, 0) + dot(pick, pos_embed, 1, 0)
    normed_one, inverse_one = layer_norm(inputs)
    low_one = (normed_one * ln1_gain).astype(LOW)
    x_a.go(low_one)
    own_qkv = own_units(after(turned, *x_a.sent), n_dp, index)
    own_up = own_units(jnp.transpose(after(w_up, *x_a.sent))[None], n_dp, index)
    near_a = links_first(x_a.finish(*own_qkv), n_dp)
    core_a = [swap(v, "dp", n_dp, 1) for v in near_a]
    shards = [turned, w_out[None], None, w_down[None]]
    sizes = [
        (3, w_qkv.shape[2] // (2 * n_dp)),
        (1, w_out.shape[0] // (2 * n_dp)),
        (1, w_up.shape[1] // (2 * n_dp)),
        (1, w_down.shape[0] // (2 * n_dp)),
    ]
    units_of = lambda halves, some: far_units(halves, some, n_dp, n_tensor)
    qkv = [None, None]

    def project(core, halves):
        full = join(own_qkv[core], units_of(halves, sizes[:1])[0], False)
        qkv[core] = dot_low(full, low_one, 1, 1).reshape(3, heads, -1, capacity)
        return full

    full_qkv = [project(0, near_a)]
    core_a = [after(c, qkv[0]) for c in core_a]
    (far_b,) = z_b.finish(*own_up)
    x_b = Flow(links, link_gathers(far_b, n_dp))
    z_c = Flow(1, gather_tensor([after(piece_down, far_b)], n_tensor))
    full_qkv.append(project(1, core_a))
    mixed_first, mixed_second, log_sums = attend(*qkv, image, scale)
    mixed = [m.reshape(-1, capacity) for m in (mixed_first, mixed_second)]
    x_b.go(mixed[0])
    own_out = own_units(after(w_out, *x_b.sent)[None], n_dp, index)
    (far_c,) = z_c.finish(*own_out)
    x_c = Flow(links, link_gathers(far_c, n_dp))
    own_down = own_units(after(w_down, *x_c.sent)[None], n_dp, index)
    near_b = links_first(x_b.finish(*own_down), n_dp)
    core_b = [swap(v, "dp", n_dp, 1) for v in near_b]
    full_out, full_up, full_down = [], [], []

    def join_b(core, halves):
        far_out, far_up = units_of(halves, sizes[1:3])
        full_out.append(join(own_out[core], far_out, False))
        full_up.append(join(own_up[core], far_up, True))

    join_b(0, near_b)
    x_c.go(full_up[0])
    join_b(1, [after(c, full_up[0], *x_c.sent) for c in core_b])
    member = (image[:, None] == jnp.arange(images, dtype=jnp.int32)[None, :]).astype(WIDE)
    row_scale = jnp.sum(member * lax.rsqrt(counts[0].astype(WIDE))[None, :], axis=1)

    hidden = inputs + dot(mixed[0], full_out[0], 0, 0) + dot(mixed[1], full_out[1], 0, 0)
    normed_two, inverse_two = layer_norm(hidden)
    low_two = (normed_two * ln2_gain).astype(LOW)
    mate_mixed, mate_one = mate(after(mixed[1], low_two)), mate(after(low_one, low_two))
    active, slope = [], []

    def feed(core, normed):
        value, rate = gelu_both(dot(normed, full_up[core], 1, 1))
        active.append(value.astype(LOW))
        slope.append(rate.astype(LOW))

    feed(0, low_two)
    near_c = links_first(x_c.finish(active[0]), n_dp)
    core_c = [swap(v, "dp", n_dp, 1) for v in near_c]
    feed(1, after(low_two, mate_mixed, mate_one, active[0]))
    full_down.append(join(own_down[0], units_of(near_c, sizes[3:])[0], True))
    fed = dot(active[0], full_down[0], 1, 0)
    mate_active, mate_two = mate(active[1]), mate(low_two)
    core_c = [after(c, active[1], full_down[0]) for c in core_c]
    full_down.append(join(own_down[1], units_of(core_c, sizes[3:])[0], True))
    output = hidden + fed + dot(active[1], full_down[1], 1, 0)
    normed_three, inverse_three = layer_norm(output)
    low_three = (normed_three * ln3_gain).astype(LOW)
    low_three = after(low_three, mate_active, mate_two)
    acted, learn_slope = gelu_both(dot(low_three, w_learn1, 1, 0))
    acted, learn_slope = acted.astype(LOW), learn_slope.astype(LOW)
    select = jax.nn.sigmoid(dot(acted, w_learn2, 1, 0))
    weights = (select * row_scale[:, None]).astype(LOW)
    table = (member.astype(LOW)[:, :, None] * weights[:, None, :]).reshape(capacity, images * tokens)
    low_out = output.astype(LOW)
    learned = dot_low(table, low_out, 0, 0)

    grad_pooled = cotangent.reshape(images * tokens, width)
    grad_output = dot(table, grad_pooled, 1, 0)
    grad_table = dot(low_out, grad_pooled, 1, 1)
    grad_weights = jnp.sum(grad_table.reshape(capacity, images, tokens) * member[:, :, None], axis=1)
    grad_logits = (grad_weights * row_scale[:, None] * select * (1.0 - select)).astype(LOW)
    grad_learn2 = dot(grad_logits, acted, 0, 0)
    grad_inner = (dot(grad_logits, w_learn2, 1, 1) * learn_slope.astype(WIDE)).astype(LOW)
    side = width // 2
    three_keep = lax.dynamic_slice_in_dim(low_three, (index & 1) * side, side, 1)
    three_away = lax.dynamic_slice_in_dim(low_three, (1 - (index & 1)) * side, side, 1)
    mate_three, mate_inner = mate(three_away), mate(grad_inner)
    grad_from_three, grad_gain3 = norm_back(
        dot(grad_inner, w_learn1, 1, 1), ln3_gain, normed_three, inverse_three
    )
    grad_output = grad_output + grad_from_three

    grad_fed = grad_output.astype(LOW)
    mate_three, mate_inner = after(mate_three, grad_fed), after(mate_inner, grad_fed)
    mate_fed = mate(grad_fed)
    units = functools.partial(split_units, n_dp=n_dp, n_tensor=n_tensor)
    upward = lambda c, grad: (dot(grad, full_down[c], 1, 1) * slope[c].astype(WIDE)).astype(LOW)
    grad_upper = [None, upward(1, grad_fed)]
    mate_upper = mate(grad_upper[1])
    mate_fed = after(mate_fed, grad_upper[1])
    away, stay = first_split(n_dp, True), first_split(n_dp, False)
    down_operands = (active[0], grad_fed, mate_active, mate_fed)
    grad_learn1, *down_away = split_product(
        *down_operands, away, n_dp // 2, index, (three_keep, grad_inner, mate_three, mate_inner)
    )
    down_stay = split_product(*down_operands, stay, n_dp // 2, index, (grad_learn1,))
    bits_left = (2,) * (n_dp.bit_length() - 3)
    kept = lambda parts: [[p.reshape(bits_left + (-1, width))] for p in parts]
    x_down = Flow(links, link_sums_from(kept(down_stay), down_away, n_dp))
    grad_upper[0] = upward(0, after(grad_fed, *down_stay))
    mate_upper = after(mate_upper, grad_upper[0])
    grad_hidden, grad_attended, grad_gain2 = rows_back(
        grad_upper, full_up, grad_output, normed_two, inverse_two, ln2_gain
    )
    grad_gain2 = grad_gain2[0]

    grad_mixed = [g.reshape(heads, -1, capacity) for g in two_products(full_out, grad_attended)]
    up_operands = (grad_upper[0], low_two, mate_upper, mate_two)
    up_away = split_product(*up_operands, away, n_dp // 2)
    up_stay = split_product(*up_operands, stay, n_dp // 2)
    x_down.go(*up_away, *up_stay, *grad_mixed)
    grad_mixed = [after(g, *x_down.sent) for g in grad_mixed]
    mate_attended = mate(after(grad_attended, *up_stay))
    grad_qkv = attend_back(*qkv, (mixed_first, mixed_second), grad_mixed, log_sums, image, scale)
    grad_qkv = [g.reshape(-1, capacity) for g in grad_qkv]
    mate_qkv = mate(grad_qkv[1])
    pair_down = x_down.finish(grad_qkv[0])
    down_rows = active[0].shape[1] // n_dp
    everywhere = [pair_down[0][:, down_rows:], learned.reshape(2, -1, width)]
    z_down = Flow(spans, reduce_tensor([pair_down[0][:, :down_rows]], everywhere, n_tensor))
    x_up = Flow(links, link_sums_from(kept(up_stay), [after(u, *pair_down) for u in up_away], n_dp))
    grad_qkv = [after(g, *z_down.sent, *x_up.sent) for g in grad_qkv]
    grad_from_one, grad_gain1 = norm_back(
        dot(grad_qkv[0], full_qkv[0], 0, 0) + dot(grad_qkv[1], full_qkv[1], 0, 0),
        ln1_gain,
        normed_one,
        inverse_one,
    )
    near = (grad_hidden + grad_from_one).astype(LOW)
    some = capacity // 2
    ring_a = Flow(spans, gather_rows(near[:some], n_tensor))
    z_down.go(near)
    x_up.go(*z_down.sent)
    ring_a.go(*x_up.sent)
    ring_b = Flow(spans, gather_rows(after(near[some:], *ring_a.sent), n_tensor))
    mate_qkv, mate_attended = [after(m, *ring_a.sent, *ring_b.sent) for m in (mate_qkv, mate_attended)]
    grad_out = pair_product(mixed[0], grad_attended, mate_mixed, mate_attended, 1)
    grad_qkv_weight = pair_product(after(grad_qkv[0], *ring_a.sent, *ring_b.sent), low_one, mate_qkv, mate_one, 1)
    extra = jnp.concatenate([jnp.stack([grad_gain1, grad_gain2, grad_gain3]), grad_learn2])
    extra = jnp.pad(extra, ((0, 16 * n_dp - extra.shape[0]), (0, 0)))
    extra = (extra + mate(extra)).astype(LOW)

    pair_up = x_up.finish(grad_qkv_weight, grad_out)
    z_up = Flow(spans, reduce_tensor(pair_up, [], n_tensor))
    x_qkv = Flow(
        links,
        link_sums(
            [
                units(after(grad_qkv_weight, *pair_up), 3, part_first=False),
                units(after(grad_out, *pair_up), 1, part_first=False),
                split_shared(after(extra, *pair_up), n_dp, index),
            ],
            n_dp,
        ),
    )
    (sum_down,) = z_down.finish(*z_up.sent, *x_qkv.sent)
    learned = sum_down[:, -(images * tokens // 2) :].reshape(images, tokens, width)
    sum_down = sum_down[:, : -(images * tokens // 2)]
    x_qkv.go(sum_down)
    z_up.go(*x_qkv.sent)
    while ring_a.left > 1:
        ring_a.go(*z_up.sent)
        ring_b.go(*ring_a.sent)
    (rows_a,) = ring_a.finish(*z_up.sent)
    ring_b.go(rows_a)
    pair_qkv = x_qkv.finish(*ring_b.sent)
    z_qkv = Flow(spans, reduce_tensor(pair_qkv[:2], pair_qkv[2:], n_tensor))

    (sum_up,) = z_up.finish(*z_qkv.sent)
    x_seen = Flow(links, link_gathers(jnp.concatenate([sum_down, sum_up], axis=1), n_dp))

    source_of = lambda j: row_map(place, counts, tensor_index ^ j, capacity)[1]
    sources = [source] + [source_of(j) for j in range(1, n_tensor)]
    blocks = [(after(source, *x_seen.sent), near)]
    blocks += [(sources[j][:some], rows_a[j]) for j in range(1, n_tensor)]
    early = rows_home(blocks, rows)
    x_seen.go(early)
    (rows_b,) = ring_b.finish(*x_seen.sent)
    z_qkv.go(rows_b)
    near_seen = x_seen.finish(*z_qkv.sent)
    blocks = [(after(sources[j][some:], *z_qkv.sent), rows_b[j]) for j in range(1, n_tensor)]
    input_grad = rows_home(blocks, rows, early)
    (sum_qkv,) = z_qkv.finish(input_grad)
    x_last = Flow(links, link_gathers(sum_qkv, n_dp))
    seen_a = both_near(near_seen, n_dp)
    seen_a[1] = [after(v, *x_last.sent) for v in seen_a[1]]
    down_rows = up_rows = active[0].shape[1] // (n_tensor * n_dp)
    out_rows, qkv_rows, extra_rows = [
        grad.shape[0] // (parts * n_dp * lead)
        for grad, parts, lead in (
            (grad_out, n_tensor, 1),
            (grad_qkv_weight, n_tensor, 3),
            (extra, 1, 1),
        )
    ]
    down_sum = place_units(seen_a, 0, 1, down_rows, n_dp, index, False)[0]
    learn_rows = grad_learn1.shape[0] // n_dp
    learn_sum = place_shared(seen_a, down_rows, learn_rows, n_dp, index)
    at = down_rows + learn_rows
    up_sum = place_units(seen_a, at, 1, up_rows, n_dp, index, True)[0]
    while x_last.left > 1:
        x_last.go(down_sum, learn_sum, up_sum)
    seen_c = both_near(x_last.finish(down_sum, learn_sum, up_sum), n_dp)
    out_sum = place_units(seen_c, 3 * qkv_rows, 1, out_rows, n_dp, index, False)[0]
    qkv_sum = place_units(seen_c, 0, 3, qkv_rows, n_dp, index, True)
    small = seen_c[0][0][:, 3 * qkv_rows + out_rows :].reshape(n_dp // 2, extra_rows, width)
    small = lax.dynamic_slice_in_dim(small, index // 2, 1, 0)[0].astype(WIDE)

    return (
        learned,
        input_grad,
        small[0],
        jnp.transpose(qkv_sum, (1, 0, 2)),
        out_sum,
        small[1],
        up_sum,
        down_sum,
        small[2],
        learn_sum,
        jnp.transpose(small[3 : 3 + tokens]),
    )


def solution(mesh):
    return jax.shard_map(
        functools.partial(local, mesh.shape["dp"], mesh.shape["tensor"]),
        mesh=mesh,
        in_specs=(
            P("dp", None),
            P("dp", None),
            P("dp", None),
            P(),
            P(None, None, "tensor"),
            P("tensor", None),
            P(),
            P(None, "tensor"),
            P("tensor", None),
            P(),
            P(),
            P(),
            P("dp", None, None),
        ),
        out_specs=(
            P("dp", None, None),
            P("dp", None),
            P(),
            P(None, None, "tensor"),
            P("tensor", None),
            P(),
            P(None, "tensor"),
            P("tensor", None),
            P(),
            P(),
            P(),
        ),
        check_vma=False,
    )
```

time: 646 us -> 545 us (0.84)
  Pallas kernels: 39.5 us -> 127 us
  matrix products: 144 us -> 65.7 us
  starting transfers between devices: 102 us -> 63.2 us
  local copies, waits for them, and re-layouts: 91.4 us -> 56 us
  waiting for transfers between devices: 191 us -> 166 us
  other arithmetic: 63.8 us -> 55.5 us
    pallas_call x0 -> x15, Pallas kernels: none -> 87.3 us  [the longest x4 29.9 us: split_product(): pl.pallas_call(functools.partial(split_kernel, picks, tile, mode), out_sh...]
    dot_general x38 -> x22, matrix products: 144 us -> 65.7 us  [dot(): lax.dot_general(left, right, (((left_dim,), (right_dim,)), ((), ())), pre...]
    ppermute x6 -> x0, waiting for transfers between devices: 48.2 us -> none  [the longest x3 30.5 us: pass_on(): lax.ppermute(above, 'tensor', [(i + 1, i) for i in range(n_tensor - 1)])]
    ppermute x6 -> x0, starting transfers between devices: 37.3 us -> none  [the longest x3 33.1 us: pass_on(): lax.ppermute(below, 'tensor', [(i, i + 1) for i in range(n_tensor - 1)])]
    unnamed x270 -> x236, local copies, waits for them, and re-layouts: 55.4 us -> 25.6 us
    ppermute x65 -> x72, waiting for transfers between devices: 143 us -> 166 us  [swap(): return lax.ppermute(value, axis, [(i, i ^ mask) for i in range(size)])]
    ppermute x65 -> x72, starting transfers between devices: 64.8 us -> 63.2 us  [swap(): return lax.ppermute(value, axis, [(i, i ^ mask) for i in range(size)])]
    another operation x36 -> x33, other arithmetic: 21.7 us -> 20.8 us  [the longest x17 9.02 us: link_gathers(): value = [jnp.stack([v, c]) for v, c in zip(value, came)]]
  transfers between devices with their start and end apart: 71 -> 72, of which waited for: 23 -> 20; matrix products, arithmetic and copies ran while one was open for 35% -> 27% of each run, Pallas kernels for 6% -> 23%
where the time goes in v2:
time: 545 us; the launch traced here: 537 us
  waiting for transfers between devices  166 us (30%)
  Pallas kernels  127 us (23%)
  matrix products  65.7 us (12%)
  starting transfers between devices  63.2 us (12%)
  local copies, waits for them, and re-layouts  56 us (10%)
  other arithmetic  55.5 us (10%)
    ppermute x72, waiting for transfers between devices, swap(): return lax.ppermute(value, axis, [(i, i ^ mask) for i in range(size)])  166 us
    dot_general x22, matrix products, dot(): lax.dot_general(left, right, (((left_dim,), (right_dim,)), ((), ())), pre...  65.7 us
    ppermute x72, starting transfers between devices, swap(): return lax.ppermute(value, axis, [(i, i ^ mask) for i in range(size)])  63.2 us
    pallas_call x4, Pallas kernels, split_product(): pl.pallas_call(functools.partial(split_kernel, picks, tile, mode), out_sh...  29.9 us
    unnamed x236, local copies, waits for them, and re-layouts  25.6 us
    pallas_call x1, Pallas kernels, attend_back(): pl.pallas_call(functools.partial(attend_back_kernel, scale), grid=(heads,...  23.3 us
    pallas_call x2, Pallas kernels, rows_home(): pl.pallas_call(functools.partial(back_kernel, len(values)), grid=(rows //...  21.1 us
    pallas_call x1, Pallas kernels, attend(): pl.pallas_call(functools.partial(attend_kernel, scale), grid=(heads,), in...  14.8 us
  transfers between devices with their start and end apart: 72, of which 20 were waited for; matrix products, arithmetic and copies ran while one was open for 27% of the time, Pallas kernels for 23%

profile of v2, /device:TPU:0, one launch (start us, length us, event | category | flops | bytes accessed | tf_op | source)
XLA Modules:
  0.0 537.0 jit_solution(2390854200197943698)
XLA Ops:
  19.7 7.3 %collective-permute-done.1 = bf16[2,48,1024]{2,1,0:T(8,128)(2,1)S(1)} collective-permute-done((bf16[2,48,1024]{2,1,0:T(8,128)(2,1)}, bf16[2,48,1024]{2,1,0:T(8,128)(2,1)S(1)}, u32[]{:S(2)}, u32[]{:S(2)}) %collective-permute-start.1) | collective-permute-done | bytes 196640 | tf_op jit(solution)/shard_map/ppermute | solution.py:146
  46.3 6.4 %collective-permute-done.3 = bf16[3,48,1024]{2,1,0:T(8,128)(2,1)S(1)} collective-permute-done((bf16[3,48,1024]{2,1,0:T(8,128)(2,1)S(1)}, bf16[3,48,1024]{2,1,0:T(8,128)(2,1)S(1)}, u32[]{:S(2)}, u32[]{:S(2)}) %collective-permute-start.3) | collective-permute-done | bytes 294944 | tf_op jit(solution)/shard_map/ppermute | solution.py:146
  86.9 14.8 %attend.1 = (bf16[16,32,640]{2,1,0:T(8,128)(2,1)S(1)}, bf16[16,32,640]{2,1,0:T(8,128)(2,1)S(1)}, f32[16,1,640]{2,1,0:T(1,128)S(1)}) custom-call(bf16[3,16,32,640]{3,2,1,0:T(8,128)(2,1)S(1)} %bitcast.582, bf16[3,16,32,640]{3,2,1,0:T(8,128)(2,1)S(1)} %bitcast.584, s32[640,1]{1,0:T(8,128)S(1)} %copy-done.18, s32[1,640]{1,0:T(1,128)S(1)} %sub.88.row_ref), custom_call_target="tpu_custom_call" | custom-call | tf_op jit(solution)/shard_map/attend/pallas_call | solution.py:593
  113.4 15.0 %collective-permute-done.18 = bf16[2,3,80,1024]{3,2,0,1:T(8,128)(2,1)S(1)} collective-permute-done((bf16[2,3,80,1024]{3,2,0,1:T(8,128)(2,1)S(1)}, bf16[2,3,80,1024]{3,2,0,1:T(8,128)(2,1)S(1)}, u32[]{:S(2)}, u32[]{:S(2)}) %collective-permute-start.18) | collective-permute-done | bytes 983072 | tf_op jit(solution)/shard_map/ppermute | solution.py:146
  164.0 6.6 %fusion.112 = f32[640,1024]{1,0:T(8,128)} fusion(bf16[640,2048]{1,0:T(8,128)(2,1)S(1)} %get-tuple-element.384.refs_0_, bf16[2048,1024]{1,0:T(8,128)(2,1)} %bitcast.648), kind=kOutput, calls=%fused_computation.426 | convolution fusion | flops 2684354560 | bytes 9437184 | tf_op jit(solution)/shard_map/dot_general | solution.py:43
  196.1 5.6 %multiply_convert_fusion.1.second_ref = bf16[640,2048]{1,0:T(8,128)(2,1)} fusion(f32[640,2048]{1,0:T(8,128)S(1)} %bitcast.758, bf16[640,1024]{1,0:T(8,128)(2,1)S(1)} %get-tuple-element.172.refs_1_, bf16[2048,1024]{1,0:T(8,128)(2,1)S(1)} %bitcast.651), kind=kOutput, calls=%fused_computation.13 | convolution fusion | flops 2700083200 | bytes 13369344 | tf_op jit(solution)/shard_map/dot_general | solution.py:43
  207.7 10.2 %split_product.4 = (bf16[512,1024]{1,0:T(8,128)(2,1)S(1)}, bf16[640,1024]{1,0:T(8,128)(2,1)}, bf16[640,1024]{1,0:T(8,128)(2,1)}) custom-call(bf16[640,2048]{1,0:T(8,128)(2,1)} %copy-done.41, bf16[640,1024]{1,0:T(8,128)(2,1)} %copy-done.11, bf16[640,2048]{1,0:T(8,128)(2,1)} %copy-done.42, bf16[640,1024]{1,0:T(8,128)(2,1)} %collective-permute-done.31.refs_3_, ...), custom_call_target="tpu_custom_call" | custom-call | tf_op jit(solution)/shard_map/split_product/pallas_call | solution.py:460
  221.1 6.5 %split_product.5 = (bf16[640,1024]{1,0:T(8,128)(2,1)S(1)}, bf16[640,1024]{1,0:T(8,128)(2,1)S(1)}) custom-call(bf16[640,2048]{1,0:T(8,128)(2,1)} %copy-done.41, bf16[640,1024]{1,0:T(8,128)(2,1)S(1)} %copy-done.12, bf16[640,2048]{1,0:T(8,128)(2,1)} %copy-done.42, bf16[640,1024]{1,0:T(8,128)(2,1)} %collective-permute-done.31.refs_3_, ...), custom_call_target="tpu_custom_call" | custom-call | tf_op jit(solution)/shard_map/split_product/pallas_call | solution.py:460
  229.2 7.8 %multiply_convert_fusion.refs_0_.first_ref = bf16[640,2048]{1,0:T(8,128)(2,1)} fusion(bf16[640,1024]{1,0:T(8,128)(2,1)S(1)} %copy-done.12, bf16[2048,1024]{1,0:T(8,128)(2,1)S(1)} %bitcast.649, f32[640,2048]{1,0:T(8,128)} %get-tuple-element.385), kind=kOutput, calls=%fused_computation.12 | convolution fusion | flops 2700083200 | bytes 13369344 | tf_op jit(solution)/shard_map/dot_general | solution.py:43
  237.0 12.7 %rows_back.1 = (f32[640,1024]{1,0:T(8,128)S(1)}, bf16[640,1024]{1,0:T(8,128)(2,1)S(1)}, f32[1,1024]{1,0:T(1,128)S(1)}) custom-call(bf16[640,2048]{1,0:T(8,128)(2,1)} %multiply_convert_fusion.refs_0_.first_ref, bf16[640,2048]{1,0:T(8,128)(2,1)} %multiply_convert_fusion.1.second_ref, bf16[2048,1024]{1,0:T(8,128)(2,1)} %bitcast.600, ...), custom_call_target="tpu_custom_call" | custom-call | tf_op jit(solution)/shard_map/rows_back/pallas_call | solution.py:533
  251.6 7.1 %split_product.6 = (bf16[512,1024]{1,0:T(8,128)(2,1)}, bf16[512,1024]{1,0:T(8,128)(2,1)}) custom-call(bf16[640,2048]{1,0:T(8,128)(2,1)} %multiply_convert_fusion.refs_0_.first_ref, bf16[640,1024]{1,0:T(8,128)(2,1)S(1)} %get-tuple-element.161.refs_1_, bf16[640,2048]{1,0:T(8,128)(2,1)} %collective-permute-done.35.refs_2_, bf16[640,1024]{1,0:T(8,128)(2,1)S(1)} %copy-done.17), custom_call_target="tpu_custom_call" | custom-call | tf_op jit(solution)/shard_map/split_product/pallas_call | solution.py:460
  258.7 6.1 %split_product.7 = (bf16[512,1024]{1,0:T(8,128)(2,1)S(1)}, bf16[512,1024]{1,0:T(8,128)(2,1)S(1)}) custom-call(bf16[640,2048]{1,0:T(8,128)(2,1)} %multiply_convert_fusion.refs_0_.first_ref, bf16[640,1024]{1,0:T(8,128)(2,1)S(1)} %get-tuple-element.161.refs_1_, bf16[640,2048]{1,0:T(8,128)(2,1)} %collective-permute-done.35.refs_2_, bf16[640,1024]{1,0:T(8,128)(2,1)S(1)} %copy-done.17), custom_call_target="tpu_custom_call" | custom-call | tf_op jit(solution)/shard_map/split_product/pallas_call | solution.py:460
  271.8 23.3 %attend_back.1 = (bf16[3,16,32,640]{3,2,1,0:T(8,128)(2,1)S(1)}, bf16[3,16,32,640]{3,2,1,0:T(8,128)(2,1)}) custom-call(bf16[3,16,32,640]{3,2,1,0:T(8,128)(2,1)} %bitcast.583, bf16[3,16,32,640]{3,2,1,0:T(8,128)(2,1)} %bitcast.585, bf16[16,32,640]{2,1,0:T(8,128)(2,1)S(1)} %copy-done.8, bf16[16,32,640]{2,1,0:T(8,128)(2,1)S(1)} %copy-done.21, ...), custom_call_target="tpu_custom_call" | custom-call | tf_op jit(solution)/shard_map/attend_back/pallas_call | solution.py:653
  308.6 12.7 %collective-permute-done.39 = bf16[2,224,1024]{2,1,0:T(8,128)(2,1)S(1)} collective-permute-done((bf16[2,224,1024]{2,1,0:T(8,128)(2,1)S(1)}, bf16[2,224,1024]{2,1,0:T(8,128)(2,1)S(1)}, u32[]{:S(2)}, u32[]{:S(2)}) %collective-permute-start.39) | collective-permute-done | bytes 917536 | tf_op jit(solution)/shard_map/ppermute | solution.py:146
  329.6 22.4 %collective-permute-done.43 = bf16[1,320,1024]{2,1,0:T(8,128)(2,1)S(1)} collective-permute-done((bf16[1,320,1024]{2,1,0:T(8,128)(2,1)S(1)}, bf16[1,320,1024]{2,1,0:T(8,128)(2,1)S(1)}, u32[]{:S(2)}, u32[]{:S(2)}) %collective-permute-start.43) | collective-permute-done | bytes 655392 | tf_op jit(solution)/shard_map/ppermute | solution.py:146
  355.1 8.0 %pair_product.2 = bf16[1536,1024]{1,0:T(8,128)(2,1)} custom-call(bf16[1536,640]{1,0:T(8,128)(2,1)S(1)} %bitcast.590, bf16[640,1024]{1,0:T(8,128)(2,1)S(1)} %copy-done.15, bf16[1536,640]{1,0:T(8,128)(2,1)} %collective-permute-done.45.left_mate_ref, bf16[640,1024]{1,0:T(8,128)(2,1)S(1)} %copy-done.23), custom_call_target="tpu_custom_call" | custom-call | tf_op jit(solution)/shard_map/pair_product/pallas_call | solution.py:404
  375.0 23.0 %collective-permute-done.40 = bf16[2,160,1024]{2,1,0:T(8,128)(2,1)} collective-permute-done((bf16[2,160,1024]{2,1,0:T(8,128)(2,1)}, bf16[2,160,1024]{2,1,0:T(8,128)(2,1)}, u32[]{:S(2)}, u32[]{:S(2)}) %collective-permute-start.40) | collective-permute-done | bytes 655392 | tf_op jit(solution)/shard_map/ppermute | solution.py:146
  403.9 33.1 %collective-permute-done.53 = bf16[2,128,1024]{2,1,0:T(8,128)(2,1)S(1)} collective-permute-done((bf16[2,128,1024]{2,1,0:T(8,128)(2,1)S(1)}, bf16[2,128,1024]{2,1,0:T(8,128)(2,1)S(1)}, u32[]{:S(2)}, u32[]{:S(2)}) %collective-permute-start.53) | collective-permute-done | bytes 524320 | tf_op jit(solution)/shard_map/ppermute | solution.py:146
  444.5 5.5 %collective-permute-done.58 = bf16[2,64,1024]{2,1,0:T(8,128)(2,1)S(1)} collective-permute-done((bf16[2,64,1024]{2,1,0:T(8,128)(2,1)S(1)}, bf16[2,64,1024]{2,1,0:T(8,128)(2,1)S(1)}, u32[]{:S(2)}, u32[]{:S(2)}) %collective-permute-start.58) | collective-permute-done | bytes 262176 | tf_op jit(solution)/shard_map/ppermute | solution.py:146
  454.4 11.9 %rows_home.2.refs_3_ = bf16[2048,1024]{1,0:T(8,128)(2,1)} custom-call(s32[1,1600]{1,0:T(1,128)S(1)} %broadcast_in_dim.31.source_ref, bf16[640,1024]{1,0:T(8,128)(2,1)S(1)} %add_convert_fusion.refs_0_, bf16[320,1024]{1,0:T(8,128)(2,1)S(1)} %get-tuple-element.257.refs_1_, bf16[320,1024]{1,0:T(8,128)(2,1)S(1)} %get-tuple-element.256.refs_2_, ...), custom_call_target="tpu_custom_call" | custom-call | tf_op jit(solution)/shard_map/rows_home/pallas_call | solution.py:491
  470.2 7.0 %collective-permute-done.57 = bf16[2,320,1024]{2,1,0:T(8,128)(2,1)} collective-permute-done((bf16[2,320,1024]{2,1,0:T(8,128)(2,1)}, bf16[2,320,1024]{2,1,0:T(8,128)(2,1)}, u32[]{:S(2)}, u32[]{:S(2)}) %collective-permute-start.57) | collective-permute-done | bytes 1310752 | tf_op jit(solution)/shard_map/ppermute | solution.py:146
  479.1 8.4 %collective-permute-done.56 = bf16[2,144,1024]{2,1,0:T(8,128)(2,1)} collective-permute-done((bf16[2,144,1024]{2,1,0:T(8,128)(2,1)}, bf16[2,144,1024]{2,1,0:T(8,128)(2,1)}, u32[]{:S(2)}, u32[]{:S(2)}) %collective-permute-start.56) | collective-permute-done | bytes 589856 | tf_op jit(solution)/shard_map/ppermute | solution.py:146
  492.9 9.2 %rows_home.3 = bf16[2048,1024]{1,0:T(8,128)(2,1)} custom-call(s32[1,960]{1,0:T(1,128)S(1)} %bitcast.597, bf16[320,1024]{1,0:T(8,128)(2,1)S(1)} %get-tuple-element.254.refs_0_, bf16[320,1024]{1,0:T(8,128)(2,1)S(1)} %get-tuple-element.253.refs_1_, bf16[320,1024]{1,0:T(8,128)(2,1)S(1)} %get-tuple-element.252.refs_2_, bf16[2048,1024]{1,0:T(8,128)(2,1)S(1)} %copy-done.2), custom_call_target="tpu_custom_call" | custom-call | tf_op jit(solution)/shard_map/rows_home/pallas_call | solution.py:491
  522.5 6.0 %collective-permute-done.67 = bf16[2,80,1024]{2,1,0:T(8,128)(2,1)S(1)} collective-permute-done((bf16[2,80,1024]{2,1,0:T(8,128)(2,1)S(1)}, bf16[2,80,1024]{2,1,0:T(8,128)(2,1)S(1)}, u32[]{:S(2)}, u32[]{:S(2)}) %collective-permute-start.67) | collective-permute-done | bytes 327712 | tf_op jit(solution)/shard_map/ppermute | solution.py:146
  (618 shorter events, 256.6 us)
Async XLA Ops:
  28.6 37.2 %collective-permute-start.11 = (bf16[2,80,1024]{2,1,0:T(8,128)(2,1)}, bf16[2,80,1024]{2,1,0:T(8,128)(2,1)}, u32[]{:S(2)}, u32[]{:S(2)}) collective-permute-start(bf16[2,80,1024]{2,1,0:T(8,128)(2,1)} %constant_dynamic-update-slice_fusion), channel_id=1, source_target_pairs={{0,3},{1,2},{2,1},{3,0},{4,7},{5,6},{6,5},{7,4},{8,11},{9,10},{10,... | collective-permute-start | bytes 983048 | tf_op jit(solution)/shard_map/ppermute | solution.py:146
  31.0 34.8 %collective-permute-start.10 = (bf16[2,80,1024]{2,1,0:T(8,128)(2,1)}, bf16[2,80,1024]{2,1,0:T(8,128)(2,1)}, u32[]{:S(2)}, u32[]{:S(2)}) collective-permute-start(bf16[2,80,1024]{2,1,0:T(8,128)(2,1)} %constant_dynamic-update-slice_fusion), channel_id=1, source_target_pairs={{0,2},{1,3},{2,0},{3,1},{4,6},{5,7},{6,4},{7,5},{8,10},{9,11},{10,... | collective-permute-start | bytes 983048 | tf_op jit(solution)/shard_map/ppermute | solution.py:146
  31.0 34.8 %collective-permute-start.9 = (bf16[2,80,1024]{2,1,0:T(8,128)(2,1)}, bf16[2,80,1024]{2,1,0:T(8,128)(2,1)}, u32[]{:S(2)}, u32[]{:S(2)}) collective-permute-start(bf16[2,80,1024]{2,1,0:T(8,128)(2,1)} %constant_dynamic-update-slice_fusion), channel_id=1, source_target_pairs={{0,1},{1,0},{2,3},{3,2},{4,5},{5,4},{6,7},{7,6},{8,9},{9,8},{10,11... | collective-permute-start | bytes 983048 | tf_op jit(solution)/shard_map/ppermute | solution.py:146
  67.1 39.4 %collective-permute-start.17 = (bf16[2,64,1024]{2,1,0:T(8,128)(2,1)}, bf16[2,64,1024]{2,1,0:T(8,128)(2,1)}, u32[]{:S(2)}, u32[]{:S(2)}) collective-permute-start(bf16[2,64,1024]{2,1,0:T(8,128)(2,1)} %dynamic-slice_bitcast_fusion), channel_id=1, source_target_pairs={{0,3},{1,2},{2,1},{3,0},{4,7},{5,6},{6,5},{7,4},{8,11},{9,10},{10,... | collective-permute-start | bytes 786440 | tf_op jit(solution)/shard_map/ppermute | solution.py:146
  69.6 36.8 %collective-permute-start.16 = (bf16[2,64,1024]{2,1,0:T(8,128)(2,1)}, bf16[2,64,1024]{2,1,0:T(8,128)(2,1)}, u32[]{:S(2)}, u32[]{:S(2)}) collective-permute-start(bf16[2,64,1024]{2,1,0:T(8,128)(2,1)} %dynamic-slice_bitcast_fusion), channel_id=1, source_target_pairs={{0,2},{1,3},{2,0},{3,1},{4,6},{5,7},{6,4},{7,5},{8,10},{9,11},{10,... | collective-permute-start | bytes 786440 | tf_op jit(solution)/shard_map/ppermute | solution.py:146
  69.7 36.8 %collective-permute-start.15 = (bf16[2,64,1024]{2,1,0:T(8,128)(2,1)}, bf16[2,64,1024]{2,1,0:T(8,128)(2,1)}, u32[]{:S(2)}, u32[]{:S(2)}) collective-permute-start(bf16[2,64,1024]{2,1,0:T(8,128)(2,1)} %dynamic-slice_bitcast_fusion), channel_id=1, source_target_pairs={{0,1},{1,0},{2,3},{3,2},{4,5},{5,4},{6,7},{7,6},{8,9},{9,8},{10,11... | collective-permute-start | bytes 786440 | tf_op jit(solution)/shard_map/ppermute | solution.py:146
  152.9 31.0 %collective-permute-start.30 = (bf16[640,1024]{1,0:T(8,128)(2,1)S(1)}, bf16[640,1024]{1,0:T(8,128)(2,1)S(1)}, u32[]{:S(2)}, u32[]{:S(2)}) collective-permute-start(bf16[640,1024]{1,0:T(8,128)(2,1)S(1)} %get-tuple-element.161.refs_1_), channel_id=1, source_target_pairs={{0,4},{4,0},{8,12},{12,8},{16,20},{20,16},{24,28},{28,24},{1,5},{5... | collective-permute-start | bytes 3932168 | tf_op jit(solution)/shard_map/ppermute | solution.py:146
  201.8 49.8 %collective-permute-start.35 = (bf16[640,2048]{1,0:T(8,128)(2,1)}, bf16[640,2048]{1,0:T(8,128)(2,1)}, u32[]{:S(2)}, u32[]{:S(2)}) collective-permute-start(bf16[640,2048]{1,0:T(8,128)(2,1)} %multiply_convert_fusion.1.second_ref), channel_id=1, source_target_pairs={{0,4},{4,0},{8,12},{12,8},{16,20},{20,16},{24,28},{28,24},{1,5},{5... | collective-permute-start | bytes 7864328 | tf_op jit(solution)/shard_map/ppermute | solution.py:146
  218.9 45.8 %collective-permute-start.34 = (bf16[640,1024]{1,0:T(8,128)(2,1)}, bf16[640,1024]{1,0:T(8,128)(2,1)}, u32[]{:S(2)}, u32[]{:S(2)}) collective-permute-start(bf16[640,1024]{1,0:T(8,128)(2,1)} %get-tuple-element.170), channel_id=1, source_target_pairs={{0,16},{4,20},{8,24},{12,28},{16,0},{20,4},{24,8},{28,12},{1,17},{... | collective-permute-start | bytes 3932168 | tf_op jit(solution)/shard_map/ppermute | solution.py:146
  227.6 39.7 %collective-permute-start.37 = (bf16[640,1024]{1,0:T(8,128)(2,1)}, bf16[640,1024]{1,0:T(8,128)(2,1)}, u32[]{:S(2)}, u32[]{:S(2)}) collective-permute-start(bf16[640,1024]{1,0:T(8,128)(2,1)} %get-tuple-element.182), channel_id=1, source_target_pairs={{0,8},{4,12},{8,0},{12,4},{16,24},{20,28},{24,16},{28,20},{1,9},{5... | collective-permute-start | bytes 3932168 | tf_op jit(solution)/shard_map/ppermute | solution.py:146
  295.2 59.9 %collective-permute-start.45 = (bf16[1536,640]{1,0:T(8,128)(2,1)}, bf16[1536,640]{1,0:T(8,128)(2,1)}, u32[]{:S(2)}, u32[]{:S(2)}) collective-permute-start(bf16[1536,640]{1,0:T(8,128)(2,1)} %bitcast.689), channel_id=1, source_target_pairs={{0,4},{4,0},{8,12},{12,8},{16,20},{20,16},{24,28},{28,24},{1,5},{5... | collective-permute-start | bytes 5898248 | tf_op jit(solution)/shard_map/ppermute | solution.py:146
  295.3 58.0 %collective-permute-start.46 = (bf16[640,1024]{1,0:T(8,128)(2,1)S(1)}, bf16[640,1024]{1,0:T(8,128)(2,1)S(1)}, u32[]{:S(2)}, u32[]{:S(2)}) collective-permute-start(bf16[640,1024]{1,0:T(8,128)(2,1)S(1)} %get-tuple-element.203.right_ref), channel_id=1, source_target_pairs={{0,4},{4,0},{8,12},{12,8},{16,20},{20,16},{24,28},{28,24},{1,5},{5... | collective-permute-start | bytes 3932168 | tf_op jit(solution)/shard_map/ppermute | solution.py:146
  321.2 30.8 %collective-permute-start.43 = (bf16[1,320,1024]{2,1,0:T(8,128)(2,1)S(1)}, bf16[1,320,1024]{2,1,0:T(8,128)(2,1)S(1)}, u32[]{:S(2)}, u32[]{:S(2)}) collective-permute-start(bf16[1,320,1024]{2,1,0:T(8,128)(2,1)S(1)} %get-tuple-element.288), channel_id=1, source_target_pairs={{0,2},{1,3},{2,0},{3,1},{4,6},{5,7},{6,4},{7,5},{8,10},{9,11},{10,... | collective-permute-start | bytes 1966088 | tf_op jit(solution)/shard_map/ppermute | solution.py:146
  325.6 37.5 %collective-permute-start.47 = (bf16[256,1024]{1,0:T(8,128)(2,1)}, bf16[256,1024]{1,0:T(8,128)(2,1)}, u32[]{:S(2)}, u32[]{:S(2)}) collective-permute-start(bf16[256,1024]{1,0:T(8,128)(2,1)} %slice.655), channel_id=1, source_target_pairs={{0,16},{4,20},{8,24},{12,28},{16,0},{20,4},{24,8},{28,12},{1,17},{... | collective-permute-start | bytes 1572872 | tf_op jit(solution)/shard_map/ppermute | solution.py:146
  328.1 36.2 %collective-permute-start.42 = (bf16[256,1024]{1,0:T(8,128)(2,1)}, bf16[256,1024]{1,0:T(8,128)(2,1)}, u32[]{:S(2)}, u32[]{:S(2)}) collective-permute-start(bf16[256,1024]{1,0:T(8,128)(2,1)} %slice.653), channel_id=1, source_target_pairs={{0,8},{4,12},{8,0},{12,4},{16,24},{20,28},{24,16},{28,20},{1,9},{5... | collective-permute-start | bytes 1572872 | tf_op jit(solution)/shard_map/ppermute | solution.py:146
  352.0 46.0 %collective-permute-start.40 = (bf16[2,160,1024]{2,1,0:T(8,128)(2,1)}, bf16[2,160,1024]{2,1,0:T(8,128)(2,1)}, u32[]{:S(2)}, u32[]{:S(2)}) collective-permute-start(bf16[2,160,1024]{2,1,0:T(8,128)(2,1)} %pad_maximum_fusion.32), channel_id=1, source_target_pairs={{0,2},{1,3},{2,0},{3,1},{4,6},{5,7},{6,4},{7,5},{8,10},{9,11},{10,... | collective-permute-start | bytes 1966088 | tf_op jit(solution)/shard_map/ppermute | solution.py:146
  371.7 66.2 %collective-permute-start.51 = (bf16[1,320,1024]{2,1,0:T(8,128)(2,1)S(1)}, bf16[1,320,1024]{2,1,0:T(8,128)(2,1)S(1)}, u32[]{:S(2)}, u32[]{:S(2)}) collective-permute-start(bf16[1,320,1024]{2,1,0:T(8,128)(2,1)S(1)} %bitcast.676), channel_id=1, source_target_pairs={{0,2},{1,3},{2,0},{3,1},{4,6},{5,7},{6,4},{7,5},{8,10},{9,11},{10,... | collective-permute-start | bytes 1966088 | tf_op jit(solution)/shard_map/ppermute | solution.py:146
  374.6 62.7 %collective-permute-start.52 = (bf16[2,320,1024]{2,1,0:T(8,128)(2,1)S(1)}, bf16[2,320,1024]{2,1,0:T(8,128)(2,1)S(1)}, u32[]{:S(2)}, u32[]{:S(2)}) collective-permute-start(bf16[2,320,1024]{2,1,0:T(8,128)(2,1)S(1)} %copy-done.71), channel_id=1, source_target_pairs={{0,1},{1,0},{2,3},{3,2},{4,5},{5,4},{6,7},{7,6},{8,9},{9,8},{10,11... | collective-permute-start | bytes 3932168 | tf_op jit(solution)/shard_map/ppermute | solution.py:146
  398.0 39.0 %collective-permute-start.53 = (bf16[2,128,1024]{2,1,0:T(8,128)(2,1)S(1)}, bf16[2,128,1024]{2,1,0:T(8,128)(2,1)S(1)}, u32[]{:S(2)}, u32[]{:S(2)}) collective-permute-start(bf16[2,128,1024]{2,1,0:T(8,128)(2,1)S(1)} %bitcast.733), channel_id=1, source_target_pairs={{0,1},{1,0},{2,3},{3,2},{4,5},{5,4},{6,7},{7,6},{8,9},{9,8},{10,11... | collective-permute-start | bytes 1572872 | tf_op jit(solution)/shard_map/ppermute | solution.py:146
  400.4 41.3 %collective-permute-start.55 = (bf16[272,1024]{1,0:T(8,128)(2,1)S(1)}, bf16[272,1024]{1,0:T(8,128)(2,1)S(1)}, u32[]{:S(2)}, u32[]{:S(2)}) collective-permute-start(bf16[272,1024]{1,0:T(8,128)(2,1)S(1)} %pad_maximum_fusion.39), channel_id=1, source_target_pairs={{0,16},{4,20},{8,24},{12,28},{16,0},{20,4},{24,8},{28,12},{1,17},{... | collective-permute-start | bytes 1671176 | tf_op jit(solution)/shard_map/ppermute | solution.py:146
  402.3 39.5 %collective-permute-start.50 = (bf16[272,1024]{1,0:T(8,128)(2,1)S(1)}, bf16[272,1024]{1,0:T(8,128)(2,1)S(1)}, u32[]{:S(2)}, u32[]{:S(2)}) collective-permute-start(bf16[272,1024]{1,0:T(8,128)(2,1)S(1)} %pad_maximum_fusion.38), channel_id=1, source_target_pairs={{0,8},{4,12},{8,0},{12,4},{16,24},{20,28},{24,16},{28,20},{1,9},{5... | collective-permute-start | bytes 1671176 | tf_op jit(solution)/shard_map/ppermute | solution.py:146
  439.5 37.7 %collective-permute-start.57 = (bf16[2,320,1024]{2,1,0:T(8,128)(2,1)}, bf16[2,320,1024]{2,1,0:T(8,128)(2,1)}, u32[]{:S(2)}, u32[]{:S(2)}) collective-permute-start(bf16[2,320,1024]{2,1,0:T(8,128)(2,1)} %get-tuple-element.284), channel_id=1, source_target_pairs={{0,1},{1,0},{2,3},{3,2},{4,5},{5,4},{6,7},{7,6},{8,9},{9,8},{10,11... | collective-permute-start | bytes 3932168 | tf_op jit(solution)/shard_map/ppermute | solution.py:146
  454.2 33.4 %collective-permute-start.56 = (bf16[2,144,1024]{2,1,0:T(8,128)(2,1)}, bf16[2,144,1024]{2,1,0:T(8,128)(2,1)}, u32[]{:S(2)}, u32[]{:S(2)}) collective-permute-start(bf16[2,144,1024]{2,1,0:T(8,128)(2,1)} %maximum_maximum_fusion), channel_id=1, source_target_pairs={{0,1},{1,0},{2,3},{3,2},{4,5},{5,4},{6,7},{7,6},{8,9},{9,8},{10,11... | collective-permute-start | bytes 1769480 | tf_op jit(solution)/shard_map/ppermute | solution.py:146
  469.5 36.4 %collective-permute-start.64 = (bf16[2,192,1024]{2,1,0:T(8,128)(2,1)S(1)}, bf16[2,192,1024]{2,1,0:T(8,128)(2,1)S(1)}, u32[]{:S(2)}, u32[]{:S(2)}) collective-permute-start(bf16[2,192,1024]{2,1,0:T(8,128)(2,1)S(1)} %get-tuple-element.307), channel_id=1, source_target_pairs={{0,8},{4,12},{8,0},{12,4},{16,24},{20,28},{24,16},{28,20},{1,9},{5... | collective-permute-start | bytes 2359304 | tf_op jit(solution)/shard_map/ppermute | solution.py:146
  (150 other events, 1598.8 us)

commit v3 on v2

--- a/solution.py
+++ b/solution.py
@@ -288,6 +288,11 @@
     ]
 
 
+def plane_spread(total, n_dp):
+    came = yield [swap(total, "dp", n_dp, 2 * link) for link in range(1, n_dp // 2)], [total]
+    yield [total] + came, []
+
+
 def reduce_tensor(scattered, shared, n_tensor):
     width = (scattered + shared)[0].shape[-1]
     held = [s.reshape(2, n_tensor, -1, width) for s in scattered]
@@ -314,6 +319,12 @@
     return [near, [swap(n, "dp", n_dp, 1) for n in near]]
 
 
+def by_link(parts):
+    links = parts[0].shape[0]
+    bits = links.bit_length() - 1
+    return [jnp.stack([parts[0][link], parts[1][backwards(link, bits)]]) for link in range(links)]
+
+
 def backwards(number, bits):
     result = 0
     for _ in range(bits):
@@ -321,65 +332,74 @@
     return result
 
 
-def shared_kernel(index_ref, near_a, near_b, far_a, far_b, out_ref):
-    links, rows, _ = near_a.shape
+def place_rows_kernel(plan, links, by_part, index_ref, *refs):
+    count = 4 if by_part else 2 * links
+    bits = links.bit_length() - 1
+    outs = refs[count : count + len(plan)]
+
+    def piece(core, half, link, start, rows):
+        if by_part:
+            return refs[2 * core + half][backwards(link, bits) if half else link, start : start + rows]
+        return refs[core * links + link][half, start : start + rows]
+
+    held = refs[-1]
     index = index_ref[0]
-    for core, refs in enumerate(((near_a, near_b), (far_a, far_b))):
-        for half, ref in enumerate(refs):
-            for link in range(links):
-                spot = (((core ^ index) & 1) * 2 + half) * links + (link ^ (index >> 1))
-                at = backwards(link, links.bit_length() - 1) if half else link
-                out_ref[pl.ds(pl.multiple_of(spot * rows, rows), rows), :] = ref[at].astype(WIDE)
-
-
-def place_shared(seen, at, rows, n_dp, index):
-    (near_a, near_b), (far_a, far_b) = seen
+    for (at, lead, rows, kind), out in zip(plan, outs):
+        for i in range(lead):
+            target = held if kind == "turned" else out.at[i]
+            for core in range(2):
+                for half in range(2):
+                    for link in range(links):
+                        if kind == "shared":
+                            spot = (((core ^ index) & 1) * 2 + half) * links + (link ^ (index >> 1))
+                        else:
+                            spot = ((2 * link + core) ^ index) * 2 + half
+                        start = at + i * rows
+                        found = piece(core, half, link, start, rows).astype(WIDE)
+                        target[pl.ds(pl.multiple_of(spot * rows, rows), rows), :] = found
+            if kind == "turned":
+                out[i] = held[: 4 * rows * links].T
+
+
+def place_parts(seen, plan, n_dp, index):
+    if any(rows % 8 for _, _, rows, _ in plan):
+        return place_rows(by_link(seen[0]), by_link(seen[1]), plan, n_dp, index)
+    return place_rows(*seen, plan, n_dp, index, True)
+
+
+def place_rows(near, far, plan, n_dp, index, by_part=False):
+    links = n_dp // 2
+    width = near[0].shape[-1]
+    shapes = [
+        (lead, width, 4 * rows * links) if kind == "turned" else (lead, 4 * rows * links, width)
+        for _, lead, rows, kind in plan
+    ]
+    if any(rows % 8 for _, _, rows, _ in plan):
+        result = []
+        both = jnp.stack([jnp.stack(near), jnp.stack(far)], axis=1)
+        for (at, lead, rows, kind), shape in zip(plan, shapes):
+            piece = both[:, :, :, at : at + lead * rows].reshape(links, 2, 2, lead, rows, width)
+            if kind == "shared":
+                piece = reorder(jnp.transpose(piece, (3, 1, 2, 0, 4, 5)), 1, 2, index & 1)
+                piece = reorder(piece, 3, links, index // 2).reshape(lead, -1, width)
+            else:
+                piece = jnp.transpose(piece, (3, 0, 1, 2, 4, 5)).reshape(lead, n_dp, 2 * rows, width)
+                piece = reorder(piece, 1, n_dp, index).reshape(lead, -1, width)
+            piece = piece.astype(WIDE)
+            result.append(jnp.swapaxes(piece, 1, 2) if kind == "turned" else piece)
+        return result
+    most = max([4 * rows * links for _, _, rows, kind in plan if kind == "turned"] or [8])
     return pl.pallas_call(
-        shared_kernel,
-        out_shape=jax.ShapeDtypeStruct((2 * n_dp * rows, near_a.shape[-1]), WIDE),
-        in_specs=[pl.BlockSpec(memory_space=pltpu.SMEM)] + [pl.BlockSpec(memory_space=pltpu.VMEM)] * 4,
-        out_specs=pl.BlockSpec(memory_space=pltpu.VMEM),
-        compiler_params=pltpu.CompilerParams(vmem_limit_bytes=32 << 20),
-        name="place_shared",
-    )(index[None], *[v[:, at : at + rows] for v in (near_a, near_b, far_a, far_b)])
-
-
-def turn_kernel(turned, index_ref, near_a, near_b, far_a, far_b, out_ref, held):
-    links, lead, rows, _ = near_a.shape
-    index = index_ref[0]
-    for i in range(lead):
-        for core, refs in enumerate(((near_a, near_b), (far_a, far_b))):
-            for half, ref in enumerate(refs):
-                for link in range(links):
-                    spot = ((2 * link + core) ^ index) * (2 * rows) + half * rows
-                    at = backwards(link, links.bit_length() - 1) if half else link
-                    held[pl.ds(pl.multiple_of(spot, rows), rows), :] = ref[at, i].astype(WIDE)
-        out_ref[i] = held[...].T if turned else held[...]
-
-
-def place_units(seen, at, lead, rows, n_dp, index, turned):
-    (near_a, near_b), (far_a, far_b) = seen
-    width = near_a.shape[-1]
-    links = n_dp // 2
-    shaped = [v[:, at : at + lead * rows].reshape(links, lead, rows, width) for v in (near_a, near_b, far_a, far_b)]
-    units = 4 * rows * links
-    if rows % 8:
-        flips = [backwards(link, links.bit_length() - 1) for link in range(links)]
-        crossed = lambda v: jnp.stack([v[at] for at in flips])
-        parts = [shaped[0], crossed(shaped[1]), shaped[2], crossed(shaped[3])]
-        pieces = jnp.transpose(jnp.stack(parts, axis=1), (2, 0, 1, 3, 4))
-        pieces = reorder(pieces.reshape(lead, n_dp, 2 * rows, width), 1, n_dp, index)
-        pieces = pieces.reshape(lead, units, width).astype(WIDE)
-        return jnp.swapaxes(pieces, 1, 2) if turned else pieces
-    return pl.pallas_call(
-        functools.partial(turn_kernel, turned),
-        out_shape=jax.ShapeDtypeStruct((lead, width, units) if turned else (lead, units, width), WIDE),
-        in_specs=[pl.BlockSpec(memory_space=pltpu.SMEM)] + [pl.BlockSpec(memory_space=pltpu.VMEM)] * 4,
-        out_specs=pl.BlockSpec(memory_space=pltpu.VMEM),
-        scratch_shapes=[pltpu.VMEM((units, width), WIDE)],
-        compiler_params=pltpu.CompilerParams(vmem_limit_bytes=32 << 20),
-        name="place_units",
-    )(index[None], *shaped)
+        functools.partial(place_rows_kernel, plan, links, by_part),
+        out_shape=[jax.ShapeDtypeStruct(shape, WIDE) for shape in shapes],
+        in_specs=[pl.BlockSpec(memory_space=pltpu.SMEM)]
+        + [pl.BlockSpec(memory_space=pltpu.VMEM)] * (len(near) + len(far)),
+        out_specs=[pl.BlockSpec(memory_space=pltpu.VMEM)] * len(plan),
+        scratch_shapes=[pltpu.VMEM((most, width), WIDE)],
+        compiler_params=pltpu.CompilerParams(vmem_limit_bytes=48 << 20),
+        cost_estimate=pl.CostEstimate(flops=0, bytes_accessed=0, transcendentals=0),
+        name="place_rows",
+    )(index[None], *near, *far)
 
 
 SMALL_COST = pl.CostEstimate(flops=0, bytes_accessed=0, transcendentals=0)
@@ -622,9 +642,9 @@
     log_ref,
     column_ref,
     row_ref,
-    out_first_ref,
-    out_second_ref,
+    *out_refs,
 ):
+    out_first_ref, out_second_ref = out_refs[-2:]
     query, key, value = [jnp.concatenate([first_ref[i, 0], second_ref[i, 0]]) for i in range(3)]
     query = query * scale
     mixed = jnp.concatenate([mixed_first_ref[0], mixed_second_ref[0]])
@@ -646,13 +666,14 @@
         out_second_ref[i, 0] = item[half:]
 
 
-def attend_back(first, second, mixed, grad_mixed, log_sums, image, scale):
+def attend_back(first, second, mixed, grad_mixed, log_sums, image, scale, part, so_far=()):
     _, heads, half, rows = first.shape
-    three = pl.BlockSpec((3, 1, half, rows), lambda h: (0, h, 0, 0))
-    one = pl.BlockSpec((1, half, rows), lambda h: (h, 0, 0))
+    base = part * (heads // 2)
+    three = pl.BlockSpec((3, 1, half, rows), lambda h: (0, base + h, 0, 0))
+    one = pl.BlockSpec((1, half, rows), lambda h: (base + h, 0, 0))
     return pl.pallas_call(
         functools.partial(attend_back_kernel, scale),
-        grid=(heads,),
+        grid=(heads // 2,),
         in_specs=[
             three,
             three,
@@ -660,16 +681,18 @@
             one,
             one,
             one,
-            pl.BlockSpec((1, 1, rows), lambda h: (h, 0, 0)),
+            pl.BlockSpec((1, 1, rows), lambda h: (base + h, 0, 0)),
             pl.BlockSpec((rows, 1), lambda h: (0, 0)),
             pl.BlockSpec((1, rows), lambda h: (0, 0)),
-        ],
+        ]
+        + [pl.BlockSpec(memory_space=pl.ANY)] * len(so_far),
         out_specs=[three, three],
         out_shape=[jax.ShapeDtypeStruct((3, heads, half, rows), LOW)] * 2,
+        input_output_aliases={9 + i: i for i in range(len(so_far))},
         compiler_params=pltpu.CompilerParams(vmem_limit_bytes=48 << 20),
         cost_estimate=SMALL_COST,
         name="attend_back",
-    )(first, second, *mixed, *grad_mixed, log_sums, image[:, None], image[None, :])
+    )(first, second, *mixed, *grad_mixed, log_sums, image[:, None], image[None, :], *so_far)
 
 
 def local(
@@ -713,13 +736,14 @@
     x_a = Flow(links, link_gathers(far_a, n_dp))
     z_b = Flow(1, gather_tensor([after(p, far_a) for p in pieces], n_tensor))
     pick = (after(source, far_a)[:, None] == jnp.arange(rows, dtype=jnp.int32)[None, :]).astype(LOW)
-    inputs = dot(pick, patches, 1, 0) + dot(pick, pos_embed, 1, 0)
+    inputs = dot(pick, patches, 1, 0)
+    x_a.go(inputs)
+    inputs = inputs + dot(pick, after(pos_embed, *x_a.sent), 1, 0)
     normed_one, inverse_one = layer_norm(inputs)
     low_one = (normed_one * ln1_gain).astype(LOW)
-    x_a.go(low_one)
     own_qkv = own_units(after(turned, *x_a.sent), n_dp, index)
     own_up = own_units(jnp.transpose(after(w_up, *x_a.sent))[None], n_dp, index)
-    near_a = links_first(x_a.finish(*own_qkv), n_dp)
+    near_a = links_first(x_a.finish(low_one), n_dp)
     core_a = [swap(v, "dp", n_dp, 1) for v in near_a]
     shards = [turned, w_out[None], None, w_down[None]]
     sizes = [
@@ -816,8 +840,9 @@
     mate_three, mate_inner = after(mate_three, grad_fed), after(mate_inner, grad_fed)
     mate_fed = mate(grad_fed)
     units = functools.partial(split_units, n_dp=n_dp, n_tensor=n_tensor)
+    ready = after(grad_fed, mate_three, mate_inner)
     upward = lambda c, grad: (dot(grad, full_down[c], 1, 1) * slope[c].astype(WIDE)).astype(LOW)
-    grad_upper = [None, upward(1, grad_fed)]
+    grad_upper = [None, upward(1, ready)]
     mate_upper = mate(grad_upper[1])
     mate_fed = after(mate_fed, grad_upper[1])
     away, stay = first_split(n_dp, True), first_split(n_dp, False)
@@ -837,21 +862,26 @@
     grad_gain2 = grad_gain2[0]
 
     grad_mixed = [g.reshape(heads, -1, capacity) for g in two_products(full_out, grad_attended)]
-    up_operands = (grad_upper[0], low_two, mate_upper, mate_two)
+    x_down.go(*grad_mixed)
+    up_operands = (after(grad_upper[0], *x_down.sent), low_two, mate_upper, mate_two)
     up_away = split_product(*up_operands, away, n_dp // 2)
     up_stay = split_product(*up_operands, stay, n_dp // 2)
-    x_down.go(*up_away, *up_stay, *grad_mixed)
-    grad_mixed = [after(g, *x_down.sent) for g in grad_mixed]
-    mate_attended = mate(after(grad_attended, *up_stay))
-    grad_qkv = attend_back(*qkv, (mixed_first, mixed_second), grad_mixed, log_sums, image, scale)
-    grad_qkv = [g.reshape(-1, capacity) for g in grad_qkv]
-    mate_qkv = mate(grad_qkv[1])
-    pair_down = x_down.finish(grad_qkv[0])
+    pair_down = x_down.finish(*up_stay)
     down_rows = active[0].shape[1] // n_dp
     everywhere = [pair_down[0][:, down_rows:], learned.reshape(2, -1, width)]
     z_down = Flow(spans, reduce_tensor([pair_down[0][:, :down_rows]], everywhere, n_tensor))
     x_up = Flow(links, link_sums_from(kept(up_stay), [after(u, *pair_down) for u in up_away], n_dp))
-    grad_qkv = [after(g, *z_down.sent, *x_up.sent) for g in grad_qkv]
+    grad_mixed = [after(g, *z_down.sent, *x_up.sent) for g in grad_mixed]
+    mate_attended = mate(after(grad_attended, *x_up.sent))
+    attended_back = functools.partial(
+        attend_back, *qkv, (mixed_first, mixed_second), log_sums=log_sums, image=image, scale=scale
+    )
+    half_qkv = attended_back(grad_mixed, part=0)
+    z_down.go(half_qkv[0])
+    grad_mixed = [after(g, *z_down.sent) for g in grad_mixed]
+    grad_qkv = attended_back(grad_mixed, part=1, so_far=half_qkv)
+    grad_qkv = [g.reshape(-1, capacity) for g in grad_qkv]
+    mate_qkv = mate(grad_qkv[1])
     grad_from_one, grad_gain1 = norm_back(
         dot(grad_qkv[0], full_qkv[0], 0, 0) + dot(grad_qkv[1], full_qkv[1], 0, 0),
         ln1_gain,
@@ -861,18 +891,16 @@
     near = (grad_hidden + grad_from_one).astype(LOW)
     some = capacity // 2
     ring_a = Flow(spans, gather_rows(near[:some], n_tensor))
-    z_down.go(near)
-    x_up.go(*z_down.sent)
-    ring_a.go(*x_up.sent)
-    ring_b = Flow(spans, gather_rows(after(near[some:], *ring_a.sent), n_tensor))
-    mate_qkv, mate_attended = [after(m, *ring_a.sent, *ring_b.sent) for m in (mate_qkv, mate_attended)]
+    x_up.go(near)
+    mate_qkv, mate_attended = [after(m, *x_up.sent) for m in (mate_qkv, mate_attended)]
     grad_out = pair_product(mixed[0], grad_attended, mate_mixed, mate_attended, 1)
-    grad_qkv_weight = pair_product(after(grad_qkv[0], *ring_a.sent, *ring_b.sent), low_one, mate_qkv, mate_one, 1)
+    grad_qkv_weight = pair_product(after(grad_qkv[0], *x_up.sent), low_one, mate_qkv, mate_one, 1)
     extra = jnp.concatenate([jnp.stack([grad_gain1, grad_gain2, grad_gain3]), grad_learn2])
     extra = jnp.pad(extra, ((0, 16 * n_dp - extra.shape[0]), (0, 0)))
     extra = (extra + mate(extra)).astype(LOW)
 
-    pair_up = x_up.finish(grad_qkv_weight, grad_out)
+    (sum_down,) = z_down.finish(grad_qkv_weight, grad_out)
+    pair_up = x_up.finish(sum_down)
     z_up = Flow(spans, reduce_tensor(pair_up, [], n_tensor))
     x_qkv = Flow(
         links,
@@ -885,36 +913,34 @@
             n_dp,
         ),
     )
-    (sum_down,) = z_down.finish(*z_up.sent, *x_qkv.sent)
     learned = sum_down[:, -(images * tokens // 2) :].reshape(images, tokens, width)
     sum_down = sum_down[:, : -(images * tokens // 2)]
-    x_qkv.go(sum_down)
-    z_up.go(*x_qkv.sent)
+    ring_a.go(*x_qkv.sent, *z_up.sent)
+    ring_b = Flow(spans, gather_rows(after(near[some:], *ring_a.sent), n_tensor))
+    z_up.go(*ring_b.sent)
+    x_qkv.go(*z_up.sent)
+    (sum_up,) = z_up.finish(*x_qkv.sent)
+    pair_qkv = x_qkv.finish(sum_up)
+    z_qkv = Flow(spans, reduce_tensor(pair_qkv[:2], pair_qkv[2:], n_tensor))
+    sum_seen = jnp.concatenate([after(sum_down, *pair_qkv), sum_up], axis=1)
+    x_seen = Flow(links, link_gathers(sum_seen, n_dp))
     while ring_a.left > 1:
-        ring_a.go(*z_up.sent)
+        ring_a.go(*x_seen.sent)
         ring_b.go(*ring_a.sent)
-    (rows_a,) = ring_a.finish(*z_up.sent)
+    (rows_a,) = ring_a.finish(*z_qkv.sent, *x_seen.sent)
     ring_b.go(rows_a)
-    pair_qkv = x_qkv.finish(*ring_b.sent)
-    z_qkv = Flow(spans, reduce_tensor(pair_qkv[:2], pair_qkv[2:], n_tensor))
-
-    (sum_up,) = z_up.finish(*z_qkv.sent)
-    x_seen = Flow(links, link_gathers(jnp.concatenate([sum_down, sum_up], axis=1), n_dp))
-
-    source_of = lambda j: row_map(place, counts, tensor_index ^ j, capacity)[1]
-    sources = [source] + [source_of(j) for j in range(1, n_tensor)]
-    blocks = [(after(source, *x_seen.sent), near)]
+    while x_seen.left > 1:
+        x_seen.go(*ring_b.sent)
+    z_qkv.go(*x_seen.sent)
+
+    sources = [source] + [row_map(place, counts, tensor_index ^ j, capacity)[1] for j in range(1, n_tensor)]
+    blocks = [(after(source, *z_qkv.sent), near)]
     blocks += [(sources[j][:some], rows_a[j]) for j in range(1, n_tensor)]
     early = rows_home(blocks, rows)
-    x_seen.go(early)
-    (rows_b,) = ring_b.finish(*x_seen.sent)
-    z_qkv.go(rows_b)
-    near_seen = x_seen.finish(*z_qkv.sent)
-    blocks = [(after(sources[j][some:], *z_qkv.sent), rows_b[j]) for j in range(1, n_tensor)]
-    input_grad = rows_home(blocks, rows, early)
-    (sum_qkv,) = z_qkv.finish(input_grad)
-    x_last = Flow(links, link_gathers(sum_qkv, n_dp))
+    near_seen = x_seen.finish(early)
     seen_a = both_near(near_seen, n_dp)
+    (sum_qkv,) = z_qkv.finish(*near_seen)
+    x_last = Flow(1, plane_spread(sum_qkv, n_dp))
     seen_a[1] = [after(v, *x_last.sent) for v in seen_a[1]]
     down_rows = up_rows = active[0].shape[1] // (n_tensor * n_dp)
     out_rows, qkv_rows, extra_rows = [
@@ -925,17 +951,24 @@
             (extra, 1, 1),
         )
     ]
-    down_sum = place_units(seen_a, 0, 1, down_rows, n_dp, index, False)[0]
     learn_rows = grad_learn1.shape[0] // n_dp
-    learn_sum = place_shared(seen_a, down_rows, learn_rows, n_dp, index)
     at = down_rows + learn_rows
-    up_sum = place_units(seen_a, at, 1, up_rows, n_dp, index, True)[0]
-    while x_last.left > 1:
-        x_last.go(down_sum, learn_sum, up_sum)
-    seen_c = both_near(x_last.finish(down_sum, learn_sum, up_sum), n_dp)
-    out_sum = place_units(seen_c, 3 * qkv_rows, 1, out_rows, n_dp, index, False)[0]
-    qkv_sum = place_units(seen_c, 0, 3, qkv_rows, n_dp, index, True)
-    small = seen_c[0][0][:, 3 * qkv_rows + out_rows :].reshape(n_dp // 2, extra_rows, width)
+    down_sum, learn_sum, up_sum = place_parts(
+        seen_a,
+        ((0, 1, down_rows, "plain"), (down_rows, 1, learn_rows, "shared"), (at, 1, up_rows, "turned")),
+        n_dp,
+        index,
+    )
+    near_c = x_last.finish(down_sum)
+    far_c = mate(jnp.stack(near_c))
+    (rows_b,) = ring_b.finish(*near_c)
+    input_grad = rows_home([(sources[j][some:], rows_b[j]) for j in range(1, n_tensor)], rows, early)
+    far_c = after(far_c, input_grad)
+    far_c = [far_c[link] for link in range(n_dp // 2)]
+    qkv_sum, out_sum = place_rows(
+        near_c, far_c, ((0, 3, qkv_rows, "turned"), (3 * qkv_rows, 1, out_rows, "plain")), n_dp, index
+    )
+    small = jnp.stack([v[0, 3 * qkv_rows + out_rows :] for v in near_c])
     small = lax.dynamic_slice_in_dim(small, index // 2, 1, 0)[0].astype(WIDE)
 
     return (
@@ -943,12 +976,12 @@
         input_grad,
         small[0],
         jnp.transpose(qkv_sum, (1, 0, 2)),
-        out_sum,
+        out_sum[0],
         small[1],
-        up_sum,
-        down_sum,
+        up_sum[0],
+        down_sum[0],
         small[2],
-        learn_sum,
+        learn_sum[0],
         jnp.transpose(small[3 : 3 + tokens]),
     )
 

time: 545 us -> 516 us (0.947)
  waiting for transfers between devices: 166 us -> 129 us
  other arithmetic: 55.5 us -> 62.1 us
    ppermute x72 -> x70, waiting for transfers between devices: 166 us -> 129 us  [swap(): return lax.ppermute(value, axis, [(i, i ^ mask) for i in range(size)])]
    another operation x17 -> x13, other arithmetic: 9.02 us -> 12.2 us  [link_gathers(): value = [jnp.stack([v, c]) for v, c in zip(value, came)]]
    ppermute x72 -> x70, starting transfers between devices: 63.2 us -> 64 us  [swap(): return lax.ppermute(value, axis, [(i, i ^ mask) for i in range(size)])]
    pallas_call x6 -> x4, Pallas kernels: 35.4 us -> 35.8 us  [the longest x2 25.1 us: attend_back(): pl.pallas_call(functools.partial(attend_back_kernel, scale), grid=(heads...]
    unnamed x236 -> x242, local copies, waits for them, and re-layouts: 25.6 us -> 25.3 us
  transfers between devices with their start and end apart: 72 -> 70, of which waited for: 20 -> 22; matrix products, arithmetic and copies ran while one was open for 27% -> 31% of each run, Pallas kernels for 23% -> 24%
where the time goes in v3:
time: 516 us; the launch traced here: 509 us
  waiting for transfers between devices  129 us (25%)
  Pallas kernels  125 us (24%)
  matrix products  70 us (14%)
  starting transfers between devices  64 us (12%)
  other arithmetic  62.1 us (12%)
  local copies, waits for them, and re-layouts  54.5 us (11%)
    ppermute x70, waiting for transfers between devices, swap(): return lax.ppermute(value, axis, [(i, i ^ mask) for i in range(size)])  129 us
    dot_general x22, matrix products, dot(): lax.dot_general(left, right, (((left_dim,), (right_dim,)), ((), ())), pre...  70 us
    ppermute x70, starting transfers between devices, swap(): return lax.ppermute(value, axis, [(i, i ^ mask) for i in range(size)])  64 us
    pallas_call x4, Pallas kernels, split_product(): pl.pallas_call(functools.partial(split_kernel, picks, tile, mode), out_sh...  27.9 us
    unnamed x242, local copies, waits for them, and re-layouts  25.3 us
    pallas_call x2, Pallas kernels, attend_back(): pl.pallas_call(functools.partial(attend_back_kernel, scale), grid=(heads...  25.1 us
    pallas_call x2, Pallas kernels, rows_home(): pl.pallas_call(functools.partial(back_kernel, len(values)), grid=(rows //...  21 us
    pallas_call x1, Pallas kernels, attend(): pl.pallas_call(functools.partial(attend_kernel, scale), grid=(heads,), in...  14.7 us
  transfers between devices with their start and end apart: 70, of which 22 were waited for; matrix products, arithmetic and copies ran while one was open for 31% of the time, Pallas kernels for 24%

profile of v3, /device:TPU:0, one launch (start us, length us, event | category | flops | bytes accessed | tf_op | source)
XLA Modules:
  0.0 508.5 jit_solution(15837395755085253341)
XLA Ops:
  5.0 5.0 collective-permute-start.2
  19.7 7.3 %collective-permute-done.1 = bf16[2,48,1024]{2,1,0:T(8,128)(2,1)S(1)} collective-permute-done((bf16[2,48,1024]{2,1,0:T(8,128)(2,1)}, bf16[2,48,1024]{2,1,0:T(8,128)(2,1)S(1)}, u32[]{:S(2)}, u32[]{:S(2)}) %collective-permute-start.1) | collective-permute-done | bytes 196640 | tf_op jit(solution)/shard_map/ppermute | solution.py:146
  84.5 14.7 %attend.1 = (bf16[16,32,640]{2,1,0:T(8,128)(2,1)S(1)}, bf16[16,32,640]{2,1,0:T(8,128)(2,1)S(1)}, f32[16,1,640]{2,1,0:T(1,128)S(1)}) custom-call(bf16[3,16,32,640]{3,2,1,0:T(8,128)(2,1)S(1)} %bitcast.527, bf16[3,16,32,640]{3,2,1,0:T(8,128)(2,1)S(1)} %bitcast.530, s32[640,1]{1,0:T(8,128)S(1)} %copy-done.13, s32[1,640]{1,0:T(1,128)S(1)} %sub.88.row_ref), custom_call_target="tpu_custom_call" | custom-call | tf_op jit(solution)/shard_map/attend/pallas_call | solution.py:613
  109.2 14.9 %collective-permute-done.18 = bf16[2,3,80,1024]{3,2,0,1:T(8,128)(2,1)S(1)} collective-permute-done((bf16[2,3,80,1024]{3,2,0,1:T(8,128)(2,1)S(1)}, bf16[2,3,80,1024]{3,2,0,1:T(8,128)(2,1)S(1)}, u32[]{:S(2)}, u32[]{:S(2)}) %collective-permute-start.18) | collective-permute-done | bytes 983072 | tf_op jit(solution)/shard_map/ppermute | solution.py:146
  142.6 5.1 multiply_convert_fusion.3
  161.4 6.5 %fusion.113 = f32[640,1024]{1,0:T(8,128)} fusion(bf16[640,2048]{1,0:T(8,128)(2,1)S(1)} %get-tuple-element.379.refs_0_, bf16[2048,1024]{1,0:T(8,128)(2,1)} %bitcast.602), kind=kOutput, calls=%fused_computation.417 | convolution fusion | flops 2684354560 | bytes 9437184 | tf_op jit(solution)/shard_map/dot_general | solution.py:43
  192.3 5.6 %multiply_convert_fusion.1.second_ref = bf16[640,2048]{1,0:T(8,128)(2,1)} fusion(f32[640,2048]{1,0:T(8,128)S(1)} %bitcast.703, bf16[640,1024]{1,0:T(8,128)(2,1)S(1)} %get-tuple-element.182.refs_1_, bf16[2048,1024]{1,0:T(8,128)(2,1)S(1)} %bitcast.605), kind=kOutput, calls=%fused_computation.13 | convolution fusion | flops 2700083200 | bytes 13369344 | tf_op jit(solution)/shard_map/dot_general | solution.py:43
  199.5 9.3 %split_product.4 = (bf16[512,1024]{1,0:T(8,128)(2,1)S(1)}, bf16[640,1024]{1,0:T(8,128)(2,1)}, bf16[640,1024]{1,0:T(8,128)(2,1)S(1)}) custom-call(bf16[640,2048]{1,0:T(8,128)(2,1)} %copy-done.48, bf16[640,1024]{1,0:T(8,128)(2,1)} %copy-done.7, bf16[640,2048]{1,0:T(8,128)(2,1)} %copy-done.49, bf16[640,1024]{1,0:T(8,128)(2,1)} %copy-done.52, ...), custom_call_target="tpu_custom_call" | custom-call | tf_op jit(solution)/shard_map/split_product/pallas_call | solution.py:480
  209.8 6.4 %split_product.5 = (bf16[640,1024]{1,0:T(8,128)(2,1)S(1)}, bf16[640,1024]{1,0:T(8,128)(2,1)S(1)}) custom-call(bf16[640,2048]{1,0:T(8,128)(2,1)} %copy-done.48, bf16[640,1024]{1,0:T(8,128)(2,1)S(1)} %copy-done.8, bf16[640,2048]{1,0:T(8,128)(2,1)} %copy-done.49, bf16[640,1024]{1,0:T(8,128)(2,1)} %copy-done.52, s32[1]{0:T(128)} %bitcast.133.refs_4_.index_ref, ...), custom_call_target="tpu_custom_call" | custom-call | tf_op jit(solution)/shard_map/split_product/pallas_call | solution.py:480
  217.7 9.0 %multiply_convert_fusion.first_ref.refs_0_ = bf16[640,2048]{1,0:T(8,128)(2,1)} fusion(bf16[640,1024]{1,0:T(8,128)(2,1)S(1)} %copy-done.8, bf16[2048,1024]{1,0:T(8,128)(2,1)} %bitcast.603, f32[640,2048]{1,0:T(8,128)} %get-tuple-element.380), kind=kOutput, calls=%fused_computation.12 | convolution fusion | flops 2700083200 | bytes 13369344 | tf_op jit(solution)/shard_map/dot_general | solution.py:43
  226.7 12.7 %rows_back.1 = (f32[640,1024]{1,0:T(8,128)S(1)}, bf16[640,1024]{1,0:T(8,128)(2,1)S(1)}, f32[1,1024]{1,0:T(1,128)S(1)}) custom-call(bf16[640,2048]{1,0:T(8,128)(2,1)} %multiply_convert_fusion.first_ref.refs_0_, bf16[640,2048]{1,0:T(8,128)(2,1)} %multiply_convert_fusion.1.second_ref, bf16[2048,1024]{1,0:T(8,128)(2,1)} %bitcast.558, ...), custom_call_target="tpu_custom_call" | custom-call | tf_op jit(solution)/shard_map/rows_back/pallas_call | solution.py:553
  250.9 6.1 %split_product.6 = (bf16[512,1024]{1,0:T(8,128)(2,1)S(1)}, bf16[512,1024]{1,0:T(8,128)(2,1)S(1)}) custom-call(bf16[640,2048]{1,0:T(8,128)(2,1)} %multiply_convert_fusion.first_ref.refs_0_, bf16[640,1024]{1,0:T(8,128)(2,1)S(1)} %get-tuple-element.170.refs_1_, bf16[640,2048]{1,0:T(8,128)(2,1)} %collective-permute-done.37.refs_2_, ...), custom_call_target="tpu_custom_call" | custom-call | tf_op jit(solution)/shard_map/split_product/pallas_call | solution.py:480
  268.5 6.1 %split_product.7 = (bf16[512,1024]{1,0:T(8,128)(2,1)}, bf16[512,1024]{1,0:T(8,128)(2,1)S(1)}) custom-call(bf16[640,2048]{1,0:T(8,128)(2,1)} %multiply_convert_fusion.first_ref.refs_0_, bf16[640,1024]{1,0:T(8,128)(2,1)S(1)} %copy-done.6, bf16[640,2048]{1,0:T(8,128)(2,1)} %collective-permute-done.37.refs_2_, bf16[640,1024]{1,0:T(8,128)(2,1)S(1)} %copy-done.16), custom_call_target="tpu_custom_call" | custom-call | tf_op jit(solution)/shard_map/split_product/pallas_call | solution.py:480
  276.8 12.5 %attend_back.2 = (bf16[3,16,32,640]{3,2,1,0:T(8,128)(2,1)S(1)}, bf16[3,16,32,640]{3,2,1,0:T(8,128)(2,1)}) custom-call(bf16[3,16,32,640]{3,2,1,0:T(8,128)(2,1)} %bitcast.528, bf16[3,16,32,640]{3,2,1,0:T(8,128)(2,1)} %bitcast.531, bf16[16,32,640]{2,1,0:T(8,128)(2,1)S(1)} %get-tuple-element.144.mixed_first_ref, ...), custom_call_target="tpu_custom_call" | custom-call | tf_op jit(solution)/shard_map/attend_back/pallas_call | solution.py:674
  296.4 12.6 %attend_back.3 = (bf16[3,16,32,640]{3,2,1,0:T(8,128)(2,1)S(1)}, bf16[3,16,32,640]{3,2,1,0:T(8,128)(2,1)}) custom-call(bf16[3,16,32,640]{3,2,1,0:T(8,128)(2,1)} %bitcast.529, bf16[3,16,32,640]{3,2,1,0:T(8,128)(2,1)} %bitcast.532, bf16[16,32,640]{2,1,0:T(8,128)(2,1)S(1)} %get-tuple-element.144.mixed_first_ref, ...), custom_call_target="tpu_custom_call", output_to_operand_aliasing={{0}: (9, {}), {1}: (10, {})} | custom-call | tf_op jit(solution)/shard_map/attend_back/pallas_call | solution.py:674
  333.2 7.9 %pair_product.2 = bf16[1536,1024]{1,0:T(8,128)(2,1)} custom-call(bf16[1536,640]{1,0:T(8,128)(2,1)S(1)} %bitcast.540, bf16[640,1024]{1,0:T(8,128)(2,1)S(1)} %copy-done.10, bf16[1536,640]{1,0:T(8,128)(2,1)} %collective-permute-done.43.left_mate_ref, bf16[640,1024]{1,0:T(8,128)(2,1)S(1)} %copy-done.24), custom_call_target="tpu_custom_call" | custom-call | tf_op jit(solution)/shard_map/pair_product/pallas_call | solution.py:424
  356.1 9.8 %collective-permute-done.52 = bf16[2,128,1024]{2,1,0:T(8,128)(2,1)S(1)} collective-permute-done((bf16[2,128,1024]{2,1,0:T(8,128)(2,1)S(1)}, bf16[2,128,1024]{2,1,0:T(8,128)(2,1)S(1)}, u32[]{:S(2)}, u32[]{:S(2)}) %collective-permute-start.52) | collective-permute-done | bytes 524320 | tf_op jit(solution)/shard_map/ppermute | solution.py:146
  366.8 8.0 %collective-permute-done.55 = bf16[544,1024]{1,0:T(8,128)(2,1)S(1)} collective-permute-done((bf16[544,1024]{1,0:T(8,128)(2,1)S(1)}, bf16[544,1024]{1,0:T(8,128)(2,1)S(1)}, u32[]{:S(2)}, u32[]{:S(2)}) %collective-permute-start.55) | collective-permute-done | bytes 1114144 | tf_op jit(solution)/shard_map/ppermute | solution.py:146
  383.7 6.5 %collective-permute-done.56 = bf16[272,1024]{1,0:T(8,128)(2,1)S(1)} collective-permute-done((bf16[272,1024]{1,0:T(8,128)(2,1)S(1)}, bf16[272,1024]{1,0:T(8,128)(2,1)S(1)}, u32[]{:S(2)}, u32[]{:S(2)}) %collective-permute-start.56) | collective-permute-done | bytes 557088 | tf_op jit(solution)/shard_map/ppermute | solution.py:146
  396.6 30.7 %collective-permute-done.50 = bf16[2,320,1024]{2,1,0:T(8,128)(2,1)S(1)} collective-permute-done((bf16[2,320,1024]{2,1,0:T(8,128)(2,1)S(1)}, bf16[2,320,1024]{2,1,0:T(8,128)(2,1)S(1)}, u32[]{:S(2)}, u32[]{:S(2)}) %collective-permute-start.50) | collective-permute-done | bytes 1310752 | tf_op jit(solution)/shard_map/ppermute | solution.py:146
  438.3 11.9 %rows_home.2.refs_3_ = bf16[2048,1024]{1,0:T(8,128)(2,1)} custom-call(s32[1,1600]{1,0:T(1,128)S(1)} %broadcast_in_dim.32.source_ref, bf16[640,1024]{1,0:T(8,128)(2,1)S(1)} %add_convert_fusion.refs_0_, bf16[320,1024]{1,0:T(8,128)(2,1)S(1)} %get-tuple-element.273.refs_1_, bf16[320,1024]{1,0:T(8,128)(2,1)S(1)} %get-tuple-element.272.refs_2_, ...), custom_call_target="tpu_custom_call" | custom-call | tf_op jit(solution)/shard_map/rows_home/pallas_call | solution.py:511
  455.6 15.7 %collective-permute-done.61 = bf16[2,80,1024]{2,1,0:T(8,128)(2,1)S(1)} collective-permute-done((bf16[2,80,1024]{2,1,0:T(8,128)(2,1)S(1)}, bf16[2,80,1024]{2,1,0:T(8,128)(2,1)S(1)}, u32[]{:S(2)}, u32[]{:S(2)}) %collective-permute-start.61) | collective-permute-done | bytes 327712 | tf_op jit(solution)/shard_map/ppermute | solution.py:146
  477.1 7.7 %place_rows.2 = (f32[1,1024,1024]{2,1,0:T(8,128)}, f32[1,1024,1024]{2,1,0:T(8,128)}, f32[1,1024,1024]{2,1,0:T(8,128)}) custom-call(s32[1]{0:T(128)} %bitcast.133.refs_4_.index_ref, bf16[4,192,1024]{2,1,0:T(8,128)(2,1)S(1)} %bitcast.542, bf16[4,192,1024]{2,1,0:T(8,128)(2,1)S(1)} %bitcast.544, bf16[4,192,1024]{2,1,0:T(8,128)(2,1)S(1)} %collective-permute-done.65.refs_2_, ...), custom_call_target="tpu_custom_call" | custom-call | tf_op jit(solution)/shard_map/place_rows/pallas_call | solution.py:392
  494.6 9.1 %rows_home.3 = bf16[2048,1024]{1,0:T(8,128)(2,1)} custom-call(s32[1,960]{1,0:T(1,128)S(1)} %bitcast.555, bf16[320,1024]{1,0:T(8,128)(2,1)S(1)} %get-tuple-element.270.refs_0_, bf16[320,1024]{1,0:T(8,128)(2,1)S(1)} %get-tuple-element.269.refs_1_, bf16[320,1024]{1,0:T(8,128)(2,1)S(1)} %get-tuple-element.268.refs_2_, bf16[2048,1024]{1,0:T(8,128)(2,1)S(1)} %copy-done.4), custom_call_target="tpu_custom_call" | custom-call | tf_op jit(solution)/shard_map/rows_home/pallas_call | solution.py:511
  (606 shorter events, 263.5 us)
Async XLA Ops:
  28.5 37.7 %collective-permute-start.11 = (bf16[2,80,1024]{2,1,0:T(8,128)(2,1)}, bf16[2,80,1024]{2,1,0:T(8,128)(2,1)}, u32[]{:S(2)}, u32[]{:S(2)}) collective-permute-start(bf16[2,80,1024]{2,1,0:T(8,128)(2,1)} %constant_dynamic-update-slice_fusion), channel_id=1, source_target_pairs={{0,3},{1,2},{2,1},{3,0},{4,7},{5,6},{6,5},{7,4},{8,11},{9,10},{10,... | collective-permute-start | bytes 983048 | tf_op jit(solution)/shard_map/ppermute | solution.py:146
  31.0 35.3 %collective-permute-start.10 = (bf16[2,80,1024]{2,1,0:T(8,128)(2,1)}, bf16[2,80,1024]{2,1,0:T(8,128)(2,1)}, u32[]{:S(2)}, u32[]{:S(2)}) collective-permute-start(bf16[2,80,1024]{2,1,0:T(8,128)(2,1)} %constant_dynamic-update-slice_fusion), channel_id=1, source_target_pairs={{0,2},{1,3},{2,0},{3,1},{4,6},{5,7},{6,4},{7,5},{8,10},{9,11},{10,... | collective-permute-start | bytes 983048 | tf_op jit(solution)/shard_map/ppermute | solution.py:146
  31.0 35.3 %collective-permute-start.9 = (bf16[2,80,1024]{2,1,0:T(8,128)(2,1)}, bf16[2,80,1024]{2,1,0:T(8,128)(2,1)}, u32[]{:S(2)}, u32[]{:S(2)}) collective-permute-start(bf16[2,80,1024]{2,1,0:T(8,128)(2,1)} %constant_dynamic-update-slice_fusion), channel_id=1, source_target_pairs={{0,1},{1,0},{2,3},{3,2},{4,5},{5,4},{6,7},{7,6},{8,9},{9,8},{10,11... | collective-permute-start | bytes 983048 | tf_op jit(solution)/shard_map/ppermute | solution.py:146
  41.7 30.3 %collective-permute-start.6 = (bf16[2,3,48,1024]{3,2,0,1:T(8,128)(2,1)}, bf16[2,3,48,1024]{3,2,0,1:T(8,128)(2,1)}, u32[]{:S(2)}, u32[]{:S(2)}) collective-permute-start(bf16[2,3,48,1024]{3,2,0,1:T(8,128)(2,1)} %get-tuple-element.334), channel_id=1, source_target_pairs={{0,8},{4,12},{8,0},{12,4},{16,24},{20,28},{24,16},{28,20},{1,9},{5... | collective-permute-start | bytes 1769480 | tf_op jit(solution)/shard_map/ppermute | solution.py:146
  43.6 29.8 %collective-permute-start.5 = (bf16[2,3,48,1024]{3,2,0,1:T(8,128)(2,1)}, bf16[2,3,48,1024]{3,2,0,1:T(8,128)(2,1)}, u32[]{:S(2)}, u32[]{:S(2)}) collective-permute-start(bf16[2,3,48,1024]{3,2,0,1:T(8,128)(2,1)} %get-tuple-element.332), channel_id=1, source_target_pairs={{0,16},{4,20},{8,24},{12,28},{16,0},{20,4},{24,8},{28,12},{1,17},{... | collective-permute-start | bytes 1769480 | tf_op jit(solution)/shard_map/ppermute | solution.py:146
  67.6 35.6 %collective-permute-start.17 = (bf16[2,64,1024]{2,1,0:T(8,128)(2,1)}, bf16[2,64,1024]{2,1,0:T(8,128)(2,1)}, u32[]{:S(2)}, u32[]{:S(2)}) collective-permute-start(bf16[2,64,1024]{2,1,0:T(8,128)(2,1)} %dynamic-slice_bitcast_fusion), channel_id=1, source_target_pairs={{0,3},{1,2},{2,1},{3,0},{4,7},{5,6},{6,5},{7,4},{8,11},{9,10},{10,... | collective-permute-start | bytes 786440 | tf_op jit(solution)/shard_map/ppermute | solution.py:146
  69.9 33.3 %collective-permute-start.16 = (bf16[2,64,1024]{2,1,0:T(8,128)(2,1)}, bf16[2,64,1024]{2,1,0:T(8,128)(2,1)}, u32[]{:S(2)}, u32[]{:S(2)}) collective-permute-start(bf16[2,64,1024]{2,1,0:T(8,128)(2,1)} %dynamic-slice_bitcast_fusion), channel_id=1, source_target_pairs={{0,2},{1,3},{2,0},{3,1},{4,6},{5,7},{6,4},{7,5},{8,10},{9,11},{10,... | collective-permute-start | bytes 786440 | tf_op jit(solution)/shard_map/ppermute | solution.py:146
  69.9 33.3 %collective-permute-start.15 = (bf16[2,64,1024]{2,1,0:T(8,128)(2,1)}, bf16[2,64,1024]{2,1,0:T(8,128)(2,1)}, u32[]{:S(2)}, u32[]{:S(2)}) collective-permute-start(bf16[2,64,1024]{2,1,0:T(8,128)(2,1)} %dynamic-slice_bitcast_fusion), channel_id=1, source_target_pairs={{0,1},{1,0},{2,3},{3,2},{4,5},{5,4},{6,7},{7,6},{8,9},{9,8},{10,11... | collective-permute-start | bytes 786440 | tf_op jit(solution)/shard_map/ppermute | solution.py:146
  106.1 26.8 %collective-permute-start.21 = (bf16[3,64,1024]{2,1,0:T(8,128)(2,1)}, bf16[3,64,1024]{2,1,0:T(8,128)(2,1)}, u32[]{:S(2)}, u32[]{:S(2)}) collective-permute-start(bf16[3,64,1024]{2,1,0:T(8,128)(2,1)} %get-tuple-element.327), channel_id=1, source_target_pairs={{0,16},{4,20},{8,24},{12,28},{16,0},{20,4},{24,8},{28,12},{1,17},{... | collective-permute-start | bytes 1179656 | tf_op jit(solution)/shard_map/ppermute | solution.py:146
  147.7 34.8 %collective-permute-start.30 = (bf16[640,1024]{1,0:T(8,128)(2,1)S(1)}, bf16[640,1024]{1,0:T(8,128)(2,1)S(1)}, u32[]{:S(2)}, u32[]{:S(2)}) collective-permute-start(bf16[640,1024]{1,0:T(8,128)(2,1)S(1)} %get-tuple-element.170.refs_1_), channel_id=1, source_target_pairs={{0,4},{4,0},{8,12},{12,8},{16,20},{20,16},{24,28},{28,24},{1,5},{5... | collective-permute-start | bytes 3932168 | tf_op jit(solution)/shard_map/ppermute | solution.py:146
  198.0 52.9 %collective-permute-start.37 = (bf16[640,2048]{1,0:T(8,128)(2,1)}, bf16[640,2048]{1,0:T(8,128)(2,1)}, u32[]{:S(2)}, u32[]{:S(2)}) collective-permute-start(bf16[640,2048]{1,0:T(8,128)(2,1)} %multiply_convert_fusion.1.second_ref), channel_id=1, source_target_pairs={{0,4},{4,0},{8,12},{12,8},{16,20},{20,16},{24,28},{28,24},{1,5},{5... | collective-permute-start | bytes 7864328 | tf_op jit(solution)/shard_map/ppermute | solution.py:146
  208.8 32.6 %collective-permute-start.34 = (bf16[640,1024]{1,0:T(8,128)(2,1)}, bf16[640,1024]{1,0:T(8,128)(2,1)}, u32[]{:S(2)}, u32[]{:S(2)}) collective-permute-start(bf16[640,1024]{1,0:T(8,128)(2,1)} %get-tuple-element.180), channel_id=1, source_target_pairs={{0,16},{4,20},{8,24},{12,28},{16,0},{20,4},{24,8},{28,12},{1,17},{... | collective-permute-start | bytes 3932168 | tf_op jit(solution)/shard_map/ppermute | solution.py:146
  216.2 30.6 %collective-permute-start.36 = (bf16[640,1024]{1,0:T(8,128)(2,1)S(1)}, bf16[640,1024]{1,0:T(8,128)(2,1)}, u32[]{:S(2)}, u32[]{:S(2)}) collective-permute-start(bf16[640,1024]{1,0:T(8,128)(2,1)S(1)} %get-tuple-element.187), channel_id=1, source_target_pairs={{0,8},{4,12},{8,0},{12,4},{16,24},{20,28},{24,16},{28,20},{1,9},{5... | collective-permute-start | bytes 3932168 | tf_op jit(solution)/shard_map/ppermute | solution.py:146
  274.6 45.5 %collective-permute-start.41 = (bf16[512,1024]{1,0:T(8,128)(2,1)}, bf16[512,1024]{1,0:T(8,128)(2,1)}, u32[]{:S(2)}, u32[]{:S(2)}) collective-permute-start(bf16[512,1024]{1,0:T(8,128)(2,1)} %get-tuple-element.196), channel_id=1, source_target_pairs={{0,16},{4,20},{8,24},{12,28},{16,0},{20,4},{24,8},{28,12},{1,17},{... | collective-permute-start | bytes 3145736 | tf_op jit(solution)/shard_map/ppermute | solution.py:146
  276.0 47.0 %collective-permute-start.42 = (bf16[512,1024]{1,0:T(8,128)(2,1)S(1)}, bf16[512,1024]{1,0:T(8,128)(2,1)}, u32[]{:S(2)}, u32[]{:S(2)}) collective-permute-start(bf16[512,1024]{1,0:T(8,128)(2,1)S(1)} %get-tuple-element.198), channel_id=1, source_target_pairs={{0,8},{4,12},{8,0},{12,4},{16,24},{20,28},{24,16},{28,20},{1,9},{5... | collective-permute-start | bytes 3145736 | tf_op jit(solution)/shard_map/ppermute | solution.py:146
  276.7 49.1 %collective-permute-start.44 = (bf16[640,1024]{1,0:T(8,128)(2,1)S(1)}, bf16[640,1024]{1,0:T(8,128)(2,1)S(1)}, u32[]{:S(2)}, u32[]{:S(2)}) collective-permute-start(bf16[640,1024]{1,0:T(8,128)(2,1)S(1)} %copy-done.12), channel_id=1, source_target_pairs={{0,4},{4,0},{8,12},{12,8},{16,20},{20,16},{24,28},{28,24},{1,5},{5... | collective-permute-start | bytes 3932168 | tf_op jit(solution)/shard_map/ppermute | solution.py:146
  293.7 47.4 %collective-permute-start.40 = (bf16[2,160,1024]{2,1,0:T(8,128)(2,1)}, bf16[2,160,1024]{2,1,0:T(8,128)(2,1)}, u32[]{:S(2)}, u32[]{:S(2)}) collective-permute-start(bf16[2,160,1024]{2,1,0:T(8,128)(2,1)} %pad_maximum_fusion.32), channel_id=1, source_target_pairs={{0,2},{1,3},{2,0},{3,1},{4,6},{5,7},{6,4},{7,5},{8,10},{9,11},{10,... | collective-permute-start | bytes 1966088 | tf_op jit(solution)/shard_map/ppermute | solution.py:146
  323.0 31.8 %collective-permute-start.45 = (bf16[1,320,1024]{2,1,0:T(8,128)(2,1)}, bf16[1,320,1024]{2,1,0:T(8,128)(2,1)}, u32[]{:S(2)}, u32[]{:S(2)}) collective-permute-start(bf16[1,320,1024]{2,1,0:T(8,128)(2,1)} %get-tuple-element.295), channel_id=1, source_target_pairs={{0,2},{1,3},{2,0},{3,1},{4,6},{5,7},{6,4},{7,5},{8,10},{9,11},{10,... | collective-permute-start | bytes 1966088 | tf_op jit(solution)/shard_map/ppermute | solution.py:146
  379.9 47.9 %collective-permute-start.49 = (bf16[1,320,1024]{2,1,0:T(8,128)(2,1)S(1)}, bf16[1,320,1024]{2,1,0:T(8,128)(2,1)S(1)}, u32[]{:S(2)}, u32[]{:S(2)}) collective-permute-start(bf16[1,320,1024]{2,1,0:T(8,128)(2,1)S(1)} %bitcast.625), channel_id=1, source_target_pairs={{0,2},{1,3},{2,0},{3,1},{4,6},{5,7},{6,4},{7,5},{8,10},{9,11},{10,... | collective-permute-start | bytes 1966088 | tf_op jit(solution)/shard_map/ppermute | solution.py:146
  382.5 44.9 %collective-permute-start.50 = (bf16[2,320,1024]{2,1,0:T(8,128)(2,1)S(1)}, bf16[2,320,1024]{2,1,0:T(8,128)(2,1)S(1)}, u32[]{:S(2)}, u32[]{:S(2)}) collective-permute-start(bf16[2,320,1024]{2,1,0:T(8,128)(2,1)S(1)} %get-tuple-element.293), channel_id=1, source_target_pairs={{0,1},{1,0},{2,3},{3,2},{4,5},{5,4},{6,7},{7,6},{8,9},{9,8},{10,11... | collective-permute-start | bytes 3932168 | tf_op jit(solution)/shard_map/ppermute | solution.py:146
  382.7 46.8 %collective-permute-start.59 = (bf16[192,1024]{1,0:T(8,128)(2,1)S(1)}, bf16[192,1024]{1,0:T(8,128)(2,1)S(1)}, u32[]{:S(2)}, u32[]{:S(2)}) collective-permute-start(bf16[192,1024]{1,0:T(8,128)(2,1)S(1)} %bitcast.636), channel_id=1, source_target_pairs={{0,8},{4,12},{8,0},{12,4},{16,24},{20,28},{24,16},{28,20},{1,9},{5... | collective-permute-start | bytes 1179656 | tf_op jit(solution)/shard_map/ppermute | solution.py:146
  390.2 39.3 %collective-permute-start.60 = (bf16[192,1024]{1,0:T(8,128)(2,1)S(1)}, bf16[192,1024]{1,0:T(8,128)(2,1)S(1)}, u32[]{:S(2)}, u32[]{:S(2)}) collective-permute-start(bf16[192,1024]{1,0:T(8,128)(2,1)S(1)} %bitcast.635), channel_id=1, source_target_pairs={{0,16},{4,20},{8,24},{12,28},{16,0},{20,4},{24,8},{28,12},{1,17},{... | collective-permute-start | bytes 1179656 | tf_op jit(solution)/shard_map/ppermute | solution.py:146
  394.9 41.5 %collective-permute-start.58 = (bf16[2,144,1024]{2,1,0:T(8,128)(2,1)S(1)}, bf16[2,144,1024]{2,1,0:T(8,128)(2,1)S(1)}, u32[]{:S(2)}, u32[]{:S(2)}) collective-permute-start(bf16[2,144,1024]{2,1,0:T(8,128)(2,1)S(1)} %maximum_maximum_fusion), channel_id=1, source_target_pairs={{0,1},{1,0},{2,3},{3,2},{4,5},{5,4},{6,7},{7,6},{8,9},{9,8},{10,11... | collective-permute-start | bytes 1769480 | tf_op jit(solution)/shard_map/ppermute | solution.py:146
  454.6 37.6 %collective-permute-start.57 = (bf16[2,320,1024]{2,1,0:T(8,128)(2,1)S(1)}, bf16[2,320,1024]{2,1,0:T(8,128)(2,1)S(1)}, u32[]{:S(2)}, u32[]{:S(2)}) collective-permute-start(bf16[2,320,1024]{2,1,0:T(8,128)(2,1)S(1)} %copy-done.75), channel_id=1, source_target_pairs={{0,1},{1,0},{2,3},{3,2},{4,5},{5,4},{6,7},{7,6},{8,9},{9,8},{10,11... | collective-permute-start | bytes 3932168 | tf_op jit(solution)/shard_map/ppermute | solution.py:146
  (150 other events, 1755.4 us)

commit v4 on v3

--- a/solution.py
+++ b/solution.py
@@ -931,17 +931,16 @@
     ring_b.go(rows_a)
     while x_seen.left > 1:
         x_seen.go(*ring_b.sent)
+
     z_qkv.go(*x_seen.sent)
-
     sources = [source] + [row_map(place, counts, tensor_index ^ j, capacity)[1] for j in range(1, n_tensor)]
     blocks = [(after(source, *z_qkv.sent), near)]
     blocks += [(sources[j][:some], rows_a[j]) for j in range(1, n_tensor)]
     early = rows_home(blocks, rows)
-    near_seen = x_seen.finish(early)
+    (sum_qkv,) = z_qkv.finish(early)
+    x_last = Flow(1, plane_spread(sum_qkv, n_dp))
+    near_seen = x_seen.finish(*x_last.sent)
     seen_a = both_near(near_seen, n_dp)
-    (sum_qkv,) = z_qkv.finish(*near_seen)
-    x_last = Flow(1, plane_spread(sum_qkv, n_dp))
-    seen_a[1] = [after(v, *x_last.sent) for v in seen_a[1]]
     down_rows = up_rows = active[0].shape[1] // (n_tensor * n_dp)
     out_rows, qkv_rows, extra_rows = [
         grad.shape[0] // (parts * n_dp * lead)
@@ -959,11 +958,10 @@
         n_dp,
         index,
     )
-    near_c = x_last.finish(down_sum)
+    (rows_b,) = ring_b.finish(*x_last.sent)
+    input_grad = rows_home([(sources[j][some:], rows_b[j]) for j in range(1, n_tensor)], rows, early)
+    near_c = x_last.finish(input_grad, down_sum)
     far_c = mate(jnp.stack(near_c))
-    (rows_b,) = ring_b.finish(*near_c)
-    input_grad = rows_home([(sources[j][some:], rows_b[j]) for j in range(1, n_tensor)], rows, early)
-    far_c = after(far_c, input_grad)
     far_c = [far_c[link] for link in range(n_dp // 2)]
     qkv_sum, out_sum = place_rows(
         near_c, far_c, ((0, 3, qkv_rows, "turned"), (3 * qkv_rows, 1, out_rows, "plain")), n_dp, index

time: 516 us -> 504 us (0.977)
  waiting for transfers between devices: 129 us -> 112 us
    ppermute x70, waiting for transfers between devices: 129 us -> 112 us  [swap(): return lax.ppermute(value, axis, [(i, i ^ mask) for i in range(size)])]
    unnamed x242 -> x238, local copies, waits for them, and re-layouts: 25.3 us -> 25.3 us
  transfers between devices with their start and end apart: 70 -> 70, of which waited for: 22 -> 19; matrix products, arithmetic and copies ran while one was open for 31% -> 32% of each run, Pallas kernels for 24% -> 25%
where the time goes in v4:
time: 504 us; the launch traced here: 496 us
  Pallas kernels  125 us (25%)
  waiting for transfers between devices  112 us (22%)
  matrix products  70.1 us (14%)
  starting transfers between devices  66 us (13%)
  other arithmetic  64.5 us (13%)
  local copies, waits for them, and re-layouts  54.2 us (11%)
    ppermute x70, waiting for transfers between devices, swap(): return lax.ppermute(value, axis, [(i, i ^ mask) for i in range(size)])  112 us
    dot_general x22, matrix products, dot(): lax.dot_general(left, right, (((left_dim,), (right_dim,)), ((), ())), pre...  70.1 us
    ppermute x70, starting transfers between devices, swap(): return lax.ppermute(value, axis, [(i, i ^ mask) for i in range(size)])  66 us
    pallas_call x4, Pallas kernels, split_product(): pl.pallas_call(functools.partial(split_kernel, picks, tile, mode), out_sh...  27.9 us
    unnamed x238, local copies, waits for them, and re-layouts  25.3 us
    pallas_call x2, Pallas kernels, attend_back(): pl.pallas_call(functools.partial(attend_back_kernel, scale), grid=(heads...  25.1 us
    pallas_call x2, Pallas kernels, rows_home(): pl.pallas_call(functools.partial(back_kernel, len(values)), grid=(rows //...  21.2 us
    pallas_call x1, Pallas kernels, attend(): pl.pallas_call(functools.partial(attend_kernel, scale), grid=(heads,), in...  14.7 us
  transfers between devices with their start and end apart: 70, of which 19 were waited for; matrix products, arithmetic and copies ran while one was open for 32% of the time, Pallas kernels for 25%

profile of v4, /device:TPU:0, one launch (start us, length us, event | category | flops | bytes accessed | tf_op | source)
XLA Modules:
  0.0 496.1 jit_solution(3030572633011911634)
XLA Ops:
  5.0 5.0 %collective-permute-start.2 = (bf16[2,48,1024]{2,1,0:T(8,128)(2,1)}, bf16[2,48,1024]{2,1,0:T(8,128)(2,1)S(1)}, u32[]{:S(2)}, u32[]{:S(2)}) collective-permute-start(bf16[2,48,1024]{2,1,0:T(8,128)(2,1)} %bitcast.8), channel_id=1, source_target_pairs={{0,3},{1,2},{2,1},{3,0},{4,7},{5,6},{6,5},{7,4},{8,11},{9,10},{10,... | collective-permute-start | bytes 589832 | tf_op jit(solution)/shard_map/ppermute | solution.py:146
  19.7 7.3 %collective-permute-done.1 = bf16[2,48,1024]{2,1,0:T(8,128)(2,1)S(1)} collective-permute-done((bf16[2,48,1024]{2,1,0:T(8,128)(2,1)}, bf16[2,48,1024]{2,1,0:T(8,128)(2,1)S(1)}, u32[]{:S(2)}, u32[]{:S(2)}) %collective-permute-start.1) | collective-permute-done | bytes 196640 | tf_op jit(solution)/shard_map/ppermute | solution.py:146
  84.5 14.7 %attend.1 = (bf16[16,32,640]{2,1,0:T(8,128)(2,1)S(1)}, bf16[16,32,640]{2,1,0:T(8,128)(2,1)S(1)}, f32[16,1,640]{2,1,0:T(1,128)S(1)}) custom-call(bf16[3,16,32,640]{3,2,1,0:T(8,128)(2,1)S(1)} %bitcast.527, bf16[3,16,32,640]{3,2,1,0:T(8,128)(2,1)S(1)} %bitcast.530, s32[640,1]{1,0:T(8,128)S(1)} %copy-done.13, s32[1,640]{1,0:T(1,128)S(1)} %sub.88.row_ref), custom_call_target="tpu_custom_call" | custom-call | tf_op jit(solution)/shard_map/attend/pallas_call | solution.py:613
  109.2 14.9 %collective-permute-done.18 = bf16[2,3,80,1024]{3,2,0,1:T(8,128)(2,1)S(1)} collective-permute-done((bf16[2,3,80,1024]{3,2,0,1:T(8,128)(2,1)S(1)}, bf16[2,3,80,1024]{3,2,0,1:T(8,128)(2,1)S(1)}, u32[]{:S(2)}, u32[]{:S(2)}) %collective-permute-start.18) | collective-permute-done | bytes 983072 | tf_op jit(solution)/shard_map/ppermute | solution.py:146
  142.6 5.1 %multiply_convert_fusion.3 = (bf16[640,2048]{1,0:T(8,128)(2,1)S(1)}, f32[640,2048]{1,0:T(8,128)}) fusion(bf16[640,1024]{1,0:T(8,128)(2,1)S(1)} %get-tuple-element.167.refs_1_, bf16[2048,1024]{1,0:T(8,128)(2,1)S(1)} %bitcast.557), kind=kOutput, calls=%fused_computation.16 | convolution fusion | flops 2690908160 | bytes 13369344 | tf_op jit(solution)/shard_map/dot_general | solution.py:43
  161.5 6.5 %fusion.113 = f32[640,1024]{1,0:T(8,128)} fusion(bf16[640,2048]{1,0:T(8,128)(2,1)S(1)} %get-tuple-element.373.refs_0_, bf16[2048,1024]{1,0:T(8,128)(2,1)} %bitcast.602), kind=kOutput, calls=%fused_computation.417 | convolution fusion | flops 2684354560 | bytes 9437184 | tf_op jit(solution)/shard_map/dot_general | solution.py:43
  168.0 4.9 multiply_convert_fusion.2
  192.4 5.7 %multiply_convert_fusion.1.second_ref = bf16[640,2048]{1,0:T(8,128)(2,1)} fusion(f32[640,2048]{1,0:T(8,128)S(1)} %bitcast.702, bf16[640,1024]{1,0:T(8,128)(2,1)S(1)} %get-tuple-element.179.refs_1_, bf16[2048,1024]{1,0:T(8,128)(2,1)S(1)} %bitcast.605), kind=kOutput, calls=%fused_computation.13 | convolution fusion | flops 2700083200 | bytes 13369344 | tf_op jit(solution)/shard_map/dot_general | solution.py:43
  199.6 9.2 %split_product.4 = (bf16[512,1024]{1,0:T(8,128)(2,1)S(1)}, bf16[640,1024]{1,0:T(8,128)(2,1)}, bf16[640,1024]{1,0:T(8,128)(2,1)S(1)}) custom-call(bf16[640,2048]{1,0:T(8,128)(2,1)} %copy-done.48, bf16[640,1024]{1,0:T(8,128)(2,1)} %copy-done.7, bf16[640,2048]{1,0:T(8,128)(2,1)} %copy-done.49, bf16[640,1024]{1,0:T(8,128)(2,1)} %copy-done.52, ...), custom_call_target="tpu_custom_call" | custom-call | tf_op jit(solution)/shard_map/split_product/pallas_call | solution.py:480
  209.8 6.4 %split_product.5 = (bf16[640,1024]{1,0:T(8,128)(2,1)S(1)}, bf16[640,1024]{1,0:T(8,128)(2,1)S(1)}) custom-call(bf16[640,2048]{1,0:T(8,128)(2,1)} %copy-done.48, bf16[640,1024]{1,0:T(8,128)(2,1)S(1)} %copy-done.8, bf16[640,2048]{1,0:T(8,128)(2,1)} %copy-done.49, bf16[640,1024]{1,0:T(8,128)(2,1)} %copy-done.52, s32[1]{0:T(128)} %bitcast.133.refs_4_.index_ref, ...), custom_call_target="tpu_custom_call" | custom-call | tf_op jit(solution)/shard_map/split_product/pallas_call | solution.py:480
  217.8 9.0 %multiply_convert_fusion.first_ref.refs_0_ = bf16[640,2048]{1,0:T(8,128)(2,1)} fusion(bf16[640,1024]{1,0:T(8,128)(2,1)S(1)} %copy-done.8, bf16[2048,1024]{1,0:T(8,128)(2,1)} %bitcast.603, f32[640,2048]{1,0:T(8,128)} %get-tuple-element.374), kind=kOutput, calls=%fused_computation.12 | convolution fusion | flops 2700083200 | bytes 13369344 | tf_op jit(solution)/shard_map/dot_general | solution.py:43
  226.8 12.7 %rows_back.1 = (f32[640,1024]{1,0:T(8,128)S(1)}, bf16[640,1024]{1,0:T(8,128)(2,1)S(1)}, f32[1,1024]{1,0:T(1,128)S(1)}) custom-call(bf16[640,2048]{1,0:T(8,128)(2,1)} %multiply_convert_fusion.first_ref.refs_0_, bf16[640,2048]{1,0:T(8,128)(2,1)} %multiply_convert_fusion.1.second_ref, bf16[2048,1024]{1,0:T(8,128)(2,1)} %bitcast.558, ...), custom_call_target="tpu_custom_call" | custom-call | tf_op jit(solution)/shard_map/rows_back/pallas_call | solution.py:553
  251.0 6.1 %split_product.6 = (bf16[512,1024]{1,0:T(8,128)(2,1)S(1)}, bf16[512,1024]{1,0:T(8,128)(2,1)S(1)}) custom-call(bf16[640,2048]{1,0:T(8,128)(2,1)} %multiply_convert_fusion.first_ref.refs_0_, bf16[640,1024]{1,0:T(8,128)(2,1)S(1)} %get-tuple-element.167.refs_1_, bf16[640,2048]{1,0:T(8,128)(2,1)} %collective-permute-done.37.refs_2_, ...), custom_call_target="tpu_custom_call" | custom-call | tf_op jit(solution)/shard_map/split_product/pallas_call | solution.py:480
  268.5 6.1 %split_product.7 = (bf16[512,1024]{1,0:T(8,128)(2,1)}, bf16[512,1024]{1,0:T(8,128)(2,1)S(1)}) custom-call(bf16[640,2048]{1,0:T(8,128)(2,1)} %multiply_convert_fusion.first_ref.refs_0_, bf16[640,1024]{1,0:T(8,128)(2,1)S(1)} %copy-done.6, bf16[640,2048]{1,0:T(8,128)(2,1)} %collective-permute-done.37.refs_2_, bf16[640,1024]{1,0:T(8,128)(2,1)S(1)} %copy-done.16), custom_call_target="tpu_custom_call" | custom-call | tf_op jit(solution)/shard_map/split_product/pallas_call | solution.py:480
  276.8 12.5 %attend_back.2 = (bf16[3,16,32,640]{3,2,1,0:T(8,128)(2,1)S(1)}, bf16[3,16,32,640]{3,2,1,0:T(8,128)(2,1)}) custom-call(bf16[3,16,32,640]{3,2,1,0:T(8,128)(2,1)} %bitcast.528, bf16[3,16,32,640]{3,2,1,0:T(8,128)(2,1)} %bitcast.531, bf16[16,32,640]{2,1,0:T(8,128)(2,1)S(1)} %get-tuple-element.141.mixed_first_ref, ...), custom_call_target="tpu_custom_call" | custom-call | tf_op jit(solution)/shard_map/attend_back/pallas_call | solution.py:674
  296.5 12.6 %attend_back.3 = (bf16[3,16,32,640]{3,2,1,0:T(8,128)(2,1)S(1)}, bf16[3,16,32,640]{3,2,1,0:T(8,128)(2,1)}) custom-call(bf16[3,16,32,640]{3,2,1,0:T(8,128)(2,1)} %bitcast.529, bf16[3,16,32,640]{3,2,1,0:T(8,128)(2,1)} %bitcast.532, bf16[16,32,640]{2,1,0:T(8,128)(2,1)S(1)} %get-tuple-element.141.mixed_first_ref, ...), custom_call_target="tpu_custom_call", output_to_operand_aliasing={{0}: (9, {}), {1}: (10, {})} | custom-call | tf_op jit(solution)/shard_map/attend_back/pallas_call | solution.py:674
  333.2 7.9 %pair_product.2 = bf16[1536,1024]{1,0:T(8,128)(2,1)} custom-call(bf16[1536,640]{1,0:T(8,128)(2,1)S(1)} %bitcast.540, bf16[640,1024]{1,0:T(8,128)(2,1)S(1)} %copy-done.10, bf16[1536,640]{1,0:T(8,128)(2,1)} %collective-permute-done.43.left_mate_ref, bf16[640,1024]{1,0:T(8,128)(2,1)S(1)} %copy-done.24), custom_call_target="tpu_custom_call" | custom-call | tf_op jit(solution)/shard_map/pair_product/pallas_call | solution.py:424
  358.5 21.5 %collective-permute-done.52 = bf16[2,128,1024]{2,1,0:T(8,128)(2,1)S(1)} collective-permute-done((bf16[2,128,1024]{2,1,0:T(8,128)(2,1)S(1)}, bf16[2,128,1024]{2,1,0:T(8,128)(2,1)S(1)}, u32[]{:S(2)}, u32[]{:S(2)}) %collective-permute-start.52) | collective-permute-done | bytes 524320 | tf_op jit(solution)/shard_map/ppermute | solution.py:146
  384.5 26.0 %collective-permute-done.54 = bf16[2,64,1024]{2,1,0:T(8,128)(2,1)S(1)} collective-permute-done((bf16[2,64,1024]{2,1,0:T(8,128)(2,1)S(1)}, bf16[2,64,1024]{2,1,0:T(8,128)(2,1)S(1)}, u32[]{:S(2)}, u32[]{:S(2)}) %collective-permute-start.54) | collective-permute-done | bytes 262176 | tf_op jit(solution)/shard_map/ppermute | solution.py:146
  422.7 5.1 %collective-permute-done.58 = bf16[2,144,1024]{2,1,0:T(8,128)(2,1)S(1)} collective-permute-done((bf16[2,144,1024]{2,1,0:T(8,128)(2,1)S(1)}, bf16[2,144,1024]{2,1,0:T(8,128)(2,1)S(1)}, u32[]{:S(2)}, u32[]{:S(2)}) %collective-permute-start.58) | collective-permute-done | bytes 589856 | tf_op jit(solution)/shard_map/ppermute | solution.py:146
  434.3 11.9 %rows_home.2.refs_3_ = bf16[2048,1024]{1,0:T(8,128)(2,1)} custom-call(s32[1,1600]{1,0:T(1,128)S(1)} %broadcast_in_dim.32.source_ref, bf16[640,1024]{1,0:T(8,128)(2,1)S(1)} %add_convert_fusion.refs_0_, bf16[320,1024]{1,0:T(8,128)(2,1)S(1)} %get-tuple-element.267.refs_1_, bf16[320,1024]{1,0:T(8,128)(2,1)S(1)} %get-tuple-element.266.refs_2_, ...), custom_call_target="tpu_custom_call" | custom-call | tf_op jit(solution)/shard_map/rows_home/pallas_call | solution.py:511
  453.6 12.1 %collective-permute-done.57 = bf16[2,320,1024]{2,1,0:T(8,128)(2,1)} collective-permute-done((bf16[2,320,1024]{2,1,0:T(8,128)(2,1)}, bf16[2,320,1024]{2,1,0:T(8,128)(2,1)}, u32[]{:S(2)}, u32[]{:S(2)}) %collective-permute-start.57) | collective-permute-done | bytes 1310752 | tf_op jit(solution)/shard_map/ppermute | solution.py:146
  471.0 9.3 %rows_home.3 = bf16[2048,1024]{1,0:T(8,128)(2,1)} custom-call(s32[1,960]{1,0:T(1,128)S(1)} %bitcast.555, bf16[320,1024]{1,0:T(8,128)(2,1)S(1)} %get-tuple-element.264.refs_0_, bf16[320,1024]{1,0:T(8,128)(2,1)S(1)} %get-tuple-element.263.refs_1_, bf16[320,1024]{1,0:T(8,128)(2,1)S(1)} %get-tuple-element.262.refs_2_, bf16[2048,1024]{1,0:T(8,128)(2,1)S(1)} %copy-done.4), custom_call_target="tpu_custom_call" | custom-call | tf_op jit(solution)/shard_map/rows_home/pallas_call | solution.py:511
  481.5 7.7 %place_rows.2 = (f32[1,1024,1024]{2,1,0:T(8,128)}, f32[1,1024,1024]{2,1,0:T(8,128)}, f32[1,1024,1024]{2,1,0:T(8,128)}) custom-call(s32[1]{0:T(128)} %bitcast.133.refs_4_.index_ref, bf16[4,192,1024]{2,1,0:T(8,128)(2,1)S(1)} %bitcast.542, bf16[4,192,1024]{2,1,0:T(8,128)(2,1)S(1)} %bitcast.544, bf16[4,192,1024]{2,1,0:T(8,128)(2,1)S(1)} %collective-permute-done.65.refs_2_, ...), custom_call_target="tpu_custom_call" | custom-call | tf_op jit(solution)/shard_map/place_rows/pallas_call | solution.py:392
  (602 shorter events, 251.6 us)
Async XLA Ops:
  28.6 37.7 %collective-permute-start.11 = (bf16[2,80,1024]{2,1,0:T(8,128)(2,1)}, bf16[2,80,1024]{2,1,0:T(8,128)(2,1)}, u32[]{:S(2)}, u32[]{:S(2)}) collective-permute-start(bf16[2,80,1024]{2,1,0:T(8,128)(2,1)} %constant_dynamic-update-slice_fusion), channel_id=1, source_target_pairs={{0,3},{1,2},{2,1},{3,0},{4,7},{5,6},{6,5},{7,4},{8,11},{9,10},{10,... | collective-permute-start | bytes 983048 | tf_op jit(solution)/shard_map/ppermute | solution.py:146
  31.0 35.3 %collective-permute-start.10 = (bf16[2,80,1024]{2,1,0:T(8,128)(2,1)}, bf16[2,80,1024]{2,1,0:T(8,128)(2,1)}, u32[]{:S(2)}, u32[]{:S(2)}) collective-permute-start(bf16[2,80,1024]{2,1,0:T(8,128)(2,1)} %constant_dynamic-update-slice_fusion), channel_id=1, source_target_pairs={{0,2},{1,3},{2,0},{3,1},{4,6},{5,7},{6,4},{7,5},{8,10},{9,11},{10,... | collective-permute-start | bytes 983048 | tf_op jit(solution)/shard_map/ppermute | solution.py:146
  31.0 35.3 %collective-permute-start.9 = (bf16[2,80,1024]{2,1,0:T(8,128)(2,1)}, bf16[2,80,1024]{2,1,0:T(8,128)(2,1)}, u32[]{:S(2)}, u32[]{:S(2)}) collective-permute-start(bf16[2,80,1024]{2,1,0:T(8,128)(2,1)} %constant_dynamic-update-slice_fusion), channel_id=1, source_target_pairs={{0,1},{1,0},{2,3},{3,2},{4,5},{5,4},{6,7},{7,6},{8,9},{9,8},{10,11... | collective-permute-start | bytes 983048 | tf_op jit(solution)/shard_map/ppermute | solution.py:146
  41.8 30.3 %collective-permute-start.6 = (bf16[2,3,48,1024]{3,2,0,1:T(8,128)(2,1)}, bf16[2,3,48,1024]{3,2,0,1:T(8,128)(2,1)}, u32[]{:S(2)}, u32[]{:S(2)}) collective-permute-start(bf16[2,3,48,1024]{3,2,0,1:T(8,128)(2,1)} %get-tuple-element.328), channel_id=1, source_target_pairs={{0,8},{4,12},{8,0},{12,4},{16,24},{20,28},{24,16},{28,20},{1,9},{5... | collective-permute-start | bytes 1769480 | tf_op jit(solution)/shard_map/ppermute | solution.py:146
  67.6 35.6 %collective-permute-start.17 = (bf16[2,64,1024]{2,1,0:T(8,128)(2,1)}, bf16[2,64,1024]{2,1,0:T(8,128)(2,1)}, u32[]{:S(2)}, u32[]{:S(2)}) collective-permute-start(bf16[2,64,1024]{2,1,0:T(8,128)(2,1)} %dynamic-slice_bitcast_fusion), channel_id=1, source_target_pairs={{0,3},{1,2},{2,1},{3,0},{4,7},{5,6},{6,5},{7,4},{8,11},{9,10},{10,... | collective-permute-start | bytes 786440 | tf_op jit(solution)/shard_map/ppermute | solution.py:146
  69.9 33.3 %collective-permute-start.16 = (bf16[2,64,1024]{2,1,0:T(8,128)(2,1)}, bf16[2,64,1024]{2,1,0:T(8,128)(2,1)}, u32[]{:S(2)}, u32[]{:S(2)}) collective-permute-start(bf16[2,64,1024]{2,1,0:T(8,128)(2,1)} %dynamic-slice_bitcast_fusion), channel_id=1, source_target_pairs={{0,2},{1,3},{2,0},{3,1},{4,6},{5,7},{6,4},{7,5},{8,10},{9,11},{10,... | collective-permute-start | bytes 786440 | tf_op jit(solution)/shard_map/ppermute | solution.py:146
  69.9 33.3 %collective-permute-start.15 = (bf16[2,64,1024]{2,1,0:T(8,128)(2,1)}, bf16[2,64,1024]{2,1,0:T(8,128)(2,1)}, u32[]{:S(2)}, u32[]{:S(2)}) collective-permute-start(bf16[2,64,1024]{2,1,0:T(8,128)(2,1)} %dynamic-slice_bitcast_fusion), channel_id=1, source_target_pairs={{0,1},{1,0},{2,3},{3,2},{4,5},{5,4},{6,7},{7,6},{8,9},{9,8},{10,11... | collective-permute-start | bytes 786440 | tf_op jit(solution)/shard_map/ppermute | solution.py:146
  147.7 34.9 %collective-permute-start.30 = (bf16[640,1024]{1,0:T(8,128)(2,1)S(1)}, bf16[640,1024]{1,0:T(8,128)(2,1)S(1)}, u32[]{:S(2)}, u32[]{:S(2)}) collective-permute-start(bf16[640,1024]{1,0:T(8,128)(2,1)S(1)} %get-tuple-element.167.refs_1_), channel_id=1, source_target_pairs={{0,4},{4,0},{8,12},{12,8},{16,20},{20,16},{24,28},{28,24},{1,5},{5... | collective-permute-start | bytes 3932168 | tf_op jit(solution)/shard_map/ppermute | solution.py:146
  198.1 52.9 %collective-permute-start.37 = (bf16[640,2048]{1,0:T(8,128)(2,1)}, bf16[640,2048]{1,0:T(8,128)(2,1)}, u32[]{:S(2)}, u32[]{:S(2)}) collective-permute-start(bf16[640,2048]{1,0:T(8,128)(2,1)} %multiply_convert_fusion.1.second_ref), channel_id=1, source_target_pairs={{0,4},{4,0},{8,12},{12,8},{16,20},{20,16},{24,28},{28,24},{1,5},{5... | collective-permute-start | bytes 7864328 | tf_op jit(solution)/shard_map/ppermute | solution.py:146
  208.8 32.6 %collective-permute-start.34 = (bf16[640,1024]{1,0:T(8,128)(2,1)}, bf16[640,1024]{1,0:T(8,128)(2,1)}, u32[]{:S(2)}, u32[]{:S(2)}) collective-permute-start(bf16[640,1024]{1,0:T(8,128)(2,1)} %get-tuple-element.177), channel_id=1, source_target_pairs={{0,16},{4,20},{8,24},{12,28},{16,0},{20,4},{24,8},{28,12},{1,17},{... | collective-permute-start | bytes 3932168 | tf_op jit(solution)/shard_map/ppermute | solution.py:146
  216.2 30.6 %collective-permute-start.36 = (bf16[640,1024]{1,0:T(8,128)(2,1)S(1)}, bf16[640,1024]{1,0:T(8,128)(2,1)}, u32[]{:S(2)}, u32[]{:S(2)}) collective-permute-start(bf16[640,1024]{1,0:T(8,128)(2,1)S(1)} %get-tuple-element.184), channel_id=1, source_target_pairs={{0,8},{4,12},{8,0},{12,4},{16,24},{20,28},{24,16},{28,20},{1,9},{5... | collective-permute-start | bytes 3932168 | tf_op jit(solution)/shard_map/ppermute | solution.py:146
  274.6 45.6 %collective-permute-start.41 = (bf16[512,1024]{1,0:T(8,128)(2,1)}, bf16[512,1024]{1,0:T(8,128)(2,1)}, u32[]{:S(2)}, u32[]{:S(2)}) collective-permute-start(bf16[512,1024]{1,0:T(8,128)(2,1)} %get-tuple-element.193), channel_id=1, source_target_pairs={{0,16},{4,20},{8,24},{12,28},{16,0},{20,4},{24,8},{28,12},{1,17},{... | collective-permute-start | bytes 3145736 | tf_op jit(solution)/shard_map/ppermute | solution.py:146
  276.0 47.1 %collective-permute-start.42 = (bf16[512,1024]{1,0:T(8,128)(2,1)S(1)}, bf16[512,1024]{1,0:T(8,128)(2,1)}, u32[]{:S(2)}, u32[]{:S(2)}) collective-permute-start(bf16[512,1024]{1,0:T(8,128)(2,1)S(1)} %get-tuple-element.195), channel_id=1, source_target_pairs={{0,8},{4,12},{8,0},{12,4},{16,24},{20,28},{24,16},{28,20},{1,9},{5... | collective-permute-start | bytes 3145736 | tf_op jit(solution)/shard_map/ppermute | solution.py:146
  276.7 49.0 %collective-permute-start.44 = (bf16[640,1024]{1,0:T(8,128)(2,1)S(1)}, bf16[640,1024]{1,0:T(8,128)(2,1)S(1)}, u32[]{:S(2)}, u32[]{:S(2)}) collective-permute-start(bf16[640,1024]{1,0:T(8,128)(2,1)S(1)} %copy-done.12), channel_id=1, source_target_pairs={{0,4},{4,0},{8,12},{12,8},{16,20},{20,16},{24,28},{28,24},{1,5},{5... | collective-permute-start | bytes 3932168 | tf_op jit(solution)/shard_map/ppermute | solution.py:146
  293.7 47.4 %collective-permute-start.40 = (bf16[2,160,1024]{2,1,0:T(8,128)(2,1)}, bf16[2,160,1024]{2,1,0:T(8,128)(2,1)}, u32[]{:S(2)}, u32[]{:S(2)}) collective-permute-start(bf16[2,160,1024]{2,1,0:T(8,128)(2,1)} %pad_maximum_fusion.32), channel_id=1, source_target_pairs={{0,2},{1,3},{2,0},{3,1},{4,6},{5,7},{6,4},{7,5},{8,10},{9,11},{10,... | collective-permute-start | bytes 1966088 | tf_op jit(solution)/shard_map/ppermute | solution.py:146
  323.1 31.8 %collective-permute-start.45 = (bf16[1,320,1024]{2,1,0:T(8,128)(2,1)}, bf16[1,320,1024]{2,1,0:T(8,128)(2,1)}, u32[]{:S(2)}, u32[]{:S(2)}) collective-permute-start(bf16[1,320,1024]{2,1,0:T(8,128)(2,1)} %get-tuple-element.289), channel_id=1, source_target_pairs={{0,2},{1,3},{2,0},{3,1},{4,6},{5,7},{6,4},{7,5},{8,10},{9,11},{10,... | collective-permute-start | bytes 1966088 | tf_op jit(solution)/shard_map/ppermute | solution.py:146
  348.8 31.5 %collective-permute-start.55 = (bf16[544,1024]{1,0:T(8,128)(2,1)S(1)}, bf16[544,1024]{1,0:T(8,128)(2,1)S(1)}, u32[]{:S(2)}, u32[]{:S(2)}) collective-permute-start(bf16[544,1024]{1,0:T(8,128)(2,1)S(1)} %pad_maximum_fusion.19), channel_id=1, source_target_pairs={{0,8},{4,12},{8,0},{12,4},{16,24},{20,28},{24,16},{28,20},{1,9},{5... | collective-permute-start | bytes 3342344 | tf_op jit(solution)/shard_map/ppermute | solution.py:146
  356.2 60.5 %collective-permute-start.50 = (bf16[2,320,1024]{2,1,0:T(8,128)(2,1)S(1)}, bf16[2,320,1024]{2,1,0:T(8,128)(2,1)S(1)}, u32[]{:S(2)}, u32[]{:S(2)}) collective-permute-start(bf16[2,320,1024]{2,1,0:T(8,128)(2,1)S(1)} %get-tuple-element.287), channel_id=1, source_target_pairs={{0,1},{1,0},{2,3},{3,2},{4,5},{5,4},{6,7},{7,6},{8,9},{9,8},{10,11... | collective-permute-start | bytes 3932168 | tf_op jit(solution)/shard_map/ppermute | solution.py:146
  356.2 60.9 %collective-permute-start.49 = (bf16[1,320,1024]{2,1,0:T(8,128)(2,1)S(1)}, bf16[1,320,1024]{2,1,0:T(8,128)(2,1)S(1)}, u32[]{:S(2)}, u32[]{:S(2)}) collective-permute-start(bf16[1,320,1024]{2,1,0:T(8,128)(2,1)S(1)} %bitcast.625), channel_id=1, source_target_pairs={{0,2},{1,3},{2,0},{3,1},{4,6},{5,7},{6,4},{7,5},{8,10},{9,11},{10,... | collective-permute-start | bytes 1966088 | tf_op jit(solution)/shard_map/ppermute | solution.py:146
  380.3 30.3 %collective-permute-start.54 = (bf16[2,64,1024]{2,1,0:T(8,128)(2,1)S(1)}, bf16[2,64,1024]{2,1,0:T(8,128)(2,1)S(1)}, u32[]{:S(2)}, u32[]{:S(2)}) collective-permute-start(bf16[2,64,1024]{2,1,0:T(8,128)(2,1)S(1)} %slice_bitcast_fusion.36), channel_id=1, source_target_pairs={{0,2},{1,3},{2,0},{3,1},{4,6},{5,7},{6,4},{7,5},{8,10},{9,11},{10,... | collective-permute-start | bytes 786440 | tf_op jit(solution)/shard_map/ppermute | solution.py:146
  431.4 34.2 %collective-permute-start.57 = (bf16[2,320,1024]{2,1,0:T(8,128)(2,1)}, bf16[2,320,1024]{2,1,0:T(8,128)(2,1)}, u32[]{:S(2)}, u32[]{:S(2)}) collective-permute-start(bf16[2,320,1024]{2,1,0:T(8,128)(2,1)} %get-tuple-element.285), channel_id=1, source_target_pairs={{0,1},{1,0},{2,3},{3,2},{4,5},{5,4},{6,7},{7,6},{8,9},{9,8},{10,11... | collective-permute-start | bytes 3932168 | tf_op jit(solution)/shard_map/ppermute | solution.py:146
  449.7 30.6 %collective-permute-start.65 = (bf16[4,192,1024]{2,1,0:T(8,128)(2,1)S(1)}, bf16[4,192,1024]{2,1,0:T(8,128)(2,1)S(1)}, u32[]{:S(2)}, u32[]{:S(2)}) collective-permute-start(bf16[4,192,1024]{2,1,0:T(8,128)(2,1)S(1)} %bitcast.541), channel_id=1, source_target_pairs={{0,4},{4,0},{8,12},{12,8},{16,20},{20,16},{24,28},{28,24},{1,5},{5... | collective-permute-start | bytes 4718600 | tf_op jit(solution)/shard_map/ppermute | solution.py:146
  451.7 37.4 %collective-permute-start.62 = (bf16[2,80,1024]{2,1,0:T(8,128)(2,1)S(1)}, bf16[2,80,1024]{2,1,0:T(8,128)(2,1)S(1)}, u32[]{:S(2)}, u32[]{:S(2)}) collective-permute-start(bf16[2,80,1024]{2,1,0:T(8,128)(2,1)S(1)} %get-tuple-element.340.refs_0_), channel_id=1, source_target_pairs={{0,8},{4,12},{8,0},{12,4},{16,24},{20,28},{24,16},{28,20},{1,9},{5... | collective-permute-start | bytes 983048 | tf_op jit(solution)/shard_map/ppermute | solution.py:146
  452.2 37.0 %collective-permute-start.67 = (bf16[2,80,1024]{2,1,0:T(8,128)(2,1)S(1)}, bf16[2,80,1024]{2,1,0:T(8,128)(2,1)S(1)}, u32[]{:S(2)}, u32[]{:S(2)}) collective-permute-start(bf16[2,80,1024]{2,1,0:T(8,128)(2,1)S(1)} %get-tuple-element.340.refs_0_), channel_id=1, source_target_pairs={{0,16},{4,20},{8,24},{12,28},{16,0},{20,4},{24,8},{28,12},{1,17},{... | collective-permute-start | bytes 983048 | tf_op jit(solution)/shard_map/ppermute | solution.py:146
  (148 other events, 1797.7 us)

commit v5 on v4

--- a/solution.py
+++ b/solution.py
@@ -919,9 +919,9 @@
     ring_b = Flow(spans, gather_rows(after(near[some:], *ring_a.sent), n_tensor))
     z_up.go(*ring_b.sent)
     x_qkv.go(*z_up.sent)
-    (sum_up,) = z_up.finish(*x_qkv.sent)
-    pair_qkv = x_qkv.finish(sum_up)
+    pair_qkv = x_qkv.finish()
     z_qkv = Flow(spans, reduce_tensor(pair_qkv[:2], pair_qkv[2:], n_tensor))
+    (sum_up,) = z_up.finish(*z_qkv.sent)
     sum_seen = jnp.concatenate([after(sum_down, *pair_qkv), sum_up], axis=1)
     x_seen = Flow(links, link_gathers(sum_seen, n_dp))
     while ring_a.left > 1:

time: 504 us -> 505 us (level)
  transfers between devices with their start and end apart: 70 -> 70, of which waited for: 19 -> 23; matrix products, arithmetic and copies ran while one was open for 32% -> 32% of each run, Pallas kernels for 25% -> 25%
where the time goes in v5:
time: 505 us; the launch traced here: 497 us
  Pallas kernels  125 us (25%)
  waiting for transfers between devices  114 us (23%)
  matrix products  70.1 us (14%)
  starting transfers between devices  64.8 us (13%)
  other arithmetic  64.3 us (13%)
  local copies, waits for them, and re-layouts  54.2 us (11%)
    ppermute x70, waiting for transfers between devices, swap(): return lax.ppermute(value, axis, [(i, i ^ mask) for i in range(size)])  114 us
    dot_general x22, matrix products, dot(): lax.dot_general(left, right, (((left_dim,), (right_dim,)), ((), ())), pre...  70.1 us
    ppermute x70, starting transfers between devices, swap(): return lax.ppermute(value, axis, [(i, i ^ mask) for i in range(size)])  64.8 us
    pallas_call x4, Pallas kernels, split_product(): pl.pallas_call(functools.partial(split_kernel, picks, tile, mode), out_sh...  27.9 us
    unnamed x238, local copies, waits for them, and re-layouts  25.3 us
    pallas_call x2, Pallas kernels, attend_back(): pl.pallas_call(functools.partial(attend_back_kernel, scale), grid=(heads...  25.1 us
    pallas_call x2, Pallas kernels, rows_home(): pl.pallas_call(functools.partial(back_kernel, len(values)), grid=(rows //...  21.3 us
    pallas_call x1, Pallas kernels, attend(): pl.pallas_call(functools.partial(attend_kernel, scale), grid=(heads,), in...  14.7 us
  transfers between devices with their start and end apart: 70, of which 23 were waited for; matrix products, arithmetic and copies ran while one was open for 32% of the time, Pallas kernels for 25%

profile of v5, /device:TPU:0, one launch (start us, length us, event | category | flops | bytes accessed | tf_op | source)
XLA Modules:
  0.0 497.0 jit_solution(6981379177764734502)
XLA Ops:
  5.0 5.0 %collective-permute-start.2 = (bf16[2,48,1024]{2,1,0:T(8,128)(2,1)}, bf16[2,48,1024]{2,1,0:T(8,128)(2,1)S(1)}, u32[]{:S(2)}, u32[]{:S(2)}) collective-permute-start(bf16[2,48,1024]{2,1,0:T(8,128)(2,1)} %bitcast.8), channel_id=1, source_target_pairs={{0,3},{1,2},{2,1},{3,0},{4,7},{5,6},{6,5},{7,4},{8,11},{9,10},{10,... | collective-permute-start | bytes 589832 | tf_op jit(solution)/shard_map/ppermute | solution.py:146
  19.7 7.3 %collective-permute-done.1 = bf16[2,48,1024]{2,1,0:T(8,128)(2,1)S(1)} collective-permute-done((bf16[2,48,1024]{2,1,0:T(8,128)(2,1)}, bf16[2,48,1024]{2,1,0:T(8,128)(2,1)S(1)}, u32[]{:S(2)}, u32[]{:S(2)}) %collective-permute-start.1) | collective-permute-done | bytes 196640 | tf_op jit(solution)/shard_map/ppermute | solution.py:146
  84.5 14.7 %attend.1 = (bf16[16,32,640]{2,1,0:T(8,128)(2,1)S(1)}, bf16[16,32,640]{2,1,0:T(8,128)(2,1)S(1)}, f32[16,1,640]{2,1,0:T(1,128)S(1)}) custom-call(bf16[3,16,32,640]{3,2,1,0:T(8,128)(2,1)S(1)} %bitcast.527, bf16[3,16,32,640]{3,2,1,0:T(8,128)(2,1)S(1)} %bitcast.530, s32[640,1]{1,0:T(8,128)S(1)} %copy-done.13, s32[1,640]{1,0:T(1,128)S(1)} %sub.88.row_ref), custom_call_target="tpu_custom_call" | custom-call | tf_op jit(solution)/shard_map/attend/pallas_call | solution.py:613
  109.2 14.9 %collective-permute-done.18 = bf16[2,3,80,1024]{3,2,0,1:T(8,128)(2,1)S(1)} collective-permute-done((bf16[2,3,80,1024]{3,2,0,1:T(8,128)(2,1)S(1)}, bf16[2,3,80,1024]{3,2,0,1:T(8,128)(2,1)S(1)}, u32[]{:S(2)}, u32[]{:S(2)}) %collective-permute-start.18) | collective-permute-done | bytes 983072 | tf_op jit(solution)/shard_map/ppermute | solution.py:146
  142.6 5.1 %multiply_convert_fusion.3 = (bf16[640,2048]{1,0:T(8,128)(2,1)S(1)}, f32[640,2048]{1,0:T(8,128)}) fusion(bf16[640,1024]{1,0:T(8,128)(2,1)S(1)} %get-tuple-element.165.refs_1_, bf16[2048,1024]{1,0:T(8,128)(2,1)S(1)} %bitcast.557), kind=kOutput, calls=%fused_computation.16 | convolution fusion | flops 2690908160 | bytes 13369344 | tf_op jit(solution)/shard_map/dot_general | solution.py:43
  161.5 6.5 %fusion.113 = f32[640,1024]{1,0:T(8,128)} fusion(bf16[640,2048]{1,0:T(8,128)(2,1)S(1)} %get-tuple-element.369.refs_0_, bf16[2048,1024]{1,0:T(8,128)(2,1)} %bitcast.602), kind=kOutput, calls=%fused_computation.417 | convolution fusion | flops 2684354560 | bytes 9437184 | tf_op jit(solution)/shard_map/dot_general | solution.py:43
  168.0 4.9 multiply_convert_fusion.2
  192.4 5.7 %multiply_convert_fusion.1.second_ref = bf16[640,2048]{1,0:T(8,128)(2,1)} fusion(f32[640,2048]{1,0:T(8,128)S(1)} %bitcast.702, bf16[640,1024]{1,0:T(8,128)(2,1)S(1)} %get-tuple-element.177.refs_1_, bf16[2048,1024]{1,0:T(8,128)(2,1)S(1)} %bitcast.605), kind=kOutput, calls=%fused_computation.13 | convolution fusion | flops 2700083200 | bytes 13369344 | tf_op jit(solution)/shard_map/dot_general | solution.py:43
  199.6 9.2 %split_product.4 = (bf16[512,1024]{1,0:T(8,128)(2,1)S(1)}, bf16[640,1024]{1,0:T(8,128)(2,1)}, bf16[640,1024]{1,0:T(8,128)(2,1)S(1)}) custom-call(bf16[640,2048]{1,0:T(8,128)(2,1)} %copy-done.48, bf16[640,1024]{1,0:T(8,128)(2,1)} %copy-done.7, bf16[640,2048]{1,0:T(8,128)(2,1)} %copy-done.49, bf16[640,1024]{1,0:T(8,128)(2,1)} %copy-done.52, ...), custom_call_target="tpu_custom_call" | custom-call | tf_op jit(solution)/shard_map/split_product/pallas_call | solution.py:480
  209.8 6.4 %split_product.5 = (bf16[640,1024]{1,0:T(8,128)(2,1)S(1)}, bf16[640,1024]{1,0:T(8,128)(2,1)S(1)}) custom-call(bf16[640,2048]{1,0:T(8,128)(2,1)} %copy-done.48, bf16[640,1024]{1,0:T(8,128)(2,1)S(1)} %copy-done.8, bf16[640,2048]{1,0:T(8,128)(2,1)} %copy-done.49, bf16[640,1024]{1,0:T(8,128)(2,1)} %copy-done.52, s32[1]{0:T(128)} %bitcast.133.refs_4_.index_ref, ...), custom_call_target="tpu_custom_call" | custom-call | tf_op jit(solution)/shard_map/split_product/pallas_call | solution.py:480
  217.8 9.0 %multiply_convert_fusion.first_ref.refs_0_ = bf16[640,2048]{1,0:T(8,128)(2,1)} fusion(bf16[640,1024]{1,0:T(8,128)(2,1)S(1)} %copy-done.8, bf16[2048,1024]{1,0:T(8,128)(2,1)} %bitcast.603, f32[640,2048]{1,0:T(8,128)} %get-tuple-element.370), kind=kOutput, calls=%fused_computation.12 | convolution fusion | flops 2700083200 | bytes 13369344 | tf_op jit(solution)/shard_map/dot_general | solution.py:43
  226.8 12.7 %rows_back.1 = (f32[640,1024]{1,0:T(8,128)S(1)}, bf16[640,1024]{1,0:T(8,128)(2,1)S(1)}, f32[1,1024]{1,0:T(1,128)S(1)}) custom-call(bf16[640,2048]{1,0:T(8,128)(2,1)} %multiply_convert_fusion.first_ref.refs_0_, bf16[640,2048]{1,0:T(8,128)(2,1)} %multiply_convert_fusion.1.second_ref, bf16[2048,1024]{1,0:T(8,128)(2,1)} %bitcast.558, ...), custom_call_target="tpu_custom_call" | custom-call | tf_op jit(solution)/shard_map/rows_back/pallas_call | solution.py:553
  251.0 6.1 %split_product.6 = (bf16[512,1024]{1,0:T(8,128)(2,1)S(1)}, bf16[512,1024]{1,0:T(8,128)(2,1)S(1)}) custom-call(bf16[640,2048]{1,0:T(8,128)(2,1)} %multiply_convert_fusion.first_ref.refs_0_, bf16[640,1024]{1,0:T(8,128)(2,1)S(1)} %get-tuple-element.165.refs_1_, bf16[640,2048]{1,0:T(8,128)(2,1)} %collective-permute-done.37.refs_2_, ...), custom_call_target="tpu_custom_call" | custom-call | tf_op jit(solution)/shard_map/split_product/pallas_call | solution.py:480
  268.5 6.1 %split_product.7 = (bf16[512,1024]{1,0:T(8,128)(2,1)}, bf16[512,1024]{1,0:T(8,128)(2,1)S(1)}) custom-call(bf16[640,2048]{1,0:T(8,128)(2,1)} %multiply_convert_fusion.first_ref.refs_0_, bf16[640,1024]{1,0:T(8,128)(2,1)S(1)} %copy-done.6, bf16[640,2048]{1,0:T(8,128)(2,1)} %collective-permute-done.37.refs_2_, bf16[640,1024]{1,0:T(8,128)(2,1)S(1)} %copy-done.16), custom_call_target="tpu_custom_call" | custom-call | tf_op jit(solution)/shard_map/split_product/pallas_call | solution.py:480
  276.8 12.5 %attend_back.2 = (bf16[3,16,32,640]{3,2,1,0:T(8,128)(2,1)S(1)}, bf16[3,16,32,640]{3,2,1,0:T(8,128)(2,1)}) custom-call(bf16[3,16,32,640]{3,2,1,0:T(8,128)(2,1)} %bitcast.528, bf16[3,16,32,640]{3,2,1,0:T(8,128)(2,1)} %bitcast.531, bf16[16,32,640]{2,1,0:T(8,128)(2,1)S(1)} %get-tuple-element.139.mixed_first_ref, ...), custom_call_target="tpu_custom_call" | custom-call | tf_op jit(solution)/shard_map/attend_back/pallas_call | solution.py:674
  296.5 12.6 %attend_back.3 = (bf16[3,16,32,640]{3,2,1,0:T(8,128)(2,1)S(1)}, bf16[3,16,32,640]{3,2,1,0:T(8,128)(2,1)}) custom-call(bf16[3,16,32,640]{3,2,1,0:T(8,128)(2,1)} %bitcast.529, bf16[3,16,32,640]{3,2,1,0:T(8,128)(2,1)} %bitcast.532, bf16[16,32,640]{2,1,0:T(8,128)(2,1)S(1)} %get-tuple-element.139.mixed_first_ref, ...), custom_call_target="tpu_custom_call", output_to_operand_aliasing={{0}: (9, {}), {1}: (10, {})} | custom-call | tf_op jit(solution)/shard_map/attend_back/pallas_call | solution.py:674
  333.2 7.9 %pair_product.2 = bf16[1536,1024]{1,0:T(8,128)(2,1)} custom-call(bf16[1536,640]{1,0:T(8,128)(2,1)S(1)} %bitcast.540, bf16[640,1024]{1,0:T(8,128)(2,1)S(1)} %copy-done.10, bf16[1536,640]{1,0:T(8,128)(2,1)} %collective-permute-done.43.left_mate_ref, bf16[640,1024]{1,0:T(8,128)(2,1)S(1)} %copy-done.24), custom_call_target="tpu_custom_call" | custom-call | tf_op jit(solution)/shard_map/pair_product/pallas_call | solution.py:424
  358.5 21.5 %collective-permute-done.52 = bf16[2,128,1024]{2,1,0:T(8,128)(2,1)S(1)} collective-permute-done((bf16[2,128,1024]{2,1,0:T(8,128)(2,1)S(1)}, bf16[2,128,1024]{2,1,0:T(8,128)(2,1)S(1)}, u32[]{:S(2)}, u32[]{:S(2)}) %collective-permute-start.52) | collective-permute-done | bytes 524320 | tf_op jit(solution)/shard_map/ppermute | solution.py:146
  384.5 11.5 %collective-permute-done.55 = bf16[272,1024]{1,0:T(8,128)(2,1)S(1)} collective-permute-done((bf16[272,1024]{1,0:T(8,128)(2,1)S(1)}, bf16[272,1024]{1,0:T(8,128)(2,1)S(1)}, u32[]{:S(2)}, u32[]{:S(2)}) %collective-permute-start.55) | collective-permute-done | bytes 557088 | tf_op jit(solution)/shard_map/ppermute | solution.py:146
  400.3 12.2 %collective-permute-done.56 = bf16[2,64,1024]{2,1,0:T(8,128)(2,1)S(1)} collective-permute-done((bf16[2,64,1024]{2,1,0:T(8,128)(2,1)S(1)}, bf16[2,64,1024]{2,1,0:T(8,128)(2,1)S(1)}, u32[]{:S(2)}, u32[]{:S(2)}) %collective-permute-start.56) | collective-permute-done | bytes 262176 | tf_op jit(solution)/shard_map/ppermute | solution.py:146
  432.9 11.9 %rows_home.2.refs_3_ = bf16[2048,1024]{1,0:T(8,128)(2,1)} custom-call(s32[1,1600]{1,0:T(1,128)S(1)} %broadcast_in_dim.32.source_ref, bf16[640,1024]{1,0:T(8,128)(2,1)S(1)} %add_convert_fusion.refs_0_, bf16[320,1024]{1,0:T(8,128)(2,1)S(1)} %get-tuple-element.263.refs_1_, bf16[320,1024]{1,0:T(8,128)(2,1)S(1)} %get-tuple-element.262.refs_2_, ...), custom_call_target="tpu_custom_call" | custom-call | tf_op jit(solution)/shard_map/rows_home/pallas_call | solution.py:511
  455.1 11.4 %collective-permute-done.57 = bf16[2,320,1024]{2,1,0:T(8,128)(2,1)} collective-permute-done((bf16[2,320,1024]{2,1,0:T(8,128)(2,1)}, bf16[2,320,1024]{2,1,0:T(8,128)(2,1)}, u32[]{:S(2)}, u32[]{:S(2)}) %collective-permute-start.57) | collective-permute-done | bytes 1310752 | tf_op jit(solution)/shard_map/ppermute | solution.py:146
  471.8 9.3 %rows_home.3 = bf16[2048,1024]{1,0:T(8,128)(2,1)} custom-call(s32[1,960]{1,0:T(1,128)S(1)} %bitcast.555, bf16[320,1024]{1,0:T(8,128)(2,1)S(1)} %get-tuple-element.260.refs_0_, bf16[320,1024]{1,0:T(8,128)(2,1)S(1)} %get-tuple-element.259.refs_1_, bf16[320,1024]{1,0:T(8,128)(2,1)S(1)} %get-tuple-element.258.refs_2_, bf16[2048,1024]{1,0:T(8,128)(2,1)S(1)} %copy-done.4), custom_call_target="tpu_custom_call" | custom-call | tf_op jit(solution)/shard_map/rows_home/pallas_call | solution.py:511
  482.3 7.7 %place_rows.2 = (f32[1,1024,1024]{2,1,0:T(8,128)}, f32[1,1024,1024]{2,1,0:T(8,128)}, f32[1,1024,1024]{2,1,0:T(8,128)}) custom-call(s32[1]{0:T(128)} %bitcast.133.refs_4_.index_ref, bf16[4,192,1024]{2,1,0:T(8,128)(2,1)S(1)} %bitcast.542, bf16[4,192,1024]{2,1,0:T(8,128)(2,1)S(1)} %bitcast.544, bf16[4,192,1024]{2,1,0:T(8,128)(2,1)S(1)} %collective-permute-done.65.refs_2_, ...), custom_call_target="tpu_custom_call" | custom-call | tf_op jit(solution)/shard_map/place_rows/pallas_call | solution.py:392
  (602 shorter events, 260.5 us)
Async XLA Ops:
  28.6 37.7 %collective-permute-start.11 = (bf16[2,80,1024]{2,1,0:T(8,128)(2,1)}, bf16[2,80,1024]{2,1,0:T(8,128)(2,1)}, u32[]{:S(2)}, u32[]{:S(2)}) collective-permute-start(bf16[2,80,1024]{2,1,0:T(8,128)(2,1)} %constant_dynamic-update-slice_fusion), channel_id=1, source_target_pairs={{0,3},{1,2},{2,1},{3,0},{4,7},{5,6},{6,5},{7,4},{8,11},{9,10},{10,... | collective-permute-start | bytes 983048 | tf_op jit(solution)/shard_map/ppermute | solution.py:146
  31.0 35.3 %collective-permute-start.10 = (bf16[2,80,1024]{2,1,0:T(8,128)(2,1)}, bf16[2,80,1024]{2,1,0:T(8,128)(2,1)}, u32[]{:S(2)}, u32[]{:S(2)}) collective-permute-start(bf16[2,80,1024]{2,1,0:T(8,128)(2,1)} %constant_dynamic-update-slice_fusion), channel_id=1, source_target_pairs={{0,2},{1,3},{2,0},{3,1},{4,6},{5,7},{6,4},{7,5},{8,10},{9,11},{10,... | collective-permute-start | bytes 983048 | tf_op jit(solution)/shard_map/ppermute | solution.py:146
  31.0 35.3 %collective-permute-start.9 = (bf16[2,80,1024]{2,1,0:T(8,128)(2,1)}, bf16[2,80,1024]{2,1,0:T(8,128)(2,1)}, u32[]{:S(2)}, u32[]{:S(2)}) collective-permute-start(bf16[2,80,1024]{2,1,0:T(8,128)(2,1)} %constant_dynamic-update-slice_fusion), channel_id=1, source_target_pairs={{0,1},{1,0},{2,3},{3,2},{4,5},{5,4},{6,7},{7,6},{8,9},{9,8},{10,11... | collective-permute-start | bytes 983048 | tf_op jit(solution)/shard_map/ppermute | solution.py:146
  41.8 30.3 %collective-permute-start.6 = (bf16[2,3,48,1024]{3,2,0,1:T(8,128)(2,1)}, bf16[2,3,48,1024]{3,2,0,1:T(8,128)(2,1)}, u32[]{:S(2)}, u32[]{:S(2)}) collective-permute-start(bf16[2,3,48,1024]{3,2,0,1:T(8,128)(2,1)} %get-tuple-element.324), channel_id=1, source_target_pairs={{0,8},{4,12},{8,0},{12,4},{16,24},{20,28},{24,16},{28,20},{1,9},{5... | collective-permute-start | bytes 1769480 | tf_op jit(solution)/shard_map/ppermute | solution.py:146
  67.6 35.6 %collective-permute-start.17 = (bf16[2,64,1024]{2,1,0:T(8,128)(2,1)}, bf16[2,64,1024]{2,1,0:T(8,128)(2,1)}, u32[]{:S(2)}, u32[]{:S(2)}) collective-permute-start(bf16[2,64,1024]{2,1,0:T(8,128)(2,1)} %dynamic-slice_bitcast_fusion), channel_id=1, source_target_pairs={{0,3},{1,2},{2,1},{3,0},{4,7},{5,6},{6,5},{7,4},{8,11},{9,10},{10,... | collective-permute-start | bytes 786440 | tf_op jit(solution)/shard_map/ppermute | solution.py:146
  69.9 33.3 %collective-permute-start.16 = (bf16[2,64,1024]{2,1,0:T(8,128)(2,1)}, bf16[2,64,1024]{2,1,0:T(8,128)(2,1)}, u32[]{:S(2)}, u32[]{:S(2)}) collective-permute-start(bf16[2,64,1024]{2,1,0:T(8,128)(2,1)} %dynamic-slice_bitcast_fusion), channel_id=1, source_target_pairs={{0,2},{1,3},{2,0},{3,1},{4,6},{5,7},{6,4},{7,5},{8,10},{9,11},{10,... | collective-permute-start | bytes 786440 | tf_op jit(solution)/shard_map/ppermute | solution.py:146
  69.9 33.3 %collective-permute-start.15 = (bf16[2,64,1024]{2,1,0:T(8,128)(2,1)}, bf16[2,64,1024]{2,1,0:T(8,128)(2,1)}, u32[]{:S(2)}, u32[]{:S(2)}) collective-permute-start(bf16[2,64,1024]{2,1,0:T(8,128)(2,1)} %dynamic-slice_bitcast_fusion), channel_id=1, source_target_pairs={{0,1},{1,0},{2,3},{3,2},{4,5},{5,4},{6,7},{7,6},{8,9},{9,8},{10,11... | collective-permute-start | bytes 786440 | tf_op jit(solution)/shard_map/ppermute | solution.py:146
  147.7 34.9 %collective-permute-start.30 = (bf16[640,1024]{1,0:T(8,128)(2,1)S(1)}, bf16[640,1024]{1,0:T(8,128)(2,1)S(1)}, u32[]{:S(2)}, u32[]{:S(2)}) collective-permute-start(bf16[640,1024]{1,0:T(8,128)(2,1)S(1)} %get-tuple-element.165.refs_1_), channel_id=1, source_target_pairs={{0,4},{4,0},{8,12},{12,8},{16,20},{20,16},{24,28},{28,24},{1,5},{5... | collective-permute-start | bytes 3932168 | tf_op jit(solution)/shard_map/ppermute | solution.py:146
  198.1 52.9 %collective-permute-start.37 = (bf16[640,2048]{1,0:T(8,128)(2,1)}, bf16[640,2048]{1,0:T(8,128)(2,1)}, u32[]{:S(2)}, u32[]{:S(2)}) collective-permute-start(bf16[640,2048]{1,0:T(8,128)(2,1)} %multiply_convert_fusion.1.second_ref), channel_id=1, source_target_pairs={{0,4},{4,0},{8,12},{12,8},{16,20},{20,16},{24,28},{28,24},{1,5},{5... | collective-permute-start | bytes 7864328 | tf_op jit(solution)/shard_map/ppermute | solution.py:146
  208.8 32.6 %collective-permute-start.34 = (bf16[640,1024]{1,0:T(8,128)(2,1)}, bf16[640,1024]{1,0:T(8,128)(2,1)}, u32[]{:S(2)}, u32[]{:S(2)}) collective-permute-start(bf16[640,1024]{1,0:T(8,128)(2,1)} %get-tuple-element.175), channel_id=1, source_target_pairs={{0,16},{4,20},{8,24},{12,28},{16,0},{20,4},{24,8},{28,12},{1,17},{... | collective-permute-start | bytes 3932168 | tf_op jit(solution)/shard_map/ppermute | solution.py:146
  216.2 30.6 %collective-permute-start.36 = (bf16[640,1024]{1,0:T(8,128)(2,1)S(1)}, bf16[640,1024]{1,0:T(8,128)(2,1)}, u32[]{:S(2)}, u32[]{:S(2)}) collective-permute-start(bf16[640,1024]{1,0:T(8,128)(2,1)S(1)} %get-tuple-element.182), channel_id=1, source_target_pairs={{0,8},{4,12},{8,0},{12,4},{16,24},{20,28},{24,16},{28,20},{1,9},{5... | collective-permute-start | bytes 3932168 | tf_op jit(solution)/shard_map/ppermute | solution.py:146
  274.6 45.6 %collective-permute-start.41 = (bf16[512,1024]{1,0:T(8,128)(2,1)}, bf16[512,1024]{1,0:T(8,128)(2,1)}, u32[]{:S(2)}, u32[]{:S(2)}) collective-permute-start(bf16[512,1024]{1,0:T(8,128)(2,1)} %get-tuple-element.191), channel_id=1, source_target_pairs={{0,16},{4,20},{8,24},{12,28},{16,0},{20,4},{24,8},{28,12},{1,17},{... | collective-permute-start | bytes 3145736 | tf_op jit(solution)/shard_map/ppermute | solution.py:146
  276.0 47.1 %collective-permute-start.42 = (bf16[512,1024]{1,0:T(8,128)(2,1)S(1)}, bf16[512,1024]{1,0:T(8,128)(2,1)}, u32[]{:S(2)}, u32[]{:S(2)}) collective-permute-start(bf16[512,1024]{1,0:T(8,128)(2,1)S(1)} %get-tuple-element.193), channel_id=1, source_target_pairs={{0,8},{4,12},{8,0},{12,4},{16,24},{20,28},{24,16},{28,20},{1,9},{5... | collective-permute-start | bytes 3145736 | tf_op jit(solution)/shard_map/ppermute | solution.py:146
  276.7 49.0 %collective-permute-start.44 = (bf16[640,1024]{1,0:T(8,128)(2,1)S(1)}, bf16[640,1024]{1,0:T(8,128)(2,1)S(1)}, u32[]{:S(2)}, u32[]{:S(2)}) collective-permute-start(bf16[640,1024]{1,0:T(8,128)(2,1)S(1)} %copy-done.12), channel_id=1, source_target_pairs={{0,4},{4,0},{8,12},{12,8},{16,20},{20,16},{24,28},{28,24},{1,5},{5... | collective-permute-start | bytes 3932168 | tf_op jit(solution)/shard_map/ppermute | solution.py:146
  293.7 47.4 %collective-permute-start.40 = (bf16[2,160,1024]{2,1,0:T(8,128)(2,1)}, bf16[2,160,1024]{2,1,0:T(8,128)(2,1)}, u32[]{:S(2)}, u32[]{:S(2)}) collective-permute-start(bf16[2,160,1024]{2,1,0:T(8,128)(2,1)} %pad_maximum_fusion.32), channel_id=1, source_target_pairs={{0,2},{1,3},{2,0},{3,1},{4,6},{5,7},{6,4},{7,5},{8,10},{9,11},{10,... | collective-permute-start | bytes 1966088 | tf_op jit(solution)/shard_map/ppermute | solution.py:146
  323.1 31.8 %collective-permute-start.45 = (bf16[1,320,1024]{2,1,0:T(8,128)(2,1)}, bf16[1,320,1024]{2,1,0:T(8,128)(2,1)}, u32[]{:S(2)}, u32[]{:S(2)}) collective-permute-start(bf16[1,320,1024]{2,1,0:T(8,128)(2,1)} %get-tuple-element.285), channel_id=1, source_target_pairs={{0,2},{1,3},{2,0},{3,1},{4,6},{5,7},{6,4},{7,5},{8,10},{9,11},{10,... | collective-permute-start | bytes 1966088 | tf_op jit(solution)/shard_map/ppermute | solution.py:146
  348.8 31.5 %collective-permute-start.54 = (bf16[544,1024]{1,0:T(8,128)(2,1)S(1)}, bf16[544,1024]{1,0:T(8,128)(2,1)S(1)}, u32[]{:S(2)}, u32[]{:S(2)}) collective-permute-start(bf16[544,1024]{1,0:T(8,128)(2,1)S(1)} %pad_maximum_fusion.19), channel_id=1, source_target_pairs={{0,8},{4,12},{8,0},{12,4},{16,24},{20,28},{24,16},{28,20},{1,9},{5... | collective-permute-start | bytes 3342344 | tf_op jit(solution)/shard_map/ppermute | solution.py:146
  356.2 58.3 %collective-permute-start.50 = (bf16[2,320,1024]{2,1,0:T(8,128)(2,1)S(1)}, bf16[2,320,1024]{2,1,0:T(8,128)(2,1)S(1)}, u32[]{:S(2)}, u32[]{:S(2)}) collective-permute-start(bf16[2,320,1024]{2,1,0:T(8,128)(2,1)S(1)} %get-tuple-element.283), channel_id=1, source_target_pairs={{0,1},{1,0},{2,3},{3,2},{4,5},{5,4},{6,7},{7,6},{8,9},{9,8},{10,11... | collective-permute-start | bytes 3932168 | tf_op jit(solution)/shard_map/ppermute | solution.py:146
  356.2 58.7 %collective-permute-start.49 = (bf16[1,320,1024]{2,1,0:T(8,128)(2,1)S(1)}, bf16[1,320,1024]{2,1,0:T(8,128)(2,1)S(1)}, u32[]{:S(2)}, u32[]{:S(2)}) collective-permute-start(bf16[1,320,1024]{2,1,0:T(8,128)(2,1)S(1)} %bitcast.625), channel_id=1, source_target_pairs={{0,2},{1,3},{2,0},{3,1},{4,6},{5,7},{6,4},{7,5},{8,10},{9,11},{10,... | collective-permute-start | bytes 1966088 | tf_op jit(solution)/shard_map/ppermute | solution.py:146
  380.3 32.2 %collective-permute-start.56 = (bf16[2,64,1024]{2,1,0:T(8,128)(2,1)S(1)}, bf16[2,64,1024]{2,1,0:T(8,128)(2,1)S(1)}, u32[]{:S(2)}, u32[]{:S(2)}) collective-permute-start(bf16[2,64,1024]{2,1,0:T(8,128)(2,1)S(1)} %slice_bitcast_fusion.36), channel_id=1, source_target_pairs={{0,2},{1,3},{2,0},{3,1},{4,6},{5,7},{6,4},{7,5},{8,10},{9,11},{10,... | collective-permute-start | bytes 786440 | tf_op jit(solution)/shard_map/ppermute | solution.py:146
  428.8 37.8 %collective-permute-start.57 = (bf16[2,320,1024]{2,1,0:T(8,128)(2,1)}, bf16[2,320,1024]{2,1,0:T(8,128)(2,1)}, u32[]{:S(2)}, u32[]{:S(2)}) collective-permute-start(bf16[2,320,1024]{2,1,0:T(8,128)(2,1)} %get-tuple-element.281), channel_id=1, source_target_pairs={{0,1},{1,0},{2,3},{3,2},{4,5},{5,4},{6,7},{7,6},{8,9},{9,8},{10,11... | collective-permute-start | bytes 3932168 | tf_op jit(solution)/shard_map/ppermute | solution.py:146
  451.1 30.1 %collective-permute-start.65 = (bf16[4,192,1024]{2,1,0:T(8,128)(2,1)S(1)}, bf16[4,192,1024]{2,1,0:T(8,128)(2,1)S(1)}, u32[]{:S(2)}, u32[]{:S(2)}) collective-permute-start(bf16[4,192,1024]{2,1,0:T(8,128)(2,1)S(1)} %bitcast.541), channel_id=1, source_target_pairs={{0,4},{4,0},{8,12},{12,8},{16,20},{20,16},{24,28},{28,24},{1,5},{5... | collective-permute-start | bytes 4718600 | tf_op jit(solution)/shard_map/ppermute | solution.py:146
  453.1 36.9 %collective-permute-start.62 = (bf16[2,80,1024]{2,1,0:T(8,128)(2,1)S(1)}, bf16[2,80,1024]{2,1,0:T(8,128)(2,1)S(1)}, u32[]{:S(2)}, u32[]{:S(2)}) collective-permute-start(bf16[2,80,1024]{2,1,0:T(8,128)(2,1)S(1)} %get-tuple-element.336.refs_0_), channel_id=1, source_target_pairs={{0,8},{4,12},{8,0},{12,4},{16,24},{20,28},{24,16},{28,20},{1,9},{5... | collective-permute-start | bytes 983048 | tf_op jit(solution)/shard_map/ppermute | solution.py:146
  454.5 35.5 %collective-permute-start.67 = (bf16[2,80,1024]{2,1,0:T(8,128)(2,1)S(1)}, bf16[2,80,1024]{2,1,0:T(8,128)(2,1)S(1)}, u32[]{:S(2)}, u32[]{:S(2)}) collective-permute-start(bf16[2,80,1024]{2,1,0:T(8,128)(2,1)S(1)} %get-tuple-element.336.refs_0_), channel_id=1, source_target_pairs={{0,16},{4,20},{8,24},{12,28},{16,0},{20,4},{24,8},{28,12},{1,17},{... | collective-permute-start | bytes 983048 | tf_op jit(solution)/shard_map/ppermute | solution.py:146
  (148 other events, 1786.3 us)

commit v6 on v4

--- a/solution.py
+++ b/solution.py
@@ -505,7 +505,7 @@
     sources = jnp.concatenate([b[0] for b in blocks])[None]
     values = [b[1] for b in blocks]
     width = values[0].shape[1]
-    tile = min(256, rows)
+    tile = min(512, rows)
     whole = lambda array: pl.BlockSpec(array.shape, lambda i: (0, 0))
     block = pl.BlockSpec((tile, width), lambda i: (i, 0))
     return pl.pallas_call(

time: 504 us -> 503 us (level)
  transfers between devices with their start and end apart: 70 -> 70, of which waited for: 19 -> 20; matrix products, arithmetic and copies ran while one was open for 32% -> 33% of each run, Pallas kernels for 25% -> 24%
where the time goes in v6:
time: 503 us; the launch traced here: 495 us
  Pallas kernels  124 us (25%)
  waiting for transfers between devices  112 us (22%)
  matrix products  70.1 us (14%)
  starting transfers between devices  66.4 us (13%)
  other arithmetic  64.5 us (13%)
  local copies, waits for them, and re-layouts  54.2 us (11%)
    ppermute x70, waiting for transfers between devices, swap(): return lax.ppermute(value, axis, [(i, i ^ mask) for i in range(size)])  112 us
    dot_general x22, matrix products, dot(): lax.dot_general(left, right, (((left_dim,), (right_dim,)), ((), ())), pre...  70.1 us
    ppermute x70, starting transfers between devices, swap(): return lax.ppermute(value, axis, [(i, i ^ mask) for i in range(size)])  66.4 us
    pallas_call x4, Pallas kernels, split_product(): pl.pallas_call(functools.partial(split_kernel, picks, tile, mode), out_sh...  27.9 us
    unnamed x238, local copies, waits for them, and re-layouts  25.3 us
    pallas_call x2, Pallas kernels, attend_back(): pl.pallas_call(functools.partial(attend_back_kernel, scale), grid=(heads...  25.1 us
    pallas_call x2, Pallas kernels, rows_home(): pl.pallas_call(functools.partial(back_kernel, len(values)), grid=(rows //...  20.1 us
    pallas_call x1, Pallas kernels, attend(): pl.pallas_call(functools.partial(attend_kernel, scale), grid=(heads,), in...  14.7 us
  transfers between devices with their start and end apart: 70, of which 20 were waited for; matrix products, arithmetic and copies ran while one was open for 33% of the time, Pallas kernels for 24%

profile of v6, /device:TPU:0, one launch (start us, length us, event | category | flops | bytes accessed | tf_op | source)
XLA Modules:
  0.0 495.4 jit_solution(10295958466426352488)
XLA Ops:
  5.0 5.0 %collective-permute-start.2 = (bf16[2,48,1024]{2,1,0:T(8,128)(2,1)}, bf16[2,48,1024]{2,1,0:T(8,128)(2,1)S(1)}, u32[]{:S(2)}, u32[]{:S(2)}) collective-permute-start(bf16[2,48,1024]{2,1,0:T(8,128)(2,1)} %bitcast.8), channel_id=1, source_target_pairs={{0,3},{1,2},{2,1},{3,0},{4,7},{5,6},{6,5},{7,4},{8,11},{9,10},{10,... | collective-permute-start | bytes 589832 | tf_op jit(solution)/shard_map/ppermute | solution.py:146
  19.7 7.3 %collective-permute-done.1 = bf16[2,48,1024]{2,1,0:T(8,128)(2,1)S(1)} collective-permute-done((bf16[2,48,1024]{2,1,0:T(8,128)(2,1)}, bf16[2,48,1024]{2,1,0:T(8,128)(2,1)S(1)}, u32[]{:S(2)}, u32[]{:S(2)}) %collective-permute-start.1) | collective-permute-done | bytes 196640 | tf_op jit(solution)/shard_map/ppermute | solution.py:146
  84.5 14.7 %attend.1 = (bf16[16,32,640]{2,1,0:T(8,128)(2,1)S(1)}, bf16[16,32,640]{2,1,0:T(8,128)(2,1)S(1)}, f32[16,1,640]{2,1,0:T(1,128)S(1)}) custom-call(bf16[3,16,32,640]{3,2,1,0:T(8,128)(2,1)S(1)} %bitcast.527, bf16[3,16,32,640]{3,2,1,0:T(8,128)(2,1)S(1)} %bitcast.530, s32[640,1]{1,0:T(8,128)S(1)} %copy-done.13, s32[1,640]{1,0:T(1,128)S(1)} %sub.88.row_ref), custom_call_target="tpu_custom_call" | custom-call | tf_op jit(solution)/shard_map/attend/pallas_call | solution.py:613
  109.2 14.9 %collective-permute-done.18 = bf16[2,3,80,1024]{3,2,0,1:T(8,128)(2,1)S(1)} collective-permute-done((bf16[2,3,80,1024]{3,2,0,1:T(8,128)(2,1)S(1)}, bf16[2,3,80,1024]{3,2,0,1:T(8,128)(2,1)S(1)}, u32[]{:S(2)}, u32[]{:S(2)}) %collective-permute-start.18) | collective-permute-done | bytes 983072 | tf_op jit(solution)/shard_map/ppermute | solution.py:146
  142.6 5.1 %multiply_convert_fusion.3 = (bf16[640,2048]{1,0:T(8,128)(2,1)S(1)}, f32[640,2048]{1,0:T(8,128)}) fusion(bf16[640,1024]{1,0:T(8,128)(2,1)S(1)} %get-tuple-element.167.refs_1_, bf16[2048,1024]{1,0:T(8,128)(2,1)S(1)} %bitcast.557), kind=kOutput, calls=%fused_computation.16 | convolution fusion | flops 2690908160 | bytes 13369344 | tf_op jit(solution)/shard_map/dot_general | solution.py:43
  161.5 6.5 %fusion.113 = f32[640,1024]{1,0:T(8,128)} fusion(bf16[640,2048]{1,0:T(8,128)(2,1)S(1)} %get-tuple-element.373.refs_0_, bf16[2048,1024]{1,0:T(8,128)(2,1)} %bitcast.602), kind=kOutput, calls=%fused_computation.417 | convolution fusion | flops 2684354560 | bytes 9437184 | tf_op jit(solution)/shard_map/dot_general | solution.py:43
  168.0 4.9 multiply_convert_fusion.2
  192.4 5.7 %multiply_convert_fusion.1.second_ref = bf16[640,2048]{1,0:T(8,128)(2,1)} fusion(f32[640,2048]{1,0:T(8,128)S(1)} %bitcast.702, bf16[640,1024]{1,0:T(8,128)(2,1)S(1)} %get-tuple-element.179.refs_1_, bf16[2048,1024]{1,0:T(8,128)(2,1)S(1)} %bitcast.605), kind=kOutput, calls=%fused_computation.13 | convolution fusion | flops 2700083200 | bytes 13369344 | tf_op jit(solution)/shard_map/dot_general | solution.py:43
  199.6 9.2 %split_product.4 = (bf16[512,1024]{1,0:T(8,128)(2,1)S(1)}, bf16[640,1024]{1,0:T(8,128)(2,1)}, bf16[640,1024]{1,0:T(8,128)(2,1)S(1)}) custom-call(bf16[640,2048]{1,0:T(8,128)(2,1)} %copy-done.48, bf16[640,1024]{1,0:T(8,128)(2,1)} %copy-done.7, bf16[640,2048]{1,0:T(8,128)(2,1)} %copy-done.49, bf16[640,1024]{1,0:T(8,128)(2,1)} %copy-done.52, ...), custom_call_target="tpu_custom_call" | custom-call | tf_op jit(solution)/shard_map/split_product/pallas_call | solution.py:480
  209.8 6.4 %split_product.5 = (bf16[640,1024]{1,0:T(8,128)(2,1)S(1)}, bf16[640,1024]{1,0:T(8,128)(2,1)S(1)}) custom-call(bf16[640,2048]{1,0:T(8,128)(2,1)} %copy-done.48, bf16[640,1024]{1,0:T(8,128)(2,1)S(1)} %copy-done.8, bf16[640,2048]{1,0:T(8,128)(2,1)} %copy-done.49, bf16[640,1024]{1,0:T(8,128)(2,1)} %copy-done.52, s32[1]{0:T(128)} %bitcast.133.refs_4_.index_ref, ...), custom_call_target="tpu_custom_call" | custom-call | tf_op jit(solution)/shard_map/split_product/pallas_call | solution.py:480
  217.8 9.0 %multiply_convert_fusion.first_ref.refs_0_ = bf16[640,2048]{1,0:T(8,128)(2,1)} fusion(bf16[640,1024]{1,0:T(8,128)(2,1)S(1)} %copy-done.8, bf16[2048,1024]{1,0:T(8,128)(2,1)} %bitcast.603, f32[640,2048]{1,0:T(8,128)} %get-tuple-element.374), kind=kOutput, calls=%fused_computation.12 | convolution fusion | flops 2700083200 | bytes 13369344 | tf_op jit(solution)/shard_map/dot_general | solution.py:43
  226.8 12.7 %rows_back.1 = (f32[640,1024]{1,0:T(8,128)S(1)}, bf16[640,1024]{1,0:T(8,128)(2,1)S(1)}, f32[1,1024]{1,0:T(1,128)S(1)}) custom-call(bf16[640,2048]{1,0:T(8,128)(2,1)} %multiply_convert_fusion.first_ref.refs_0_, bf16[640,2048]{1,0:T(8,128)(2,1)} %multiply_convert_fusion.1.second_ref, bf16[2048,1024]{1,0:T(8,128)(2,1)} %bitcast.558, ...), custom_call_target="tpu_custom_call" | custom-call | tf_op jit(solution)/shard_map/rows_back/pallas_call | solution.py:553
  251.0 6.1 %split_product.6 = (bf16[512,1024]{1,0:T(8,128)(2,1)S(1)}, bf16[512,1024]{1,0:T(8,128)(2,1)S(1)}) custom-call(bf16[640,2048]{1,0:T(8,128)(2,1)} %multiply_convert_fusion.first_ref.refs_0_, bf16[640,1024]{1,0:T(8,128)(2,1)S(1)} %get-tuple-element.167.refs_1_, bf16[640,2048]{1,0:T(8,128)(2,1)} %collective-permute-done.37.refs_2_, ...), custom_call_target="tpu_custom_call" | custom-call | tf_op jit(solution)/shard_map/split_product/pallas_call | solution.py:480
  268.5 6.1 %split_product.7 = (bf16[512,1024]{1,0:T(8,128)(2,1)}, bf16[512,1024]{1,0:T(8,128)(2,1)S(1)}) custom-call(bf16[640,2048]{1,0:T(8,128)(2,1)} %multiply_convert_fusion.first_ref.refs_0_, bf16[640,1024]{1,0:T(8,128)(2,1)S(1)} %copy-done.6, bf16[640,2048]{1,0:T(8,128)(2,1)} %collective-permute-done.37.refs_2_, bf16[640,1024]{1,0:T(8,128)(2,1)S(1)} %copy-done.16), custom_call_target="tpu_custom_call" | custom-call | tf_op jit(solution)/shard_map/split_product/pallas_call | solution.py:480
  276.8 12.5 %attend_back.2 = (bf16[3,16,32,640]{3,2,1,0:T(8,128)(2,1)S(1)}, bf16[3,16,32,640]{3,2,1,0:T(8,128)(2,1)}) custom-call(bf16[3,16,32,640]{3,2,1,0:T(8,128)(2,1)} %bitcast.528, bf16[3,16,32,640]{3,2,1,0:T(8,128)(2,1)} %bitcast.531, bf16[16,32,640]{2,1,0:T(8,128)(2,1)S(1)} %get-tuple-element.141.mixed_first_ref, ...), custom_call_target="tpu_custom_call" | custom-call | tf_op jit(solution)/shard_map/attend_back/pallas_call | solution.py:674
  296.5 12.6 %attend_back.3 = (bf16[3,16,32,640]{3,2,1,0:T(8,128)(2,1)S(1)}, bf16[3,16,32,640]{3,2,1,0:T(8,128)(2,1)}) custom-call(bf16[3,16,32,640]{3,2,1,0:T(8,128)(2,1)} %bitcast.529, bf16[3,16,32,640]{3,2,1,0:T(8,128)(2,1)} %bitcast.532, bf16[16,32,640]{2,1,0:T(8,128)(2,1)S(1)} %get-tuple-element.141.mixed_first_ref, ...), custom_call_target="tpu_custom_call", output_to_operand_aliasing={{0}: (9, {}), {1}: (10, {})} | custom-call | tf_op jit(solution)/shard_map/attend_back/pallas_call | solution.py:674
  333.2 7.9 %pair_product.2 = bf16[1536,1024]{1,0:T(8,128)(2,1)} custom-call(bf16[1536,640]{1,0:T(8,128)(2,1)S(1)} %bitcast.540, bf16[640,1024]{1,0:T(8,128)(2,1)S(1)} %copy-done.10, bf16[1536,640]{1,0:T(8,128)(2,1)} %collective-permute-done.43.left_mate_ref, bf16[640,1024]{1,0:T(8,128)(2,1)S(1)} %copy-done.24), custom_call_target="tpu_custom_call" | custom-call | tf_op jit(solution)/shard_map/pair_product/pallas_call | solution.py:424
  358.5 21.5 %collective-permute-done.52 = bf16[2,128,1024]{2,1,0:T(8,128)(2,1)S(1)} collective-permute-done((bf16[2,128,1024]{2,1,0:T(8,128)(2,1)S(1)}, bf16[2,128,1024]{2,1,0:T(8,128)(2,1)S(1)}, u32[]{:S(2)}, u32[]{:S(2)}) %collective-permute-start.52) | collective-permute-done | bytes 524320 | tf_op jit(solution)/shard_map/ppermute | solution.py:146
  384.5 26.0 %collective-permute-done.54 = bf16[2,64,1024]{2,1,0:T(8,128)(2,1)S(1)} collective-permute-done((bf16[2,64,1024]{2,1,0:T(8,128)(2,1)S(1)}, bf16[2,64,1024]{2,1,0:T(8,128)(2,1)S(1)}, u32[]{:S(2)}, u32[]{:S(2)}) %collective-permute-start.54) | collective-permute-done | bytes 262176 | tf_op jit(solution)/shard_map/ppermute | solution.py:146
  422.7 5.1 %collective-permute-done.58 = bf16[2,144,1024]{2,1,0:T(8,128)(2,1)S(1)} collective-permute-done((bf16[2,144,1024]{2,1,0:T(8,128)(2,1)S(1)}, bf16[2,144,1024]{2,1,0:T(8,128)(2,1)S(1)}, u32[]{:S(2)}, u32[]{:S(2)}) %collective-permute-start.58) | collective-permute-done | bytes 589856 | tf_op jit(solution)/shard_map/ppermute | solution.py:146
  434.3 11.4 %rows_home.2.refs_3_ = bf16[2048,1024]{1,0:T(8,128)(2,1)} custom-call(s32[1,1600]{1,0:T(1,128)S(1)} %broadcast_in_dim.32.source_ref, bf16[640,1024]{1,0:T(8,128)(2,1)S(1)} %add_convert_fusion.refs_0_, bf16[320,1024]{1,0:T(8,128)(2,1)S(1)} %get-tuple-element.267.refs_1_, bf16[320,1024]{1,0:T(8,128)(2,1)S(1)} %get-tuple-element.266.refs_2_, ...), custom_call_target="tpu_custom_call" | custom-call | tf_op jit(solution)/shard_map/rows_home/pallas_call | solution.py:511
  453.5 12.1 %collective-permute-done.57 = bf16[2,320,1024]{2,1,0:T(8,128)(2,1)} collective-permute-done((bf16[2,320,1024]{2,1,0:T(8,128)(2,1)}, bf16[2,320,1024]{2,1,0:T(8,128)(2,1)}, u32[]{:S(2)}, u32[]{:S(2)}) %collective-permute-start.57) | collective-permute-done | bytes 1310752 | tf_op jit(solution)/shard_map/ppermute | solution.py:146
  471.0 8.6 %rows_home.3 = bf16[2048,1024]{1,0:T(8,128)(2,1)} custom-call(s32[1,960]{1,0:T(1,128)S(1)} %bitcast.555, bf16[320,1024]{1,0:T(8,128)(2,1)S(1)} %get-tuple-element.264.refs_0_, bf16[320,1024]{1,0:T(8,128)(2,1)S(1)} %get-tuple-element.263.refs_1_, bf16[320,1024]{1,0:T(8,128)(2,1)S(1)} %get-tuple-element.262.refs_2_, bf16[2048,1024]{1,0:T(8,128)(2,1)S(1)} %copy-done.4), custom_call_target="tpu_custom_call" | custom-call | tf_op jit(solution)/shard_map/rows_home/pallas_call | solution.py:511
  480.8 7.7 %place_rows.2 = (f32[1,1024,1024]{2,1,0:T(8,128)}, f32[1,1024,1024]{2,1,0:T(8,128)}, f32[1,1024,1024]{2,1,0:T(8,128)}) custom-call(s32[1]{0:T(128)} %bitcast.133.refs_4_.index_ref, bf16[4,192,1024]{2,1,0:T(8,128)(2,1)S(1)} %bitcast.542, bf16[4,192,1024]{2,1,0:T(8,128)(2,1)S(1)} %bitcast.544, bf16[4,192,1024]{2,1,0:T(8,128)(2,1)S(1)} %collective-permute-done.65.refs_2_, ...), custom_call_target="tpu_custom_call" | custom-call | tf_op jit(solution)/shard_map/place_rows/pallas_call | solution.py:392
  (602 shorter events, 252.1 us)
Async XLA Ops:
  28.6 37.7 %collective-permute-start.11 = (bf16[2,80,1024]{2,1,0:T(8,128)(2,1)}, bf16[2,80,1024]{2,1,0:T(8,128)(2,1)}, u32[]{:S(2)}, u32[]{:S(2)}) collective-permute-start(bf16[2,80,1024]{2,1,0:T(8,128)(2,1)} %constant_dynamic-update-slice_fusion), channel_id=1, source_target_pairs={{0,3},{1,2},{2,1},{3,0},{4,7},{5,6},{6,5},{7,4},{8,11},{9,10},{10,... | collective-permute-start | bytes 983048 | tf_op jit(solution)/shard_map/ppermute | solution.py:146
  31.0 35.3 %collective-permute-start.10 = (bf16[2,80,1024]{2,1,0:T(8,128)(2,1)}, bf16[2,80,1024]{2,1,0:T(8,128)(2,1)}, u32[]{:S(2)}, u32[]{:S(2)}) collective-permute-start(bf16[2,80,1024]{2,1,0:T(8,128)(2,1)} %constant_dynamic-update-slice_fusion), channel_id=1, source_target_pairs={{0,2},{1,3},{2,0},{3,1},{4,6},{5,7},{6,4},{7,5},{8,10},{9,11},{10,... | collective-permute-start | bytes 983048 | tf_op jit(solution)/shard_map/ppermute | solution.py:146
  31.0 35.3 %collective-permute-start.9 = (bf16[2,80,1024]{2,1,0:T(8,128)(2,1)}, bf16[2,80,1024]{2,1,0:T(8,128)(2,1)}, u32[]{:S(2)}, u32[]{:S(2)}) collective-permute-start(bf16[2,80,1024]{2,1,0:T(8,128)(2,1)} %constant_dynamic-update-slice_fusion), channel_id=1, source_target_pairs={{0,1},{1,0},{2,3},{3,2},{4,5},{5,4},{6,7},{7,6},{8,9},{9,8},{10,11... | collective-permute-start | bytes 983048 | tf_op jit(solution)/shard_map/ppermute | solution.py:146
  41.8 30.3 %collective-permute-start.6 = (bf16[2,3,48,1024]{3,2,0,1:T(8,128)(2,1)}, bf16[2,3,48,1024]{3,2,0,1:T(8,128)(2,1)}, u32[]{:S(2)}, u32[]{:S(2)}) collective-permute-start(bf16[2,3,48,1024]{3,2,0,1:T(8,128)(2,1)} %get-tuple-element.328), channel_id=1, source_target_pairs={{0,8},{4,12},{8,0},{12,4},{16,24},{20,28},{24,16},{28,20},{1,9},{5... | collective-permute-start | bytes 1769480 | tf_op jit(solution)/shard_map/ppermute | solution.py:146
  67.6 35.6 %collective-permute-start.17 = (bf16[2,64,1024]{2,1,0:T(8,128)(2,1)}, bf16[2,64,1024]{2,1,0:T(8,128)(2,1)}, u32[]{:S(2)}, u32[]{:S(2)}) collective-permute-start(bf16[2,64,1024]{2,1,0:T(8,128)(2,1)} %dynamic-slice_bitcast_fusion), channel_id=1, source_target_pairs={{0,3},{1,2},{2,1},{3,0},{4,7},{5,6},{6,5},{7,4},{8,11},{9,10},{10,... | collective-permute-start | bytes 786440 | tf_op jit(solution)/shard_map/ppermute | solution.py:146
  69.9 33.3 %collective-permute-start.16 = (bf16[2,64,1024]{2,1,0:T(8,128)(2,1)}, bf16[2,64,1024]{2,1,0:T(8,128)(2,1)}, u32[]{:S(2)}, u32[]{:S(2)}) collective-permute-start(bf16[2,64,1024]{2,1,0:T(8,128)(2,1)} %dynamic-slice_bitcast_fusion), channel_id=1, source_target_pairs={{0,2},{1,3},{2,0},{3,1},{4,6},{5,7},{6,4},{7,5},{8,10},{9,11},{10,... | collective-permute-start | bytes 786440 | tf_op jit(solution)/shard_map/ppermute | solution.py:146
  69.9 33.3 %collective-permute-start.15 = (bf16[2,64,1024]{2,1,0:T(8,128)(2,1)}, bf16[2,64,1024]{2,1,0:T(8,128)(2,1)}, u32[]{:S(2)}, u32[]{:S(2)}) collective-permute-start(bf16[2,64,1024]{2,1,0:T(8,128)(2,1)} %dynamic-slice_bitcast_fusion), channel_id=1, source_target_pairs={{0,1},{1,0},{2,3},{3,2},{4,5},{5,4},{6,7},{7,6},{8,9},{9,8},{10,11... | collective-permute-start | bytes 786440 | tf_op jit(solution)/shard_map/ppermute | solution.py:146
  147.7 34.9 %collective-permute-start.30 = (bf16[640,1024]{1,0:T(8,128)(2,1)S(1)}, bf16[640,1024]{1,0:T(8,128)(2,1)S(1)}, u32[]{:S(2)}, u32[]{:S(2)}) collective-permute-start(bf16[640,1024]{1,0:T(8,128)(2,1)S(1)} %get-tuple-element.167.refs_1_), channel_id=1, source_target_pairs={{0,4},{4,0},{8,12},{12,8},{16,20},{20,16},{24,28},{28,24},{1,5},{5... | collective-permute-start | bytes 3932168 | tf_op jit(solution)/shard_map/ppermute | solution.py:146
  198.1 52.9 %collective-permute-start.37 = (bf16[640,2048]{1,0:T(8,128)(2,1)}, bf16[640,2048]{1,0:T(8,128)(2,1)}, u32[]{:S(2)}, u32[]{:S(2)}) collective-permute-start(bf16[640,2048]{1,0:T(8,128)(2,1)} %multiply_convert_fusion.1.second_ref), channel_id=1, source_target_pairs={{0,4},{4,0},{8,12},{12,8},{16,20},{20,16},{24,28},{28,24},{1,5},{5... | collective-permute-start | bytes 7864328 | tf_op jit(solution)/shard_map/ppermute | solution.py:146
  208.8 32.6 %collective-permute-start.34 = (bf16[640,1024]{1,0:T(8,128)(2,1)}, bf16[640,1024]{1,0:T(8,128)(2,1)}, u32[]{:S(2)}, u32[]{:S(2)}) collective-permute-start(bf16[640,1024]{1,0:T(8,128)(2,1)} %get-tuple-element.177), channel_id=1, source_target_pairs={{0,16},{4,20},{8,24},{12,28},{16,0},{20,4},{24,8},{28,12},{1,17},{... | collective-permute-start | bytes 3932168 | tf_op jit(solution)/shard_map/ppermute | solution.py:146
  216.2 30.6 %collective-permute-start.36 = (bf16[640,1024]{1,0:T(8,128)(2,1)S(1)}, bf16[640,1024]{1,0:T(8,128)(2,1)}, u32[]{:S(2)}, u32[]{:S(2)}) collective-permute-start(bf16[640,1024]{1,0:T(8,128)(2,1)S(1)} %get-tuple-element.184), channel_id=1, source_target_pairs={{0,8},{4,12},{8,0},{12,4},{16,24},{20,28},{24,16},{28,20},{1,9},{5... | collective-permute-start | bytes 3932168 | tf_op jit(solution)/shard_map/ppermute | solution.py:146
  274.6 45.6 %collective-permute-start.41 = (bf16[512,1024]{1,0:T(8,128)(2,1)}, bf16[512,1024]{1,0:T(8,128)(2,1)}, u32[]{:S(2)}, u32[]{:S(2)}) collective-permute-start(bf16[512,1024]{1,0:T(8,128)(2,1)} %get-tuple-element.193), channel_id=1, source_target_pairs={{0,16},{4,20},{8,24},{12,28},{16,0},{20,4},{24,8},{28,12},{1,17},{... | collective-permute-start | bytes 3145736 | tf_op jit(solution)/shard_map/ppermute | solution.py:146
  276.0 47.1 %collective-permute-start.42 = (bf16[512,1024]{1,0:T(8,128)(2,1)S(1)}, bf16[512,1024]{1,0:T(8,128)(2,1)}, u32[]{:S(2)}, u32[]{:S(2)}) collective-permute-start(bf16[512,1024]{1,0:T(8,128)(2,1)S(1)} %get-tuple-element.195), channel_id=1, source_target_pairs={{0,8},{4,12},{8,0},{12,4},{16,24},{20,28},{24,16},{28,20},{1,9},{5... | collective-permute-start | bytes 3145736 | tf_op jit(solution)/shard_map/ppermute | solution.py:146
  276.7 49.0 %collective-permute-start.44 = (bf16[640,1024]{1,0:T(8,128)(2,1)S(1)}, bf16[640,1024]{1,0:T(8,128)(2,1)S(1)}, u32[]{:S(2)}, u32[]{:S(2)}) collective-permute-start(bf16[640,1024]{1,0:T(8,128)(2,1)S(1)} %copy-done.12), channel_id=1, source_target_pairs={{0,4},{4,0},{8,12},{12,8},{16,20},{20,16},{24,28},{28,24},{1,5},{5... | collective-permute-start | bytes 3932168 | tf_op jit(solution)/shard_map/ppermute | solution.py:146
  293.7 47.4 %collective-permute-start.40 = (bf16[2,160,1024]{2,1,0:T(8,128)(2,1)}, bf16[2,160,1024]{2,1,0:T(8,128)(2,1)}, u32[]{:S(2)}, u32[]{:S(2)}) collective-permute-start(bf16[2,160,1024]{2,1,0:T(8,128)(2,1)} %pad_maximum_fusion.32), channel_id=1, source_target_pairs={{0,2},{1,3},{2,0},{3,1},{4,6},{5,7},{6,4},{7,5},{8,10},{9,11},{10,... | collective-permute-start | bytes 1966088 | tf_op jit(solution)/shard_map/ppermute | solution.py:146
  323.1 31.8 %collective-permute-start.45 = (bf16[1,320,1024]{2,1,0:T(8,128)(2,1)}, bf16[1,320,1024]{2,1,0:T(8,128)(2,1)}, u32[]{:S(2)}, u32[]{:S(2)}) collective-permute-start(bf16[1,320,1024]{2,1,0:T(8,128)(2,1)} %get-tuple-element.289), channel_id=1, source_target_pairs={{0,2},{1,3},{2,0},{3,1},{4,6},{5,7},{6,4},{7,5},{8,10},{9,11},{10,... | collective-permute-start | bytes 1966088 | tf_op jit(solution)/shard_map/ppermute | solution.py:146
  348.8 31.5 %collective-permute-start.55 = (bf16[544,1024]{1,0:T(8,128)(2,1)S(1)}, bf16[544,1024]{1,0:T(8,128)(2,1)S(1)}, u32[]{:S(2)}, u32[]{:S(2)}) collective-permute-start(bf16[544,1024]{1,0:T(8,128)(2,1)S(1)} %pad_maximum_fusion.19), channel_id=1, source_target_pairs={{0,8},{4,12},{8,0},{12,4},{16,24},{20,28},{24,16},{28,20},{1,9},{5... | collective-permute-start | bytes 3342344 | tf_op jit(solution)/shard_map/ppermute | solution.py:146
  356.2 60.5 %collective-permute-start.50 = (bf16[2,320,1024]{2,1,0:T(8,128)(2,1)S(1)}, bf16[2,320,1024]{2,1,0:T(8,128)(2,1)S(1)}, u32[]{:S(2)}, u32[]{:S(2)}) collective-permute-start(bf16[2,320,1024]{2,1,0:T(8,128)(2,1)S(1)} %get-tuple-element.287), channel_id=1, source_target_pairs={{0,1},{1,0},{2,3},{3,2},{4,5},{5,4},{6,7},{7,6},{8,9},{9,8},{10,11... | collective-permute-start | bytes 3932168 | tf_op jit(solution)/shard_map/ppermute | solution.py:146
  356.2 60.9 %collective-permute-start.49 = (bf16[1,320,1024]{2,1,0:T(8,128)(2,1)S(1)}, bf16[1,320,1024]{2,1,0:T(8,128)(2,1)S(1)}, u32[]{:S(2)}, u32[]{:S(2)}) collective-permute-start(bf16[1,320,1024]{2,1,0:T(8,128)(2,1)S(1)} %bitcast.625), channel_id=1, source_target_pairs={{0,2},{1,3},{2,0},{3,1},{4,6},{5,7},{6,4},{7,5},{8,10},{9,11},{10,... | collective-permute-start | bytes 1966088 | tf_op jit(solution)/shard_map/ppermute | solution.py:146
  380.3 30.3 %collective-permute-start.54 = (bf16[2,64,1024]{2,1,0:T(8,128)(2,1)S(1)}, bf16[2,64,1024]{2,1,0:T(8,128)(2,1)S(1)}, u32[]{:S(2)}, u32[]{:S(2)}) collective-permute-start(bf16[2,64,1024]{2,1,0:T(8,128)(2,1)S(1)} %slice_bitcast_fusion.36), channel_id=1, source_target_pairs={{0,2},{1,3},{2,0},{3,1},{4,6},{5,7},{6,4},{7,5},{8,10},{9,11},{10,... | collective-permute-start | bytes 786440 | tf_op jit(solution)/shard_map/ppermute | solution.py:146
  431.4 34.2 %collective-permute-start.57 = (bf16[2,320,1024]{2,1,0:T(8,128)(2,1)}, bf16[2,320,1024]{2,1,0:T(8,128)(2,1)}, u32[]{:S(2)}, u32[]{:S(2)}) collective-permute-start(bf16[2,320,1024]{2,1,0:T(8,128)(2,1)} %get-tuple-element.285), channel_id=1, source_target_pairs={{0,1},{1,0},{2,3},{3,2},{4,5},{5,4},{6,7},{7,6},{8,9},{9,8},{10,11... | collective-permute-start | bytes 3932168 | tf_op jit(solution)/shard_map/ppermute | solution.py:146
  449.3 30.3 %collective-permute-start.65 = (bf16[4,192,1024]{2,1,0:T(8,128)(2,1)S(1)}, bf16[4,192,1024]{2,1,0:T(8,128)(2,1)S(1)}, u32[]{:S(2)}, u32[]{:S(2)}) collective-permute-start(bf16[4,192,1024]{2,1,0:T(8,128)(2,1)S(1)} %bitcast.541), channel_id=1, source_target_pairs={{0,4},{4,0},{8,12},{12,8},{16,20},{20,16},{24,28},{28,24},{1,5},{5... | collective-permute-start | bytes 4718600 | tf_op jit(solution)/shard_map/ppermute | solution.py:146
  451.3 37.2 %collective-permute-start.62 = (bf16[2,80,1024]{2,1,0:T(8,128)(2,1)S(1)}, bf16[2,80,1024]{2,1,0:T(8,128)(2,1)S(1)}, u32[]{:S(2)}, u32[]{:S(2)}) collective-permute-start(bf16[2,80,1024]{2,1,0:T(8,128)(2,1)S(1)} %get-tuple-element.340.refs_0_), channel_id=1, source_target_pairs={{0,8},{4,12},{8,0},{12,4},{16,24},{20,28},{24,16},{28,20},{1,9},{5... | collective-permute-start | bytes 983048 | tf_op jit(solution)/shard_map/ppermute | solution.py:146
  452.1 36.4 %collective-permute-start.67 = (bf16[2,80,1024]{2,1,0:T(8,128)(2,1)S(1)}, bf16[2,80,1024]{2,1,0:T(8,128)(2,1)S(1)}, u32[]{:S(2)}, u32[]{:S(2)}) collective-permute-start(bf16[2,80,1024]{2,1,0:T(8,128)(2,1)S(1)} %get-tuple-element.340.refs_0_), channel_id=1, source_target_pairs={{0,16},{4,20},{8,24},{12,28},{16,0},{20,4},{24,8},{28,12},{1,17},{... | collective-permute-start | bytes 983048 | tf_op jit(solution)/shard_map/ppermute | solution.py:146
  (148 other events, 1795.0 us)
